TPU v7x, 32 devices: a whole 2x2x4 slice. The times are simulated.
32 devices in a mesh: bins: 8 (over z, y), scans: 4 (over x, core).
Axes of the slice: x: 2, y: 2, z: 4, core: 2. Of those that a mesh axis runs over, the one named last changes fastest.
Arguments:
- profiles: float32 [4, 262144], P('scans', 'bins'), may hold values from -150 to 150
- band_edges: int32 [6], replicated, may hold values from 0 to 256, as said below
- owner_counts: int32 [8], replicated, may hold values from 1 to 64, 256 in all
- dynamics: float32 [5, 64, 64], replicated, may hold values from -0.6 to 0.6
- prev_state: float32 [512, 4, 128], P('bins', 'scans'), may hold values from -6 to 6
Outputs:
- new_state: float32 [512, 4, 128], P('bins', 'scans')
Inputs may be any that keep to these rules, and one draw needn't show every extreme that they name: Strictly increasing, band_edges[0] = 0 and band_edges[5] = 256. `owner_counts`: the counts sum to 256, and some owner holds exactly 64 tiles.
All inputs are finite; a program needn't handle non-finite values.
Results may differ from a plain program's by a relative error of at most 0.0001.
Values sent between devices are 32-bit elements; how exact they have to be, the bound alone decides.
No kernel may reach another device: no remote copies, remote signals or barrier semaphores. Data moves between devices by JAX's collectives and lax.ppermute only.
A program may use at most 64 MiB of HBM per device.

v0:
```python
import math

import jax
import jax.numpy as jnp
import numpy as np
from jax import lax
from jax.sharding import PartitionSpec as P

TILE = 512
STATES = 64
NCLASS = 5


EPSILON = 1e-05
HIGHEST = lax.Precision.HIGHEST


def swapped(shard, axis, apart):
    return lax.ppermute(shard, axis, [(i, i ^ 1 << apart) for i in range(lax.axis_size(axis))])


def reversed_bits(entry_count, levels):
    sources = np.arange(entry_count)
    flipped = np.zeros(entry_count, dtype=np.int64)
    for bit_number in range(levels):
        flipped = flipped | (sources >> bit_number & 1) << levels - 1 - bit_number
    return flipped.astype(np.int32)


def rotate(real_part, imag_part, angles):
    cosine_part = jnp.cos(angles)
    sine_part = jnp.sin(angles)
    return (
        real_part * cosine_part + imag_part * sine_part,
        imag_part * cosine_part - real_part * sine_part,
    )


def transform(pattern, cosine_part, sine_part, real_part, imag_part):
    real_out = jnp.einsum(pattern, cosine_part, real_part, precision=HIGHEST) + jnp.einsum(
        pattern, sine_part, imag_part, precision=HIGHEST
    )
    imag_out = jnp.einsum(pattern, cosine_part, imag_part, precision=HIGHEST) - jnp.einsum(
        pattern, sine_part, real_part, precision=HIGHEST
    )
    return (real_out, imag_out)


def measure(fine_sums, mean_power, band_index):
    measured = jnp.zeros_like(fine_sums)
    for class_index in range(NCLASS):
        group_span = 2**class_index
        state_count = STATES // group_span
        coarse = jnp.sum(
            fine_sums.reshape(fine_sums.shape[:-1] + (state_count, group_span)), axis=-1
        )
        coarse = jnp.pad(coarse, [(0, 0)] * (coarse.ndim - 1) + [(0, STATES - state_count)])
        scaling = 1.0 / jnp.sqrt(TILE // state_count * (mean_power + EPSILON))
        chosen = band_index == class_index
        measured = measured + jnp.where(
            chosen[:, None, None, None], coarse * scaling[:, None, None, None], 0.0
        )
    return measured


def update(dynamics, band_index, previous, measured, occupied):
    state_index = jnp.arange(STATES)
    blocks = []
    for class_index in range(NCLASS):
        state_count = STATES // 2**class_index
        inside = state_index < state_count
        blocks.append(jnp.where(inside[:, None] & inside[None, :], dynamics[class_index], 0.0))
    masked = jnp.stack(blocks)
    selection = (band_index[:, None] == jnp.arange(NCLASS)[None, :]).astype(masked.dtype)
    picked = jnp.einsum("rk,kij->rij", selection, masked, precision=HIGHEST)
    updated = jnp.einsum("rij,rpcj->rpci", picked, previous, precision=HIGHEST) + measured
    return jnp.where(occupied[:, None, None, None], updated, 0.0)


def owner_relay(values, powers):
    return (
        lax.all_to_all(values, "bins", split_axis=0, concat_axis=0, tiled=True),
        lax.all_to_all(powers, "bins", split_axis=0, concat_axis=0, tiled=True),
    )


def strided_owners(real_part, imag_part, source_residue, owner_counts, capacity):
    groups = lax.axis_size("bins")
    prof_rows, length = real_part.shape
    leading = 128
    trailing = length // leading
    retained = trailing // 2
    lead_index = jnp.arange(leading, dtype=jnp.int32)
    trail_index = jnp.arange(trailing, dtype=jnp.int32)
    keep_index = jnp.arange(retained, dtype=jnp.int32)
    angle_one = (
        2.0
        * math.pi
        * (lead_index[:, None] * lead_index[None, :] % leading).astype(jnp.float32)
        / leading
    )
    grid_real = real_part.reshape(prof_rows, leading, trailing)
    grid_imag = imag_part.reshape(prof_rows, leading, trailing)
    step_real, step_imag = transform(
        "bk,pkn->pbn", jnp.cos(angle_one), jnp.sin(angle_one), grid_real, grid_imag
    )
    angle_two = (
        2.0
        * math.pi
        * (lead_index[:, None] * trail_index[None, :] % length).astype(jnp.float32)
        / length
    )
    step_real, step_imag = rotate(step_real, step_imag, angle_two[None, :, :])
    angle_three = (
        2.0
        * math.pi
        * (trail_index[:, None] * keep_index[None, :] % trailing).astype(jnp.float32)
        / trailing
    )
    out_real, out_imag = transform(
        "nc,pbn->cbp", jnp.cos(angle_three), jnp.sin(angle_three), step_real, step_imag
    )
    share_bins = TILE // groups
    tile_count = retained * leading // share_bins
    payload = jnp.stack(
        [
            out_real.reshape(tile_count, share_bins, prof_rows),
            out_imag.reshape(tile_count, share_bins, prof_rows),
        ],
        axis=1,
    )
    payload = payload.reshape(tile_count, 2 * share_bins * prof_rows)
    starts = jnp.cumsum(owner_counts) - owner_counts
    slot_index = jnp.arange(capacity, dtype=jnp.int32)
    wanted = starts[:, None] + slot_index[None, :]
    filled = slot_index[None, :] < owner_counts[:, None]
    chosen = jnp.clip(wanted, 0, tile_count - 1)
    buffer = jnp.where(filled[:, :, None], payload[chosen], 0.0)
    piece_power = jnp.sum(buffer * buffer, axis=2)
    arrived, arrived_power = owner_relay(buffer, piece_power)
    arrived = arrived.reshape(groups, capacity, 2, share_bins, prof_rows)
    sub_width = TILE // STATES
    offsets = (
        groups * jnp.arange(share_bins, dtype=jnp.int32)[None, :]
        + jnp.asarray(source_residue)[:, None]
    )
    selector = (
        offsets[:, :, None] // sub_width == jnp.arange(STATES, dtype=jnp.int32)[None, None, :]
    ).astype(jnp.float32)
    fine_sums = jnp.einsum("drcjp,dji->rpci", arrived, selector, precision=HIGHEST)
    partial_power = jnp.sum(arrived_power, axis=0)
    return (fine_sums, partial_power)


def body(profiles, band_edges, owner_counts, dynamics, prev_state):
    groups = lax.axis_size("bins")
    levels = groups.bit_length() - 1
    own_index = lax.axis_index("bins")
    prof_rows, length = profiles.shape
    full_length = length * groups
    capacity = prev_state.shape[0]
    top_bit = levels - 1
    partner = swapped(profiles, "bins", top_bit)
    upper_half = own_index >> top_bit & 1 == 1
    angles = math.pi * (own_index % 2**top_bit).astype(jnp.float32) / 2**top_bit
    differ = partner - profiles
    real_part = jnp.where(upper_half, differ * jnp.cos(angles), profiles + partner)
    imag_part = jnp.where(upper_half, -differ * jnp.sin(angles), jnp.zeros_like(profiles))
    for bit_number in range(levels - 2, -1, -1):
        partner_real, partner_imag = swapped((real_part, imag_part), "bins", bit_number)
        upper_half = own_index >> bit_number & 1 == 1
        half_span = 2**bit_number
        angles = math.pi * (own_index % half_span).astype(jnp.float32) / half_span
        turned_real, turned_imag = rotate(
            partner_real - real_part, partner_imag - imag_part, angles
        )
        summed_real = real_part + partner_real
        summed_imag = imag_part + partner_imag
        real_part = jnp.where(upper_half, turned_real, summed_real)
        imag_part = jnp.where(upper_half, turned_imag, summed_imag)
    source_residue = reversed_bits(groups, levels)
    residue = jnp.asarray(source_residue)[own_index]
    positions = jnp.arange(length, dtype=jnp.int32)
    angles = 2.0 * math.pi * (positions * residue % full_length).astype(jnp.float32) / full_length
    real_part, imag_part = rotate(real_part, imag_part, angles[None, :])
    fine_sums, partial_power = strided_owners(
        real_part, imag_part, source_residue, owner_counts, capacity
    )
    summed_power = lax.psum(partial_power, "scans")
    mean_power = summed_power / (prof_rows * lax.axis_size("scans") * TILE)
    starts = jnp.cumsum(owner_counts) - owner_counts
    slot_index = jnp.arange(capacity, dtype=jnp.int32)
    own_start = starts[own_index]
    own_count = owner_counts[own_index]
    tile_ids = own_start + slot_index
    band_index = jnp.sum(
        (tile_ids[:, None] >= band_edges[None, 1:NCLASS]).astype(jnp.int32), axis=1
    )
    measured = measure(fine_sums, mean_power, band_index)
    previous = prev_state.reshape(capacity, prof_rows, 2, STATES)
    occupied = slot_index < own_count
    updated = update(dynamics, band_index, previous, measured, occupied)
    return updated.reshape(capacity, prof_rows, 2 * STATES)


def solution(mesh):
    return jax.shard_map(
        body,
        mesh=mesh,
        in_specs=(P("scans", "bins"), P(), P(), P(), P("bins", "scans", None)),
        out_specs=P("bins", "scans", None),
        check_vma=False,
    )
```

profile of v0, /device:TPU:0, one launch (start us, length us, event | category | flops | bytes accessed | tf_op | source)
XLA Modules:
  0.0 75.9 jit_solution(8045731173455339749)
XLA Ops:
  0.0 4.0 %collective-permute-start = (f32[1,32768]{1,0:T(1,128)}, f32[1,32768]{1,0:T(1,128)S(1)}, u32[]{:S(2)}, u32[]{:S(2)}) collective-permute-start(f32[1,32768]{1,0:T(1,128)} %param.6), channel_id=1, source_target_pairs={{0,16},{4,20},{8,24},{12,28},{16,0},{20,4},{24,8},{28,12},{1,17},{... | collective-permute-start | bytes 393224 | tf_op jit(solution)/shard_map/ppermute | solution.py:19
  4.4 0.8 %reduce-window.9 = s32[8,1]{0,1:T(1,128)S(1)} reduce-window(s32[8,1]{0,1:T(1,128)} %bitcast.100, s32[]{:T(128)} %constant.154.clone.1), window={size=8x1 pad=7_0x0_0}, to_apply=%region_0.1 | reduce-window | flops 56 | bytes 68 | tf_op jit(solution)/shard_map/reduce-window.4
  5.3 0.7 bitcast_subtract_fusion
  5.9 0.8 %fusion.117 = (f32[1,64,64]{2,1,0:T(8,128)S(1)}, f32[1,64,64]{2,1,0:T(8,128)S(1)}, f32[1,64,64]{2,1,0:T(8,128)S(1)}, f32[1,64,64]{2,1,0:T(8,128)S(1)}, f32[1,64,64]{2,1,0:T(8,128)S(1)}) fusion(f32[5,64,64]{2,1,0:T(8,128)} %param.9), kind=kLoop, calls=%fused_computation.171 | loop fusion | bytes 163840 | tf_op jit(solution)/shard_map/slice | solution.py:72
  6.8 0.6 dynamic_slice.10
  7.3 0.6 iota_add_fusion
  8.0 0.7 slice.18
  8.7 0.1 and_select_fusion.5
  9.0 0.2 and_select_fusion.1
  9.2 0.2 and_select_fusion.3
  9.4 0.2 stack.4
  9.6 1.0 %fusion.70 = f32[64,64,64]{2,0,1:T(8,128)S(1)} fusion(f32[5,64,64]{2,0,1:T(8,128)S(1)} %stack.4, s32[64]{0:T(128)S(1)} %convert_reduce_fusion), kind=kOutput, calls=%fused_computation.104 | convolution fusion | flops 15728960 | bytes 1130752 | tf_op jit(solution)/shard_map/rk,kij->rij/dot_general | solution.py:75
  10.8 0.2 broadcast_select_fusion
  11.0 1.6 %collective-permute-start.1 = (f32[1,32768]{1,0:T(1,128)S(1)}, f32[1,32768]{1,0:T(1,128)S(1)}, u32[]{:S(2)}, u32[]{:S(2)}) collective-permute-start(f32[1,32768]{1,0:T(1,128)S(1)} %get-tuple-element.14), channel_id=1, source_target_pairs={{0,8},{4,12},{8,0},{12,4},{16,24},{20,28},{24,16},{28,20},{1,9},{5... | collective-permute-start | bytes 393224 | tf_op jit(solution)/shard_map/ppermute | solution.py:19
  12.7 0.5 collective-permute-start.2
  13.1 4.3 %collective-permute-done.1 = f32[1,32768]{1,0:T(1,128)S(1)} collective-permute-done((f32[1,32768]{1,0:T(1,128)S(1)}, f32[1,32768]{1,0:T(1,128)S(1)}, u32[]{:S(2)}, u32[]{:S(2)}) %collective-permute-start.1) | collective-permute-done | bytes 131104 | tf_op jit(solution)/shard_map/ppermute | solution.py:19
  17.5 1.4 %collective-permute-done.2 = f32[1,32768]{1,0:T(1,128)S(1)} collective-permute-done((f32[1,32768]{1,0:T(1,128)S(1)}, f32[1,32768]{1,0:T(1,128)S(1)}, u32[]{:S(2)}, u32[]{:S(2)}) %collective-permute-start.2) | collective-permute-done | bytes 131104 | tf_op jit(solution)/shard_map/ppermute | solution.py:19
  18.9 0.4 broadcast_select_fusion.2
  19.3 1.6 %collective-permute-start.3 = (f32[1,32768]{1,0:T(1,128)S(1)}, f32[1,32768]{1,0:T(1,128)S(1)}, u32[]{:S(2)}, u32[]{:S(2)}) collective-permute-start(f32[1,32768]{1,0:T(1,128)S(1)} %get-tuple-element.12), channel_id=1, source_target_pairs={{0,4},{4,0},{8,12},{12,8},{16,20},{20,16},{24,28},{28,24},{1,5},{5... | collective-permute-start | bytes 393224 | tf_op jit(solution)/shard_map/ppermute | solution.py:19
  20.9 0.5 collective-permute-start.4
  21.5 0.6 dynamic_slice.11
  22.1 2.7 %collective-permute-done.3 = f32[1,32768]{1,0:T(1,128)S(1)} collective-permute-done((f32[1,32768]{1,0:T(1,128)S(1)}, f32[1,32768]{1,0:T(1,128)S(1)}, u32[]{:S(2)}, u32[]{:S(2)}) %collective-permute-start.3) | collective-permute-done | bytes 131104 | tf_op jit(solution)/shard_map/ppermute | solution.py:19
  24.8 1.4 %collective-permute-done.4 = f32[1,32768]{1,0:T(1,128)S(1)} collective-permute-done((f32[1,32768]{1,0:T(1,128)S(1)}, f32[1,32768]{1,0:T(1,128)S(1)}, u32[]{:S(2)}, u32[]{:S(2)}) %collective-permute-start.4) | collective-permute-done | bytes 131104 | tf_op jit(solution)/shard_map/ppermute | solution.py:19
  26.2 0.3 broadcast_select_fusion.4
  26.6 6.5 %subtract_reduce_fusion = (f32[32768]{0:T(1024)S(1)}, f32[32768]{0:T(1024)S(1)}) fusion(f32[1,32768]{1,0:T(1,128)S(1)} %get-tuple-element.10, f32[1,32768]{1,0:T(1,128)S(1)} %get-tuple-element.9, s32[]{:T(128)} %bitcast.13), kind=kLoop, calls=%fused_computation.57 | loop fusion | flops 655360 | bytes 524292 | tf_op jit(solution)/shard_map/sub | solution.py:35
  33.1 0.6 fusion.58
  33.7 0.5 fusion.60
  34.2 0.5 fusion.2
  34.8 0.5 fusion.3
  35.3 1.3 %fusion.31 = f32[128,128]{1,0:T(8,128)S(1)} fusion(f32[1,128,256]{1,2,0:T(8,128)S(1)} %fusion.2, f32[1,128,256]{1,2,0:T(8,128)S(1)} %fusion.3), kind=kOutput, calls=%fused_computation.48 | convolution fusion | flops 51347456 | bytes 327680 | tf_op jit(solution)/shard_map/nc,pbn->cbp/dot_general | solution.py:40
  36.6 1.3 %fusion.27 = f32[128,128]{1,0:T(8,128)S(1)} fusion(f32[1,128,256]{1,2,0:T(8,128)S(1)} %fusion.3, f32[1,128,256]{1,2,0:T(8,128)S(1)} %fusion.2), kind=kOutput, calls=%fused_computation.44 | convolution fusion | flops 51347456 | bytes 327680 | tf_op jit(solution)/shard_map/nc,pbn->cbp/dot_general | solution.py:43
  37.9 1.3 %fusion.8 = f32[128,128,1]{0,1,2:T(8,128)S(1)} fusion(f32[128,128]{1,0:T(8,128)S(1)} %fusion.31, f32[1,128,256]{1,2,0:T(8,128)S(1)} %fusion.3, f32[1,128,256]{1,2,0:T(8,128)S(1)} %fusion.2), kind=kOutput, calls=%fused_computation.11 | convolution fusion | flops 51363840 | bytes 393216 | tf_op jit(solution)/shard_map/nc,pbn->cbp/dot_general | solution.py:40
  39.4 1.3 %fusion.7 = f32[128,128,1]{0,1,2:T(8,128)S(1)} fusion(f32[128,128]{1,0:T(8,128)S(1)} %fusion.27, f32[1,128,256]{1,2,0:T(8,128)S(1)} %fusion.2, f32[1,128,256]{1,2,0:T(8,128)S(1)} %fusion.3), kind=kOutput, calls=%fused_computation.9 | convolution fusion | flops 51363840 | bytes 393216 | tf_op jit(solution)/shard_map/nc,pbn->cbp/dot_general | solution.py:43
  41.2 1.0 %gather_fusion = f32[512,128]{1,0:T(8,128)S(1)} fusion(f32[256,128]{1,0:T(8,128)S(1)} %copy.50, s32[1024]{0:T(1024)S(1)} %pad_clamp_fusion), kind=kCustom, calls=%fused_computation | custom fusion | bytes 526336 | tf_op jit(solution)/shard_map/gather | solution.py:138
  42.2 1.4 %multiply_reduce_fusion = (f32[8,64]{1,0:T(8,128)}, f32[8,64,128]{2,1,0:T(8,128)}) fusion(f32[8,64,128]{2,1,0:T(8,128)S(1)} %bitcast.88, pred[8,64]{1,0:T(8,128)(4,1)S(1)} %iota_compare_fusion.1), kind=kLoop, calls=%fused_computation.20 | loop fusion | flops 196096 | bytes 526848 | tf_op jit(solution)/shard_map/reduce_sum | solution.py:139
  43.6 6.5 %all-to-all-start.1 = ((f32[8,1,64]{2,1,0:T(1,128)}), f32[8,1,64]{2,1,0:T(1,128)S(1)}, u32[]{:S(2)}, u32[]{:S(2)}) async-start(f32[8,1,64]{2,1,0:T(1,128)} %bitcast.32), calls=%async_computation.1 | async-start | bytes 8192 | tf_op jit(solution)/shard_map/all_to_all | solution.py:83
  50.2 0.7 dynamic_slice.9
  50.8 5.7 %all-to-all-done.1 = f32[8,1,64]{2,1,0:T(1,128)S(1)} async-done(((f32[8,1,64]{2,1,0:T(1,128)}), f32[8,1,64]{2,1,0:T(1,128)S(1)}, u32[]{:S(2)}, u32[]{:S(2)}) %all-to-all-start.1) | async-done | bytes 2080 | tf_op jit(solution)/shard_map/all_to_all | solution.py:83
  56.6 3.4 %all-to-all-start = ((f32[8,64,128]{2,1,0:T(8,128)}), f32[8,64,128]{2,1,0:T(8,128)S(1)}, u32[]{:S(2)}, u32[]{:S(2)}) async-start(f32[8,64,128]{2,1,0:T(8,128)} %get-tuple-element.8), calls=%async_computation | async-start | bytes 524288 | tf_op jit(solution)/shard_map/all_to_all | solution.py:82
  60.0 0.6 iota_compare_fusion.8
  60.6 0.5 broadcast.716
  61.1 0.7 reduce.16
  62.1 6.2 %psum.7 = f32[64]{0:T(128)S(1)} all-reduce(f32[64]{0:T(128)S(1)} %reduce_sum.77), channel_id=1, replica_groups=mesh['bins'=8,'scans'=4] {'scans'}, use_global_device_ids=true, to_apply=%region_4.5 | all-reduce | flops 64 | bytes 512 | tf_op jit(solution)/shard_map/psum | solution.py:189
  68.3 0.3 reshape.673
  68.6 0.5 convolution_bitcast_fusion
  69.8 0.1 copy.60
  69.9 5.2 %fusion.12 = f32[64,1,2,64]{3,2,0,1:T(2,128)S(1)} fusion(f32[64,2,64]{2,1,0:T(2,128)S(1)} %reshape.667, f32[64,64,64]{2,0,1:T(8,128)S(1)} %fusion.70, f32[64,1,2,4]{3,2,0,1:T(2,128)S(1)} %bitcast.99, f32[64,1,2,8]{3,2,0,1:T(2,128)S(1)} %bitcast.98, f32[64,1,2,16]{3,2,0,1:T(2,128)S(1)} %bitcast.96, f32[64,1,2,32]{3,2,0,1:T(2,128)S(1)} %bitcast.97, ...), kind=kOutput, calls=%fused_computation.14 | convolution fusion | flops 6422528 | bytes 1179264 | tf_op jit(solution)/shard_map/rij,rpcj->rpci/dot_general | solution.py:76
  75.2 0.7 reshape.678
  (44 shorter events, 1.9 us)
Async XLA Ops:
  0.0 10.8 %copy-start = (f32[1,32768]{1,0:T(1,128)S(1)}, f32[1,32768]{1,0:T(1,128)}, u32[]{:S(2)}) copy-start(f32[1,32768]{1,0:T(1,128)} %param.6) | copy-start | bytes 393220
  0.0 10.8 %collective-permute-start = (f32[1,32768]{1,0:T(1,128)}, f32[1,32768]{1,0:T(1,128)S(1)}, u32[]{:S(2)}, u32[]{:S(2)}) collective-permute-start(f32[1,32768]{1,0:T(1,128)} %param.6), channel_id=1, source_target_pairs={{0,16},{4,20},{8,24},{12,28},{16,0},{20,4},{24,8},{28,12},{1,17},{... | collective-permute-start | bytes 393224 | tf_op jit(solution)/shard_map/ppermute | solution.py:19
  9.2 12.2 %copy-start.3 = (s32[8]{0:T(128)S(1)}, s32[8]{0:T(128)}, u32[]{:S(2)}) copy-start(s32[8]{0:T(128)} %param.8) | copy-start | bytes 100
  9.4 12.1 %copy-start.2 = (s32[8]{0:T(128)S(1)}, s32[8]{0:T(128)}, u32[]{:S(2)}) copy-start(s32[8]{0:T(128)} %constant.187.clone) | copy-start | bytes 100
  11.0 6.4 %collective-permute-start.1 = (f32[1,32768]{1,0:T(1,128)S(1)}, f32[1,32768]{1,0:T(1,128)S(1)}, u32[]{:S(2)}, u32[]{:S(2)}) collective-permute-start(f32[1,32768]{1,0:T(1,128)S(1)} %get-tuple-element.14), channel_id=1, source_target_pairs={{0,8},{4,12},{8,0},{12,4},{16,24},{20,28},{24,16},{28,20},{1,9},{5... | collective-permute-start | bytes 393224 | tf_op jit(solution)/shard_map/ppermute | solution.py:19
  12.7 6.2 %collective-permute-start.2 = (f32[1,32768]{1,0:T(1,128)S(1)}, f32[1,32768]{1,0:T(1,128)S(1)}, u32[]{:S(2)}, u32[]{:S(2)}) collective-permute-start(f32[1,32768]{1,0:T(1,128)S(1)} %get-tuple-element.13), channel_id=1, source_target_pairs={{0,8},{4,12},{8,0},{12,4},{16,24},{20,28},{24,16},{28,20},{1,9},{5... | collective-permute-start | bytes 393224 | tf_op jit(solution)/shard_map/ppermute | solution.py:19
  19.3 5.5 %collective-permute-start.3 = (f32[1,32768]{1,0:T(1,128)S(1)}, f32[1,32768]{1,0:T(1,128)S(1)}, u32[]{:S(2)}, u32[]{:S(2)}) collective-permute-start(f32[1,32768]{1,0:T(1,128)S(1)} %get-tuple-element.12), channel_id=1, source_target_pairs={{0,4},{4,0},{8,12},{12,8},{16,20},{20,16},{24,28},{28,24},{1,5},{5... | collective-permute-start | bytes 393224 | tf_op jit(solution)/shard_map/ppermute | solution.py:19
  20.9 5.3 %collective-permute-start.4 = (f32[1,32768]{1,0:T(1,128)S(1)}, f32[1,32768]{1,0:T(1,128)S(1)}, u32[]{:S(2)}, u32[]{:S(2)}) collective-permute-start(f32[1,32768]{1,0:T(1,128)S(1)} %get-tuple-element.11), channel_id=1, source_target_pairs={{0,4},{4,0},{8,12},{12,8},{16,20},{20,16},{24,28},{28,24},{1,5},{5... | collective-permute-start | bytes 393224 | tf_op jit(solution)/shard_map/ppermute | solution.py:19
  40.9 20.2 %copy-start.1 = (f32[64,1,128]{2,1,0:T(1,128)S(1)}, f32[64,1,128]{2,1,0:T(1,128)}, u32[]{:S(2)}) copy-start(f32[64,1,128]{2,1,0:T(1,128)} %param.10) | copy-start | bytes 98308
  43.6 12.9 %all-to-all-start.1 = ((f32[8,1,64]{2,1,0:T(1,128)}), f32[8,1,64]{2,1,0:T(1,128)S(1)}, u32[]{:S(2)}, u32[]{:S(2)}) async-start(f32[8,1,64]{2,1,0:T(1,128)} %bitcast.32), calls=%async_computation.1 | async-start | bytes 8192 | tf_op jit(solution)/shard_map/all_to_all | solution.py:83
  56.6 11.7 %all-to-all-start = ((f32[8,64,128]{2,1,0:T(8,128)}), f32[8,64,128]{2,1,0:T(8,128)S(1)}, u32[]{:S(2)}, u32[]{:S(2)}) async-start(f32[8,64,128]{2,1,0:T(8,128)} %get-tuple-element.8), calls=%async_computation | async-start | bytes 524288 | tf_op jit(solution)/shard_map/all_to_all | solution.py:82
where the time goes:
time: 76.3 us; the launch traced here: 75.9 us
  starting transfers between devices  18.2 us (24%)
  waiting for transfers between devices  15.6 us (20%)
  matrix products  14.2 us (19%)
  other arithmetic  13.5 us (18%)
  local copies, waits for them, and re-layouts  7.61 us (10%)
  blocking collectives  6.17 us (8%)
    ppermute x5, waiting for transfers between devices, swapped(): lax.ppermute(shard, axis, [(i, i ^ 1 << apart) for i in range(lax.axis_si...  9.82 us
    ppermute x5, starting transfers between devices, swapped(): lax.ppermute(shard, axis, [(i, i ^ 1 << apart) for i in range(lax.axis_si...  8.22 us
    all_to_all x1, starting transfers between devices, owner_relay(): lax.all_to_all(powers, 'bins', split_axis=0, concat_axis=0, tiled=True)  6.54 us
    sub x1, other arithmetic, rotate(): imag_part * cosine_part - real_part * sine_part  6.46 us
    psum x1, blocking collectives, body(): summed_power = lax.psum(partial_power, 'scans')  6.17 us
    all_to_all x1, waiting for transfers between devices, owner_relay(): lax.all_to_all(powers, 'bins', split_axis=0, concat_axis=0, tiled=True)  5.73 us
    dot_general x1, matrix products, update(): jnp.einsum('rij,rpcj->rpci', picked, previous, precision=HIGHEST) + measured  5.23 us
    all_to_all x1, starting transfers between devices, owner_relay(): lax.all_to_all(values, 'bins', split_axis=0, concat_axis=0, tiled=True)  3.41 us
  transfers between devices with their start and end apart: 7, of which 5 were waited for; matrix products, arithmetic and copies ran while one was open for 13% of the time, Pallas kernels for 0%

commit v1 on v0

v1 whole, which is shorter than its diff:
```python
import functools
import math

import jax
import jax.numpy as jnp
import numpy as np
from jax import lax
from jax.experimental import pallas as pl
from jax.experimental.pallas import tpu as pltpu
from jax.sharding import PartitionSpec as P

TILE = 512
STATES = 64
NCLASS = 5
LANES = 128

EPSILON = 1e-05
HIGHEST = lax.Precision.HIGHEST
BF16 = jnp.bfloat16
F32 = jnp.float32


def unit_root(order, exponents):
    angles = 2.0 * np.pi * (np.asarray(exponents, dtype=np.int64) % order) / order
    return np.cos(angles), -np.sin(angles)


def two_terms(values):
    high = np.asarray(values, np.float32).astype(BF16)
    low = (np.asarray(values, np.float64) - high.astype(np.float64)).astype(BF16)
    return high, low


def three_terms(values):
    high, low = two_terms(values)
    rest = np.asarray(values, np.float64) - high.astype(np.float64) - low.astype(np.float64)
    return high, low, rest.astype(BF16)


def split_two(values):
    high = values.astype(BF16)
    return high, (values - high.astype(F32)).astype(BF16)


def split_three(values):
    high = values.astype(BF16)
    rest = values - high.astype(F32)
    middle = rest.astype(BF16)
    return high, middle, (rest - middle.astype(F32)).astype(BF16)


def dot(left, right):
    return jnp.dot(left, right, preferred_element_type=F32)


VMEM = pl.BlockSpec(memory_space=pltpu.VMEM)
SMEM = pl.BlockSpec(memory_space=pltpu.SMEM)


def coarse_tables(coarse, groups):
    total = coarse * groups * LANES
    k_index = np.arange(coarse)
    real, imag = unit_root(coarse, k_index[:, None] * np.arange(coarse)[None, :])
    dft = np.stack(two_terms(np.concatenate([real, imag])))
    turn = np.stack(unit_root(total, k_index[:, None] * np.arange(LANES)[None, :]))
    real, imag = unit_root(total // LANES, k_index[:, None] * np.arange(groups)[None, :])
    row_turn = np.concatenate(three_terms(np.concatenate([real, imag])), axis=1)
    return dft, turn.astype(np.float32), row_turn


def coarse_kernel(coarse, groups, shares, x_ref, dft_ref, turn_ref, row_ref, out_ref):
    own = lax.axis_index("bins")
    high, low = split_two(x_ref[...])
    both = dot(dft_ref[0], jnp.concatenate([high, low], axis=1))
    spectrum = both[:, :LANES] + both[:, LANES:] + dot(dft_ref[1], high)
    picked = lax.broadcasted_iota(jnp.int32, (3 * groups, LANES), 0) % groups == own
    row_turn = dot(row_ref[...], jnp.where(picked, 1.0, 0.0).astype(BF16))
    row_real, row_imag = row_turn[:coarse], row_turn[coarse:]
    turn_real = turn_ref[0] * row_real - turn_ref[1] * row_imag
    turn_imag = turn_ref[0] * row_imag + turn_ref[1] * row_real
    real, imag = spectrum[:coarse], spectrum[coarse:]
    rows = coarse // shares
    out_ref[:, :rows, :] = (real * turn_real - imag * turn_imag).reshape(shares, rows, LANES)
    out_ref[:, rows:, :] = (real * turn_imag + imag * turn_real).reshape(shares, rows, LANES)


def coarse_step(columns, groups, shares):
    coarse = columns.shape[0]
    dft, turn, row_turn = coarse_tables(coarse, groups)
    return pl.pallas_call(
        functools.partial(coarse_kernel, coarse, groups, shares),
        out_shape=jax.ShapeDtypeStruct((shares, 2 * coarse // shares, LANES), F32),
        in_specs=[VMEM] * 4,
        out_specs=VMEM,
        compiler_params=pltpu.CompilerParams(vmem_limit_bytes=32 << 20),
        name="coarse_dft",
    )(columns, jnp.asarray(dft), jnp.asarray(turn), jnp.asarray(row_turn))


def fine_tables(groups):
    turn = np.stack(
        unit_root(groups * LANES, np.arange(groups)[:, None] * np.arange(LANES)[None, :])
    )
    real, imag = unit_root(LANES, np.arange(LANES)[:, None] * np.arange(LANES // 2)[None, :])
    matrix = np.block([[real, imag], [-imag, real]])
    return turn.astype(np.float32), np.concatenate(two_terms(matrix), axis=1)


def eight_point(values):
    half = math.sqrt(0.5)

    def add(p, q):
        return (p[0] + q[0], p[1] + q[1])

    def sub(p, q):
        return (p[0] - q[0], p[1] - q[1])

    def down(p):
        return (p[1], -p[0])

    def four(a, b, c, d):
        s0, s1, s2, s3 = add(a, c), sub(a, c), add(b, d), down(sub(b, d))
        return add(s0, s2), add(s1, s3), sub(s0, s2), sub(s1, s3)

    even = four(values[0], values[2], values[4], values[6])
    odd = four(values[1], values[3], values[5], values[7])
    turned = [
        odd[0],
        ((odd[1][0] + odd[1][1]) * half, (odd[1][1] - odd[1][0]) * half),
        down(odd[2]),
        ((odd[3][1] - odd[3][0]) * half, -(odd[3][0] + odd[3][1]) * half),
    ]
    return [add(e, t) for e, t in zip(even, turned)] + [sub(e, t) for e, t in zip(even, turned)]


def fine_kernel(profiles, capacity, counts_ref, x_ref, turn_ref, matrix_ref, out_ref):
    groups = 8
    blocks = {}
    for p in range(profiles):
        pieces = [
            (x_ref[c * profiles + p, :8, :], x_ref[c * profiles + p, 8:, :]) for c in range(groups)
        ]
        for u, (real, imag) in enumerate(eight_point(pieces)):
            if u:
                turn_real, turn_imag = turn_ref[0, u : u + 1, :], turn_ref[1, u : u + 1, :]
                real, imag = (
                    real * turn_real - imag * turn_imag,
                    real * turn_imag + imag * turn_real,
                )
            blocks[u, p] = (real, imag)
    order = [(u, p) for u in range(groups) for p in range(profiles)]
    left = jnp.concatenate(
        [
            jnp.concatenate([blocks[at][0] for at in order], axis=0),
            jnp.concatenate([blocks[at][1] for at in order], axis=0),
        ],
        axis=1,
    )
    high, low = split_two(left)
    both = dot(high, matrix_ref[...])
    spectrum = both[:, :LANES] + both[:, LANES:] + dot(low, matrix_ref[:, :LANES])
    by_block = spectrum.reshape(groups * profiles, 8, LANES)
    fine = jnp.sum(by_block, axis=1, keepdims=True)
    power = jnp.sum(
        (spectrum * spectrum).reshape(groups // 2, 2 * profiles * 8, LANES), axis=1, keepdims=True
    )
    power = power + pltpu.roll(power.reshape(groups // 2, LANES), LANES // 2, 1).reshape(
        groups // 2, 1, LANES
    )
    row_kind = lax.broadcasted_iota(jnp.int32, (4 * profiles, LANES), 0)
    halves = []
    for pair in range(groups // 2):
        block = jnp.where(row_kind % 4 == 2, jnp.broadcast_to(power[pair], row_kind.shape), 0.0)
        for h in range(2):
            for p in range(profiles):
                piece = jnp.broadcast_to(fine[(2 * pair + h) * profiles + p], row_kind.shape)
                block = jnp.where(row_kind == 4 * p + h, piece, block)
        halves.append(block)
    half = LANES // 2
    left = jnp.concatenate(
        [
            jnp.concatenate([block[:, :half] for block in halves], axis=1),
            jnp.concatenate([block[:, half:] for block in halves], axis=1),
        ],
        axis=0,
    )
    owner_of = lax.broadcasted_iota(jnp.int32, (1, groups * capacity), 1)
    rank_of, owner_of = owner_of % capacity, owner_of // capacity
    wanted = jnp.full((1, groups * capacity), -1, jnp.int32)
    start = jnp.int32(0)
    for owner in range(groups):
        count = counts_ref[owner]
        wanted = jnp.where((owner_of == owner) & (rank_of < count), start + rank_of, wanted)
        start = start + count
    tile_of = lax.broadcasted_iota(jnp.int32, (groups // 2 * half, groups * capacity), 0)
    tile_of = tile_of // half + (groups // 2) * (tile_of % half)
    chosen = jnp.where(tile_of == wanted, 1.0, 0.0).astype(BF16)
    rows = left.shape[0]
    routed = dot(jnp.concatenate(split_three(left), axis=0), chosen)
    routed = routed[:rows] + routed[rows : 2 * rows] + routed[2 * rows :]
    for owner in range(groups):
        piece = routed[:, owner * capacity : (owner + 1) * capacity]
        block = jnp.concatenate([piece[: rows // 2], piece[rows // 2 :]], axis=1)
        out_ref[owner] = block


def fine_step(arrived, owner_counts, groups, profiles, capacity):
    turn, matrix = fine_tables(groups)
    out = pl.pallas_call(
        functools.partial(fine_kernel, profiles, capacity),
        out_shape=jax.ShapeDtypeStruct((groups, 4 * profiles, LANES), F32),
        in_specs=[SMEM] + [VMEM] * 3,
        out_specs=VMEM,
        compiler_params=pltpu.CompilerParams(vmem_limit_bytes=32 << 20),
        name="fine_dft",
    )(owner_counts, arrived, jnp.asarray(turn), jnp.asarray(matrix))
    return out.reshape(groups * profiles, 4, LANES)


def fine_step_general(arrived, owner_counts, groups, capacity):
    rows = arrived.shape[1] // 2
    real, imag = arrived[:, :rows], arrived[:, rows:]

    def turned(pattern, root, parts):
        cosine, sine = (jnp.asarray(part.astype(np.float32)) for part in root)
        mul = functools.partial(jnp.einsum, pattern, precision=HIGHEST)
        return (
            mul(cosine, parts[0]) - mul(sine, parts[1]),
            mul(cosine, parts[1]) + mul(sine, parts[0]),
        )

    group_index, lane_index = np.arange(groups), np.arange(LANES)
    parts = turned(
        "cu,crj->urj", unit_root(groups, group_index[:, None] * group_index), (real, imag)
    )
    parts = turned(
        "uj,urj->urj", unit_root(groups * LANES, group_index[:, None] * lane_index), parts
    )
    real, imag = turned(
        "jv,urj->vur", unit_root(LANES, lane_index[:, None] * lane_index[: LANES // 2]), parts
    )
    tiles = groups * LANES // 4
    power = jnp.sum((real * real + imag * imag).reshape(tiles, 2 * rows), axis=1)
    fine_real = jnp.sum(real.reshape(tiles, 2, rows), axis=2)
    fine_imag = jnp.sum(imag.reshape(tiles, 2, rows), axis=2)
    starts = jnp.cumsum(owner_counts) - owner_counts
    slot_index = jnp.arange(capacity, dtype=jnp.int32)
    filled = slot_index[None, :] < owner_counts[:, None]
    chosen = jnp.clip(starts[:, None] + slot_index[None, :], 0, tiles - 1)

    def routed(values):
        return jnp.where(filled, values[chosen], 0.0)

    empty = jnp.zeros((groups, capacity), F32)
    payload = [
        [routed(fine_real[:, 0]), routed(fine_imag[:, 0])],
        [routed(fine_real[:, 1]), routed(fine_imag[:, 1])],
        [routed(power), routed(power)],
        [empty, empty],
    ]
    return jnp.stack([jnp.concatenate(row, axis=1) for row in payload], axis=1)


def pool_table(shares):
    pool = np.zeros((shares, 4, 6, STATES), np.float32)
    for share in range(shares):
        for h in range(2):
            for band in range(NCLASS):
                pool[share, h, band, (share + shares * h) >> band] = 1.0
        pool[share, 2, NCLASS, :] = 1.0
    return np.tile(pool.reshape(shares * 4, 6 * STATES), (3, 1)).astype(BF16)


def update_kernel(count, edges_ref, counts_ref, x_ref, pool_ref, dynamics_ref, state_ref, out_ref):
    own = lax.axis_index("bins")
    groups = counts_ref.shape[0]
    capacity = state_ref.shape[0]
    wide = NCLASS * STATES

    def before(owner, start):
        return start + jnp.where(owner < own, counts_ref[owner], 0)

    start = lax.fori_loop(0, groups, before, jnp.int32(0))
    own_count = counts_ref[own]
    state = state_ref[...]
    state = jnp.concatenate([state[:, :STATES], state[:, STATES:]], axis=0)
    row = lax.broadcasted_iota(jnp.int32, (wide, STATES), 0)
    column = lax.broadcasted_iota(jnp.int32, (wide, STATES), 1)
    limit = STATES >> (row // STATES)
    inside = (row % STATES < limit) & (column < limit)
    dynamics = jnp.where(inside, dynamics_ref[...], 0.0)
    moved = lax.dot_general(
        state, dynamics, (((1,), (1,)), ((), ())), precision=HIGHEST, preferred_element_type=F32
    )
    moved = jnp.concatenate([moved, jnp.zeros((2 * capacity, STATES), F32)], axis=1)
    sums = lax.dot_general(
        jnp.concatenate(split_three(x_ref[...]), axis=0),
        pool_ref[...],
        (((0,), (0,)), ((), ())),
        preferred_element_type=F32,
    )
    slot = lax.broadcasted_iota(jnp.int32, (2 * capacity, 6 * STATES), 0) % capacity
    lane_band = lax.broadcasted_iota(jnp.int32, (2 * capacity, 6 * STATES), 1) // STATES
    band = jnp.zeros_like(slot)
    for edge in range(1, NCLASS):
        band = band + jnp.where(slot + start >= edges_ref[edge], 1, 0)
    wanted = lane_band == band

    def of_band(values):
        values = jnp.where(wanted, values, 0.0)
        folded = values[:, :LANES] + values[:, LANES : 2 * LANES] + values[:, 2 * LANES :]
        return folded[:, :STATES] + folded[:, STATES:]

    power = sums[:, wide:] * (1.0 / count)
    span = jnp.left_shift(TILE // STATES, band[:, :STATES]).astype(F32)
    scaling = 1.0 / jnp.sqrt(span * (power + EPSILON))
    result = of_band(moved) + of_band(sums) * scaling
    result = jnp.where(slot[:, :STATES] < own_count, result, 0.0)
    out_ref[...] = jnp.concatenate([result[:capacity], result[capacity:]], axis=1)


def update_step(arrived, band_edges, owner_counts, dynamics, state, count):
    shares = arrived.shape[0]
    return pl.pallas_call(
        functools.partial(update_kernel, count),
        out_shape=jax.ShapeDtypeStruct(state.shape, F32),
        in_specs=[SMEM, SMEM] + [VMEM] * 4,
        out_specs=VMEM,
        compiler_params=pltpu.CompilerParams(vmem_limit_bytes=32 << 20),
        name="state_update",
    )(
        band_edges,
        owner_counts,
        arrived.reshape(shares * 4, LANES),
        jnp.asarray(pool_table(shares)),
        dynamics.reshape(NCLASS * STATES, STATES),
        state,
    )


def exchanged(values, axes):
    return lax.all_to_all(values, axes, split_axis=0, concat_axis=0, tiled=True)


def body(profiles, band_edges, owner_counts, dynamics, prev_state):
    groups, scans = lax.axis_size("bins"), lax.axis_size("scans")
    prof_rows, length = profiles.shape
    capacity = prev_state.shape[0]
    coarse = length // LANES
    shares = TILE // 16
    count = prof_rows * scans * TILE
    columns = profiles.reshape(coarse // groups, groups, LANES).transpose(1, 0, 2)
    columns = exchanged(columns, "bins").reshape(coarse, LANES)
    if groups * scans == shares and groups == 8:
        blocks = coarse_step(columns, groups, shares)
        blocks = exchanged(blocks, ("bins", "scans"))
        payload = fine_step(blocks, owner_counts, groups, scans, capacity)
        arrived = exchanged(payload, ("bins", "scans"))
    else:
        blocks = coarse_step(columns, groups, groups)
        blocks = exchanged(blocks, "bins")
        payload = fine_step_general(blocks, owner_counts, groups, capacity)
        arrived = exchanged(payload, "bins")
        arrived = jnp.sum(arrived.reshape(shares, groups // shares, 4, LANES), axis=1)
        power = lax.psum(arrived[:, 2], "scans")
        arrived = jnp.concatenate([arrived[:, :2], power[:, None], arrived[:, 3:]], axis=1)
    state = prev_state.reshape(capacity, 2 * STATES)
    updated = update_step(arrived, band_edges, owner_counts, dynamics, state, count)
    return updated.reshape(prev_state.shape)


def solution(mesh):
    return jax.shard_map(
        body,
        mesh=mesh,
        in_specs=(P("scans", "bins"), P(), P(), P(), P("bins", "scans", None)),
        out_specs=P("bins", "scans", None),
        check_vma=False,
    )
```

time: 76.3 us -> 44.1 us (0.58)
  blocking collectives: 6.17 us -> 36.8 us
  starting transfers between devices: 18.2 us -> 0 us
  waiting for transfers between devices: 15.6 us -> 0 us
  matrix products: 14.2 us -> 0 us
  other arithmetic: 13.5 us -> 0 us
  local copies, waits for them, and re-layouts: 7.61 us -> 3.53 us
  Pallas kernels: 0 us -> 3.33 us
    all_to_all x0 -> x3, blocking collectives: none -> 36.8 us  [exchanged(): return lax.all_to_all(values, axes, split_axis=0, concat_axis=0, tiled=True)]
    dot_general x11 -> x0, matrix products: 14.2 us -> none  [the longest x1 5.23 us: update(): jnp.einsum('rij,rpcj->rpci', picked, previous, precision=HIGHEST) + measured]
    all_to_all x2 -> x0, starting transfers between devices: 9.95 us -> none  [the longest x1 6.54 us: owner_relay(): lax.all_to_all(powers, 'bins', split_axis=0, concat_axis=0, tiled=True)]
    ppermute x5 -> x0, waiting for transfers between devices: 9.82 us -> none  [swapped(): lax.ppermute(shard, axis, [(i, i ^ 1 << apart) for i in range(lax.axis_si...]
    ppermute x5 -> x0, starting transfers between devices: 8.22 us -> none  [swapped(): lax.ppermute(shard, axis, [(i, i ^ 1 << apart) for i in range(lax.axis_si...]
    sub x2 -> x0, other arithmetic: 7.12 us -> none  [the longest x1 6.46 us: rotate(): imag_part * cosine_part - real_part * sine_part]
    psum x1 -> x0, blocking collectives: 6.17 us -> none  [body(): summed_power = lax.psum(partial_power, 'scans')]
    all_to_all x2 -> x0, waiting for transfers between devices: 5.74 us -> none  [the longest x1 5.73 us: owner_relay(): lax.all_to_all(powers, 'bins', split_axis=0, concat_axis=0, tiled=True)]
  transfers between devices with their start and end apart: 7 -> 0, of which waited for: 5 -> 0; matrix products, arithmetic and copies ran while one was open for 13% -> 0% of each run, Pallas kernels for 0% -> 0%
where the time goes in v1:
time: 44.1 us; the launch traced here: 43.8 us
  blocking collectives  36.8 us (83%)
  local copies, waits for them, and re-layouts  3.53 us (8%)
  Pallas kernels  3.33 us (8%)
    all_to_all x3, blocking collectives, exchanged(): return lax.all_to_all(values, axes, split_axis=0, concat_axis=0, tiled=True)  36.8 us
    unnamed x20, local copies, waits for them, and re-layouts  2.54 us
    pallas_call x1, Pallas kernels, update_step(): pl.pallas_call(functools.partial(update_kernel, count), out_shape=jax.Sha...  1.8 us
    pallas_call x1, Pallas kernels, fine_step(): pl.pallas_call(functools.partial(fine_kernel, profiles, capacity), out_sh...  1.17 us
    reshape x1, local copies, waits for them, and re-layouts, body(): profiles.reshape(coarse // groups, groups, LANES).transpose(1, 0, 2)  0.99 us

profile of v1, /device:TPU:0, one launch (start us, length us, event | category | flops | bytes accessed | tf_op | source)
XLA Modules:
  0.0 43.8 jit_solution(8898268569349341791)
XLA Ops:
  0.0 0.0 copy-start
  0.0 1.0 %copy.15 = f32[32,8,128]{2,0,1:T(8,128)S(1)} copy(f32[32,8,128]{2,1,0:T(8,128)} %bitcast.18) | data formatting | bytes 262144 | tf_op jit(solution)/shard_map/reshape | solution.py:352
  1.0 14.4 %all_to_all.15 = f32[8,32,128]{2,1,0:T(8,128)S(1)} all-to-all(f32[8,32,128]{2,1,0:T(8,128)S(1)} %bitcast.17), channel_id=1, replica_groups=mesh['bins'=8,'scans'=4] {'bins'}, dimensions={0} | all-to-all | bytes 262144 | tf_op jit(solution)/shard_map/all_to_all | solution.py:342
  15.4 0.0 copy-done
  15.4 0.0 copy-start.2
  15.4 0.9 %copy-done.2 = f32[2,256,128]{2,1,0:T(8,128)S(1)} copy-done((f32[2,256,128]{2,1,0:T(8,128)S(1)}, f32[2,256,128]{2,1,0:T(8,128)}, u32[]{:S(2)}) %copy-start.2) | copy-done | bytes 262168
  16.4 0.0 copy-start.4
  16.4 0.9 %copy-done.4 = bf16[512,24]{1,0:T(8,128)(2,1)S(1)} copy-done((bf16[512,24]{1,0:T(8,128)(2,1)S(1)}, bf16[512,24]{1,0:T(8,128)(2,1)}, u32[]{:S(2)}) %copy-start.4) | copy-done | bytes 24600
  17.3 0.4 coarse_dft.1
  17.6 0.0 copy-start.5
  17.7 0.0 copy-start.7
  17.7 0.0 copy-start.8
  17.7 12.8 %all_to_all.16.x_ref = f32[32,16,128]{2,1,0:T(8,128)S(1)} all-to-all(f32[32,16,128]{2,1,0:T(8,128)S(1)} %coarse_dft.1), channel_id=1, replica_groups=mesh['bins'=8,'scans'=4] {'bins','scans'}, dimensions={0} | all-to-all | bytes 524288 | tf_op jit(solution)/shard_map/all_to_all | solution.py:342
  30.5 0.0 copy-done.5
  30.5 0.0 copy-done.7
  30.5 0.0 copy-done.8
  30.5 0.0 copy-start.1
  30.5 0.0 copy-start.3
  30.5 1.2 %fine_dft.1 = f32[8,16,128]{2,1,0:T(8,128)S(1)} custom-call(s32[8]{0:T(128)S(1)} %copy-done.8, f32[32,16,128]{2,1,0:T(8,128)S(1)} %all_to_all.16.x_ref, f32[2,8,128]{2,1,0:T(8,128)S(1)} %copy-done.7, bf16[256,256]{1,0:T(8,128)(2,1)S(1)} %copy-done.5), custom_call_target="tpu_custom_call" | custom-call | tf_op jit(solution)/shard_map/fine_dft/pallas_call | solution.py:209
  31.7 0.0 copy-start.6
  31.7 9.6 %all_to_all.17 = f32[32,4,128]{2,1,0:T(4,128)S(1)} all-to-all(f32[32,4,128]{2,1,0:T(4,128)S(1)} %bitcast.14), channel_id=1, replica_groups=mesh['bins'=8,'scans'=4] {'bins','scans'}, dimensions={0} | all-to-all | bytes 131072 | tf_op jit(solution)/shard_map/all_to_all | solution.py:342
  41.3 0.0 copy-start.9
  41.3 0.0 copy-done.1
  41.3 0.0 copy-done.3
  41.3 0.0 copy-done.6
  41.3 0.6 %copy-done.9 = s32[6]{0:T(128)S(1)} copy-done((s32[6]{0:T(128)S(1)}, s32[6]{0:T(128)}, u32[]{:S(2)}) %copy-start.9) | copy-done | bytes 48
  42.0 1.8 %state_update.1 = f32[64,128]{1,0:T(8,128)} custom-call(s32[6]{0:T(128)S(1)} %copy-done.9, s32[8]{0:T(128)S(1)} %copy-done.8, f32[128,128]{1,0:T(8,128)S(1)} %bitcast.13, bf16[384,384]{1,0:T(8,128)(2,1)S(1)} %copy-done.1, f32[320,64]{1,0:T(8,128)S(1)} %bitcast.15, f32[64,128]{1,0:T(8,128)S(1)} %bitcast.16), custom_call_target="tpu_custom_call" | custom-call | tf_op jit(solution)/shard_map/state_update/pallas_call | solution.py:324
Async XLA Ops:
  0.0 15.4 %copy-start = (bf16[2,512,256]{2,1,0:T(8,128)(2,1)S(1)}, bf16[2,512,256]{2,1,0:T(8,128)(2,1)}, u32[]{:S(2)}) copy-start(bf16[2,512,256]{2,1,0:T(8,128)(2,1)} %constant.12.clone.dft_ref) | copy-start | bytes 1572868
  15.4 1.0 %copy-start.2 = (f32[2,256,128]{2,1,0:T(8,128)S(1)}, f32[2,256,128]{2,1,0:T(8,128)}, u32[]{:S(2)}) copy-start(f32[2,256,128]{2,1,0:T(8,128)} %constant.13.clone.turn_ref) | copy-start | bytes 786436
  16.4 0.9 %copy-start.4 = (bf16[512,24]{1,0:T(8,128)(2,1)S(1)}, bf16[512,24]{1,0:T(8,128)(2,1)}, u32[]{:S(2)}) copy-start(bf16[512,24]{1,0:T(8,128)(2,1)} %constant.14.clone.row_ref) | copy-start | bytes 73732
  17.6 12.8 %copy-start.5 = (bf16[256,256]{1,0:T(8,128)(2,1)S(1)}, bf16[256,256]{1,0:T(8,128)(2,1)}, u32[]{:S(2)}) copy-start(bf16[256,256]{1,0:T(8,128)(2,1)} %constant.16.clone.matrix_ref) | copy-start | bytes 393220
  17.7 12.8 %copy-start.7 = (f32[2,8,128]{2,1,0:T(8,128)S(1)}, f32[2,8,128]{2,1,0:T(8,128)}, u32[]{:S(2)}) copy-start(f32[2,8,128]{2,1,0:T(8,128)} %constant.15.clone.turn_ref) | copy-start | bytes 24580
  17.7 12.8 %copy-start.8 = (s32[8]{0:T(128)S(1)}, s32[8]{0:T(128)}, u32[]{:S(2)}) copy-start(s32[8]{0:T(128)} %counts_ref.3) | copy-start | bytes 100
  30.5 10.8 %copy-start.1 = (bf16[384,384]{1,0:T(8,128)(2,1)S(1)}, bf16[384,384]{1,0:T(8,128)(2,1)}, u32[]{:S(2)}) copy-start(bf16[384,384]{1,0:T(8,128)(2,1)} %constant.17.clone.pool_ref) | copy-start | bytes 884740
  30.5 10.8 %copy-start.3 = (f32[5,64,64]{2,1,0:T(8,128)S(1)}, f32[5,64,64]{2,1,0:T(8,128)}, u32[]{:S(2)}) copy-start(f32[5,64,64]{2,1,0:T(8,128)} %param.14) | copy-start | bytes 245764
  31.7 9.6 %copy-start.6 = (f32[64,1,128]{2,1,0:T(1,128)S(1)}, f32[64,1,128]{2,1,0:T(1,128)}, u32[]{:S(2)}) copy-start(f32[64,1,128]{2,1,0:T(1,128)} %param.15) | copy-start | bytes 98308
  41.3 0.7 %copy-start.9 = (s32[6]{0:T(128)S(1)}, s32[6]{0:T(128)}, u32[]{:S(2)}) copy-start(s32[6]{0:T(128)} %edges_ref.1) | copy-start | bytes 76

commit v2 on v1

--- a/solution.py
+++ b/solution.py
@@ -57,27 +57,35 @@
 SMEM = pl.BlockSpec(memory_space=pltpu.SMEM)
 
 
-def coarse_tables(coarse, groups):
+def coarse_table(coarse, groups):
     total = coarse * groups * LANES
     k_index = np.arange(coarse)
-    real, imag = unit_root(coarse, k_index[:, None] * np.arange(coarse)[None, :])
-    dft = np.stack(two_terms(np.concatenate([real, imag])))
-    turn = np.stack(unit_root(total, k_index[:, None] * np.arange(LANES)[None, :]))
-    real, imag = unit_root(total // LANES, k_index[:, None] * np.arange(groups)[None, :])
-    row_turn = np.concatenate(three_terms(np.concatenate([real, imag])), axis=1)
-    return dft, turn.astype(np.float32), row_turn
-
-
-def coarse_kernel(coarse, groups, shares, x_ref, dft_ref, turn_ref, row_ref, out_ref):
+
+    def stacked(order, others):
+        return np.concatenate(unit_root(order, k_index[:, None] * others[None, :]))
+
+    columns = two_terms(stacked(coarse, np.arange(coarse)))
+    columns += three_terms(stacked(total, np.arange(LANES)))
+    columns += three_terms(stacked(total // LANES, np.arange(groups)))
+    table = np.concatenate(columns, axis=1)
+    return np.pad(table, [(0, 0), (0, -table.shape[1] % LANES)])
+
+
+def coarse_kernel(coarse, groups, shares, x_ref, table_ref, out_ref):
     own = lax.axis_index("bins")
     high, low = split_two(x_ref[...])
-    both = dot(dft_ref[0], jnp.concatenate([high, low], axis=1))
-    spectrum = both[:, :LANES] + both[:, LANES:] + dot(dft_ref[1], high)
-    picked = lax.broadcasted_iota(jnp.int32, (3 * groups, LANES), 0) % groups == own
-    row_turn = dot(row_ref[...], jnp.where(picked, 1.0, 0.0).astype(BF16))
+    both = dot(table_ref[:, :coarse], jnp.concatenate([high, low], axis=1))
+    spectrum = both[:, :LANES] + both[:, LANES:] + dot(table_ref[:, coarse : 2 * coarse], high)
+    at = 2 * coarse
+    turn = sum(table_ref[:, at + i * LANES : at + (i + 1) * LANES].astype(F32) for i in range(3))
+    at += 3 * LANES
+    entries = table_ref.shape[1] - at
+    entry = lax.broadcasted_iota(jnp.int32, (entries, LANES), 0)
+    picked = (entry % groups == own) & (entry < 3 * groups)
+    row_turn = dot(table_ref[:, at:], jnp.where(picked, 1.0, 0.0).astype(BF16))
     row_real, row_imag = row_turn[:coarse], row_turn[coarse:]
-    turn_real = turn_ref[0] * row_real - turn_ref[1] * row_imag
-    turn_imag = turn_ref[0] * row_imag + turn_ref[1] * row_real
+    turn_real = turn[:coarse] * row_real - turn[coarse:] * row_imag
+    turn_imag = turn[:coarse] * row_imag + turn[coarse:] * row_real
     real, imag = spectrum[:coarse], spectrum[coarse:]
     rows = coarse // shares
     out_ref[:, :rows, :] = (real * turn_real - imag * turn_imag).reshape(shares, rows, LANES)
@@ -86,15 +94,14 @@
 
 def coarse_step(columns, groups, shares):
     coarse = columns.shape[0]
-    dft, turn, row_turn = coarse_tables(coarse, groups)
     return pl.pallas_call(
         functools.partial(coarse_kernel, coarse, groups, shares),
         out_shape=jax.ShapeDtypeStruct((shares, 2 * coarse // shares, LANES), F32),
-        in_specs=[VMEM] * 4,
+        in_specs=[VMEM] * 2,
         out_specs=VMEM,
         compiler_params=pltpu.CompilerParams(vmem_limit_bytes=32 << 20),
         name="coarse_dft",
-    )(columns, jnp.asarray(dft), jnp.asarray(turn), jnp.asarray(row_turn))
+    )(columns, jnp.asarray(coarse_table(coarse, groups)))
 
 
 def fine_tables(groups):
@@ -271,7 +278,7 @@
     return np.tile(pool.reshape(shares * 4, 6 * STATES), (3, 1)).astype(BF16)
 
 
-def update_kernel(count, edges_ref, counts_ref, x_ref, pool_ref, dynamics_ref, state_ref, out_ref):
+def state_kernel(edges_ref, counts_ref, dynamics_ref, state_ref, moved_ref, band_ref):
     own = lax.axis_index("bins")
     groups = counts_ref.shape[0]
     capacity = state_ref.shape[0]
@@ -281,7 +288,12 @@
         return start + jnp.where(owner < own, counts_ref[owner], 0)
 
     start = lax.fori_loop(0, groups, before, jnp.int32(0))
-    own_count = counts_ref[own]
+    slot = lax.broadcasted_iota(jnp.int32, (2 * capacity, LANES), 0) % capacity
+    band = jnp.zeros_like(slot)
+    for edge in range(1, NCLASS):
+        band = band + jnp.where(slot + start >= edges_ref[edge], 1, 0)
+    band = jnp.where(slot < counts_ref[own], band, -1)
+    band_ref[...] = band
     state = state_ref[...]
     state = jnp.concatenate([state[:, :STATES], state[:, STATES:]], axis=0)
     row = lax.broadcasted_iota(jnp.int32, (wide, STATES), 0)
@@ -293,49 +305,60 @@
         state, dynamics, (((1,), (1,)), ((), ())), precision=HIGHEST, preferred_element_type=F32
     )
     moved = jnp.concatenate([moved, jnp.zeros((2 * capacity, STATES), F32)], axis=1)
+    moved_ref[...] = of_band(moved, band)
+
+
+def of_band(values, band):
+    lane = lax.broadcasted_iota(jnp.int32, band.shape, 1) // STATES
+    folded = jnp.zeros(band.shape, F32)
+    for pair in range((NCLASS + 1) // 2):
+        piece = values[:, pair * LANES : (pair + 1) * LANES]
+        folded = folded + jnp.where(lane + 2 * pair == band, piece, 0.0)
+    return folded[:, :STATES] + folded[:, STATES:]
+
+
+def update_kernel(count, x_ref, pool_ref, moved_ref, band_ref, out_ref):
+    capacity = out_ref.shape[0]
+    band = band_ref[...]
     sums = lax.dot_general(
         jnp.concatenate(split_three(x_ref[...]), axis=0),
         pool_ref[...],
         (((0,), (0,)), ((), ())),
         preferred_element_type=F32,
     )
-    slot = lax.broadcasted_iota(jnp.int32, (2 * capacity, 6 * STATES), 0) % capacity
-    lane_band = lax.broadcasted_iota(jnp.int32, (2 * capacity, 6 * STATES), 1) // STATES
-    band = jnp.zeros_like(slot)
-    for edge in range(1, NCLASS):
-        band = band + jnp.where(slot + start >= edges_ref[edge], 1, 0)
-    wanted = lane_band == band
-
-    def of_band(values):
-        values = jnp.where(wanted, values, 0.0)
-        folded = values[:, :LANES] + values[:, LANES : 2 * LANES] + values[:, 2 * LANES :]
-        return folded[:, :STATES] + folded[:, STATES:]
-
-    power = sums[:, wide:] * (1.0 / count)
-    span = jnp.left_shift(TILE // STATES, band[:, :STATES]).astype(F32)
+    power = sums[:, NCLASS * STATES :] * (1.0 / count)
+    span = jnp.left_shift(TILE // STATES, jnp.maximum(band[:, :STATES], 0)).astype(F32)
     scaling = 1.0 / jnp.sqrt(span * (power + EPSILON))
-    result = of_band(moved) + of_band(sums) * scaling
-    result = jnp.where(slot[:, :STATES] < own_count, result, 0.0)
+    result = moved_ref[...] + of_band(sums, band) * scaling
     out_ref[...] = jnp.concatenate([result[:capacity], result[capacity:]], axis=1)
 
 
-def update_step(arrived, band_edges, owner_counts, dynamics, state, count):
+def state_step(band_edges, owner_counts, dynamics, state):
+    rows = 2 * state.shape[0]
+    return pl.pallas_call(
+        state_kernel,
+        out_shape=(
+            jax.ShapeDtypeStruct((rows, STATES), F32),
+            jax.ShapeDtypeStruct((rows, LANES), jnp.int32),
+        ),
+        in_specs=[SMEM, SMEM, VMEM, VMEM],
+        out_specs=(VMEM, VMEM),
+        compiler_params=pltpu.CompilerParams(vmem_limit_bytes=32 << 20),
+        cost_estimate=pl.CostEstimate(flops=1 << 25, bytes_accessed=1 << 19, transcendentals=0),
+        name="state_step",
+    )(band_edges, owner_counts, dynamics.reshape(NCLASS * STATES, STATES), state)
+
+
+def update_step(arrived, moved, band, count):
     shares = arrived.shape[0]
     return pl.pallas_call(
         functools.partial(update_kernel, count),
-        out_shape=jax.ShapeDtypeStruct(state.shape, F32),
-        in_specs=[SMEM, SMEM] + [VMEM] * 4,
+        out_shape=jax.ShapeDtypeStruct((moved.shape[0] // 2, 2 * STATES), F32),
+        in_specs=[VMEM] * 4,
         out_specs=VMEM,
         compiler_params=pltpu.CompilerParams(vmem_limit_bytes=32 << 20),
         name="state_update",
-    )(
-        band_edges,
-        owner_counts,
-        arrived.reshape(shares * 4, LANES),
-        jnp.asarray(pool_table(shares)),
-        dynamics.reshape(NCLASS * STATES, STATES),
-        state,
-    )
+    )(arrived.reshape(shares * 4, LANES), jnp.asarray(pool_table(shares)), moved, band)
 
 
 def exchanged(values, axes):
@@ -349,6 +372,8 @@
     coarse = length // LANES
     shares = TILE // 16
     count = prof_rows * scans * TILE
+    state = prev_state.reshape(capacity, 2 * STATES)
+    moved, band = state_step(band_edges, owner_counts, dynamics, state)
     columns = profiles.reshape(coarse // groups, groups, LANES).transpose(1, 0, 2)
     columns = exchanged(columns, "bins").reshape(coarse, LANES)
     if groups * scans == shares and groups == 8:
@@ -364,8 +389,7 @@
         arrived = jnp.sum(arrived.reshape(shares, groups // shares, 4, LANES), axis=1)
         power = lax.psum(arrived[:, 2], "scans")
         arrived = jnp.concatenate([arrived[:, :2], power[:, None], arrived[:, 3:]], axis=1)
-    state = prev_state.reshape(capacity, 2 * STATES)
-    updated = update_step(arrived, band_edges, owner_counts, dynamics, state, count)
+    updated = update_step(arrived, moved, band, count)
     return updated.reshape(prev_state.shape)
 
 

time: 44.1 us -> 43.1 us (0.977)
  blocking collectives: 36.8 us -> 27.2 us
  waiting for transfers between devices: 0 us -> 5.71 us
  starting transfers between devices: 0 us -> 2.68 us
  Pallas kernels: 3.33 us -> 4.23 us
  local copies, waits for them, and re-layouts: 3.53 us -> 2.82 us
    all_to_all x3 -> x2, blocking collectives: 36.8 us -> 27.2 us  [exchanged(): return lax.all_to_all(values, axes, split_axis=0, concat_axis=0, tiled=True)]
    all_to_all x0 -> x1, waiting for transfers between devices: none -> 5.71 us  [exchanged(): return lax.all_to_all(values, axes, split_axis=0, concat_axis=0, tiled=True)]
    all_to_all x0 -> x1, starting transfers between devices: none -> 2.68 us  [exchanged(): return lax.all_to_all(values, axes, split_axis=0, concat_axis=0, tiled=True)]
    pallas_call x0 -> x1, Pallas kernels: none -> 1.03 us  [state_step(): pl.pallas_call(state_kernel, out_shape=(jax.ShapeDtypeStruct((rows, STATE...]
    pallas_call x1, Pallas kernels: 1.8 us -> 1.04 us  [update_step(): pl.pallas_call(functools.partial(update_kernel, count), out_shape=jax.Sha...]
    unnamed x20 -> x16, local copies, waits for them, and re-layouts: 2.54 us -> 1.89 us
    pallas_call x1, Pallas kernels: 1.17 us -> 1.8 us  [fine_step(): pl.pallas_call(functools.partial(fine_kernel, profiles, capacity), out_sh...]
  transfers between devices with their start and end apart: 0 -> 1, of which waited for: 0 -> 1; matrix products, arithmetic and copies ran while one was open for 0% -> 0% of each run, Pallas kernels for 0% -> 2%
where the time goes in v2:
time: 43.1 us; the launch traced here: 42.8 us
  blocking collectives  27.2 us (63%)
  waiting for transfers between devices  5.71 us (13%)
  Pallas kernels  4.23 us (10%)
  local copies, waits for them, and re-layouts  2.82 us (7%)
  starting transfers between devices  2.68 us (6%)
    all_to_all x2, blocking collectives, exchanged(): return lax.all_to_all(values, axes, split_axis=0, concat_axis=0, tiled=True)  27.2 us
    all_to_all x1, waiting for transfers between devices, exchanged(): return lax.all_to_all(values, axes, split_axis=0, concat_axis=0, tiled=True)  5.71 us
    all_to_all x1, starting transfers between devices, exchanged(): return lax.all_to_all(values, axes, split_axis=0, concat_axis=0, tiled=True)  2.68 us
    unnamed x16, local copies, waits for them, and re-layouts  1.89 us
    pallas_call x1, Pallas kernels, fine_step(): pl.pallas_call(functools.partial(fine_kernel, profiles, capacity), out_sh...  1.8 us
    pallas_call x1, Pallas kernels, update_step(): pl.pallas_call(functools.partial(update_kernel, count), out_shape=jax.Sha...  1.04 us
    pallas_call x1, Pallas kernels, state_step(): pl.pallas_call(state_kernel, out_shape=(jax.ShapeDtypeStruct((rows, STATE...  1.03 us
    reshape x1, local copies, waits for them, and re-layouts, body(): profiles.reshape(coarse // groups, groups, LANES).transpose(1, 0, 2)  0.93 us
  transfers between devices with their start and end apart: 1, of which 1 were waited for; matrix products, arithmetic and copies ran while one was open for 0% of the time, Pallas kernels for 2%

profile of v2, /device:TPU:0, one launch (start us, length us, event | category | flops | bytes accessed | tf_op | source)
XLA Modules:
  0.0 42.8 jit_solution(4363543269932933240)
XLA Ops:
  0.0 0.9 %copy.13 = f32[32,8,128]{2,0,1:T(8,128)S(1)} copy(f32[32,8,128]{2,1,0:T(8,128)} %bitcast.17) | data formatting | bytes 262144 | tf_op jit(solution)/shard_map/reshape | solution.py:377
  0.9 14.4 %all_to_all.15 = f32[8,32,128]{2,1,0:T(8,128)S(1)} all-to-all(f32[8,32,128]{2,1,0:T(8,128)S(1)} %bitcast.16), channel_id=1, replica_groups=mesh['bins'=8,'scans'=4] {'bins'}, dimensions={0} | all-to-all | bytes 262144 | tf_op jit(solution)/shard_map/all_to_all | solution.py:365
  15.4 0.0 copy-start
  15.4 1.2 %copy-done = bf16[512,1024]{1,0:T(8,128)(2,1)S(1)} copy-done((bf16[512,1024]{1,0:T(8,128)(2,1)S(1)}, bf16[512,1024]{1,0:T(8,128)(2,1)}, u32[]{:S(2)}) %copy-start) | copy-done | bytes 1048600
  16.6 0.4 coarse_dft.1
  17.0 0.0 copy-start.3
  17.0 0.0 copy-start.5
  17.0 0.0 copy-start.6
  17.0 12.8 %all_to_all.16.x_ref = f32[32,16,128]{2,1,0:T(8,128)S(1)} all-to-all(f32[32,16,128]{2,1,0:T(8,128)S(1)} %coarse_dft.1), channel_id=1, replica_groups=mesh['bins'=8,'scans'=4] {'bins','scans'}, dimensions={0} | all-to-all | bytes 524288 | tf_op jit(solution)/shard_map/all_to_all | solution.py:365
  29.8 0.0 copy-done.3
  29.8 0.0 copy-done.5
  29.8 0.0 copy-done.6
  29.8 0.0 copy-start.2
  29.8 0.0 copy-start.1
  29.8 1.8 %fine_dft.1 = f32[8,16,128]{2,1,0:T(8,128)} custom-call(s32[8]{0:T(128)S(1)} %copy-done.6, f32[32,16,128]{2,1,0:T(8,128)S(1)} %all_to_all.16.x_ref, f32[2,8,128]{2,1,0:T(8,128)S(1)} %copy-done.5, bf16[256,256]{1,0:T(8,128)(2,1)S(1)} %copy-done.3), custom_call_target="tpu_custom_call" | custom-call | tf_op jit(solution)/shard_map/fine_dft/pallas_call | solution.py:216
  31.6 0.0 copy-start.4
  31.6 2.7 %all-to-all-start.2 = ((f32[32,4,128]{2,1,0:T(4,128)}), f32[32,4,128]{2,1,0:T(4,128)S(1)}, u32[]{:S(2)}, u32[]{:S(2)}) async-start(f32[32,4,128]{2,1,0:T(4,128)} %bitcast.3), calls=%async_computation.2 | async-start | bytes 131072 | tf_op jit(solution)/shard_map/all_to_all | solution.py:365
  34.3 0.0 copy-start.7
  34.3 0.0 copy-done.2
  34.3 0.0 copy-done.4
  34.3 0.6 %copy-done.7 = s32[6]{0:T(128)S(1)} copy-done((s32[6]{0:T(128)S(1)}, s32[6]{0:T(128)}, u32[]{:S(2)}) %copy-start.7) | copy-done | bytes 48
  35.0 1.0 %state_step.1 = (f32[128,64]{1,0:T(8,128)S(1)}, s32[128,128]{1,0:T(8,128)S(1)}) custom-call(s32[6]{0:T(128)S(1)} %copy-done.7, s32[8]{0:T(128)S(1)} %copy-done.6, f32[320,64]{1,0:T(8,128)S(1)} %bitcast.14, f32[64,128]{1,0:T(8,128)S(1)} %bitcast.15), custom_call_target="tpu_custom_call" | custom-call | flops 33554432 | bytes 524288 | tf_op jit(solution)/shard_map/state_step/pallas_call | solution.py:338
  36.0 5.7 %all-to-all-done.2 = f32[32,4,128]{2,1,0:T(4,128)S(1)} async-done(((f32[32,4,128]{2,1,0:T(4,128)}), f32[32,4,128]{2,1,0:T(4,128)S(1)}, u32[]{:S(2)}, u32[]{:S(2)}) %all-to-all-start.2) | async-done | bytes 65568 | tf_op jit(solution)/shard_map/all_to_all | solution.py:365
  41.7 0.0 copy-done.1
  41.7 1.0 %state_update.1 = f32[64,128]{1,0:T(8,128)} custom-call(f32[128,128]{1,0:T(8,128)S(1)} %bitcast.13, bf16[384,384]{1,0:T(8,128)(2,1)S(1)} %copy-done.1, f32[128,64]{1,0:T(8,128)S(1)} %get-tuple-element.7.moved_ref, s32[128,128]{1,0:T(8,128)S(1)} %get-tuple-element.8.band_ref), custom_call_target="tpu_custom_call" | custom-call | tf_op jit(solution)/shard_map/state_update/pallas_call | solution.py:354
Async XLA Ops:
  15.4 1.2 %copy-start = (bf16[512,1024]{1,0:T(8,128)(2,1)S(1)}, bf16[512,1024]{1,0:T(8,128)(2,1)}, u32[]{:S(2)}) copy-start(bf16[512,1024]{1,0:T(8,128)(2,1)} %constant.8.clone.table_ref) | copy-start | bytes 3145732
  17.0 12.8 %copy-start.3 = (bf16[256,256]{1,0:T(8,128)(2,1)S(1)}, bf16[256,256]{1,0:T(8,128)(2,1)}, u32[]{:S(2)}) copy-start(bf16[256,256]{1,0:T(8,128)(2,1)} %constant.10.clone.matrix_ref) | copy-start | bytes 393220
  17.0 12.8 %copy-start.5 = (f32[2,8,128]{2,1,0:T(8,128)S(1)}, f32[2,8,128]{2,1,0:T(8,128)}, u32[]{:S(2)}) copy-start(f32[2,8,128]{2,1,0:T(8,128)} %constant.9.clone.turn_ref) | copy-start | bytes 24580
  17.0 12.8 %copy-start.6 = (s32[8]{0:T(128)S(1)}, s32[8]{0:T(128)}, u32[]{:S(2)}) copy-start(s32[8]{0:T(128)} %counts_ref.3) | copy-start | bytes 100
  29.8 4.5 %copy-start.2 = (f32[5,64,64]{2,1,0:T(8,128)S(1)}, f32[5,64,64]{2,1,0:T(8,128)}, u32[]{:S(2)}) copy-start(f32[5,64,64]{2,1,0:T(8,128)} %param.12) | copy-start | bytes 245764
  29.8 11.9 %copy-start.1 = (bf16[384,384]{1,0:T(8,128)(2,1)S(1)}, bf16[384,384]{1,0:T(8,128)(2,1)}, u32[]{:S(2)}) copy-start(bf16[384,384]{1,0:T(8,128)(2,1)} %constant.11.clone.pool_ref) | copy-start | bytes 884740
  31.6 2.7 %copy-start.4 = (f32[64,1,128]{2,1,0:T(1,128)S(1)}, f32[64,1,128]{2,1,0:T(1,128)}, u32[]{:S(2)}) copy-start(f32[64,1,128]{2,1,0:T(1,128)} %param.13) | copy-start | bytes 98308
  31.6 10.1 %all-to-all-start.2 = ((f32[32,4,128]{2,1,0:T(4,128)}), f32[32,4,128]{2,1,0:T(4,128)S(1)}, u32[]{:S(2)}, u32[]{:S(2)}) async-start(f32[32,4,128]{2,1,0:T(4,128)} %bitcast.3), calls=%async_computation.2 | async-start | bytes 131072 | tf_op jit(solution)/shard_map/all_to_all | solution.py:365
  34.3 0.7 %copy-start.7 = (s32[6]{0:T(128)S(1)}, s32[6]{0:T(128)}, u32[]{:S(2)}) copy-start(s32[6]{0:T(128)} %edges_ref.1) | copy-start | bytes 76

commit v3 on v2

v3 whole, which is shorter than its diff:
```python
import functools
import math

import jax
import jax.numpy as jnp
import numpy as np
from jax import lax
from jax.experimental import pallas as pl
from jax.experimental.pallas import tpu as pltpu
from jax.sharding import PartitionSpec as P

TILE = 512
STATES = 64
NCLASS = 5
LANES = 128

EPSILON = 1e-05
HIGHEST = lax.Precision.HIGHEST
BF16 = jnp.bfloat16
F32 = jnp.float32


def unit_root(order, exponents):
    angles = 2.0 * np.pi * (np.asarray(exponents, dtype=np.int64) % order) / order
    return np.cos(angles), -np.sin(angles)


def two_terms(values):
    high = np.asarray(values, np.float32).astype(BF16)
    low = (np.asarray(values, np.float64) - high.astype(np.float64)).astype(BF16)
    return high, low


def split_two(values):
    high = values.astype(BF16)
    return high, (values - high.astype(F32)).astype(BF16)


def dot(left, right):
    return jnp.dot(left, right, preferred_element_type=F32)


VMEM = pl.BlockSpec(memory_space=pltpu.VMEM)
SMEM = pl.BlockSpec(memory_space=pltpu.SMEM)


KINDS = 8


def doubled(values):
    return jnp.concatenate([values, values], axis=0)


def coarse_table(coarse, shares):
    half = coarse // 2
    real, imag = unit_root(coarse, np.arange(half)[:, None] * np.arange(coarse)[None, :])
    imag[0] = 1 - 2 * (np.arange(coarse) % 2)
    rows = half // shares
    parts = [part.reshape(shares, 1, rows, coarse) for part in (real, imag)]
    return np.concatenate(two_terms(np.concatenate(parts, axis=1).reshape(coarse, coarse)), axis=1)


def coarse_kernel(x_ref, table_ref, out_ref):
    coarse = x_ref.shape[0]
    high, low = split_two(x_ref[...])
    both = dot(table_ref[:, :coarse], jnp.concatenate([high, low], axis=1))
    out_ref[...] = both[:, :LANES] + both[:, LANES:] + dot(table_ref[:, coarse:], high)


def coarse_step(columns, shares):
    coarse = columns.shape[0]
    out = pl.pallas_call(
        coarse_kernel,
        out_shape=jax.ShapeDtypeStruct(columns.shape, F32),
        in_specs=[VMEM] * 2,
        out_specs=VMEM,
        compiler_params=pltpu.CompilerParams(vmem_limit_bytes=32 << 20),
        name="coarse_dft",
    )(columns, jnp.asarray(coarse_table(coarse, shares)))
    return out.reshape(shares, coarse // shares, LANES)


def fine_tables(groups, profiles, coarse):
    total = coarse * groups * LANES
    turn = unit_root(groups * LANES, np.arange(groups)[:, None] * np.arange(LANES)[None, :])
    extra = unit_root(total, np.arange(groups * LANES) * (coarse // 2))
    extra = [np.repeat(part.reshape(groups, 1, LANES), profiles, axis=1) for part in extra]
    lanes = np.arange(LANES)
    order = np.where(lanes < LANES // 2, lanes, LANES - 1 - (lanes - LANES // 2))
    high, low = two_terms(np.concatenate(unit_root(LANES, lanes[:, None] * order[None, :]), axis=1))
    turns = np.concatenate([np.concatenate(turn), np.concatenate(extra, axis=1).reshape(-1, LANES)])
    return turns.astype(np.float32), np.concatenate([high, low], axis=1)


def sum_table(profiles):
    table = np.zeros((2, 2, profiles, KINDS, 96), np.float32)
    for part in range(2):
        for p in range(profiles):
            for h in range(2):
                first = (h * profiles + p) * 8 + part * 4
                sign = 1 - 2 * part
                table[0, part, p, h, first : first + 4] = 1
                table[1, part, p, 2 + h, first + 1 : first + 4] = sign
                table[1, part, p, 4 + h, first] = sign
                table[0, part, p, 4 + h, 16 * profiles + h * 8 + part * 4 + p] = 1
            table[:, part, p, 6, 80:88] = 1
    return np.tile(table.reshape(-1, 96), (1, 2)).astype(BF16)


def unit_turn(phase, order):
    shifted = phase + order // 8
    quadrant = (shifted >> (order.bit_length() - 3)) & 3
    x = ((shifted & (order // 4 - 1)) - order // 8).astype(F32) * (2.0 * math.pi / order)
    y = x * x
    cosine = 1.0 + y * (-1 / 2 + y * (1 / 24 + y * (-1 / 720 + y * (1 / 40320))))
    sine = x * (1.0 + y * (-1 / 6 + y * (1 / 120 + y * (-1 / 5040 + y * (1 / 362880)))))
    odd = (quadrant & 1) == 1
    real, imag = jnp.where(odd, sine, cosine), jnp.where(odd, cosine, sine)
    real = jnp.where((quadrant == 1) | (quadrant == 2), -real, real)
    return real, jnp.where(quadrant >= 2, -imag, imag)


def eight_point(values, down):
    half = math.sqrt(0.5)

    def four(a, b, c, d):
        s0, s1, s2, s3 = a + c, a - c, b + d, down(b - d)
        return s0 + s2, s1 + s3, s0 - s2, s1 - s3

    even = four(values[0], values[2], values[4], values[6])
    odd = four(values[1], values[3], values[5], values[7])
    turned = [
        odd[0],
        (odd[1] + down(odd[1])) * half,
        down(odd[2]),
        (down(odd[3]) - odd[3]) * half,
    ]
    return [e + t for e, t in zip(even, turned)] + [e - t for e, t in zip(even, turned)]


def fine_kernel(
    profiles,
    order,
    edges_ref,
    counts_ref,
    x_ref,
    turns_ref,
    matrix_ref,
    sums_ref,
    dynamics_ref,
    state_ref,
    out_ref,
    moved_ref,
    band_ref,
):
    groups = counts_ref.shape[0]
    capacity = state_ref.shape[0]
    own = lax.axis_index("bins") * profiles + lax.axis_index("scans")
    row = lax.broadcasted_iota(jnp.int32, (8, LANES), 0)
    lane = lax.broadcasted_iota(jnp.int32, (8, LANES), 1)
    low_side = lane < LANES // 2
    first = own == 0
    side = jnp.where(row < 4, -1.0, 1.0)

    def swapped(values):
        return pltpu.roll(values, 4, 0)

    def down(values):
        return swapped(values) * -side

    columns = [[] for _ in range(profiles + 1)]
    for c in range(groups):
        cosine, sine = unit_turn(((c * LANES + lane) * (4 * own + (row & 3))) & (order - 1), order)
        sine = sine * -side
        real_only = []
        for p in range(profiles):
            block = x_ref[c * profiles + p]
            real_only.append(block[4:5])
            block = jnp.where(first & (row == 4), 0.0, block)
            columns[p].append(block * cosine + swapped(block) * sine)
        block = doubled(jnp.concatenate(real_only, axis=0))
        turn = turns_ref[2 * groups + 8 * c : 2 * groups + 8 * (c + 1), :]
        columns[profiles].append(jnp.where(first, block * turn, 0.0))
    transformed = [eight_point(column, down) for column in columns]
    blocks = []
    for u in range(groups):
        cosine, sine = turns_ref[u : u + 1, :], turns_ref[groups + u : groups + u + 1, :] * side
        for column in transformed:
            block = column[u]
            blocks.append(block * cosine + swapped(block) * sine if u else block)
    high, low = split_two(jnp.concatenate(blocks, axis=0))
    wide = 2 * LANES
    product = dot(high, matrix_ref[...])
    product = product[:, :wide] + product[:, wide:] + dot(low, matrix_ref[:, :wide])
    spectrum = []
    for at in range(len(blocks)):
        piece = product[8 * at : 8 * (at + 1)]
        block = piece[:, :LANES] + swapped(piece[:, LANES:]) * side
        if at % (profiles + 1) < profiles:
            block = jnp.where(first & ~low_side & ((row & 3) == 0), 0.0, block)
        else:
            block = jnp.where(low_side, block, 0.0)
        spectrum.append(block)
    spectrum = [
        spectrum[u * (profiles + 1) : (u + 1) * (profiles + 1)] for u in range(groups)
    ]
    pairs = groups // 2
    power = [
        sum(block * block for block in spectrum[2 * q] + spectrum[2 * q + 1]) for q in range(pairs)
    ]
    summands = []
    for q in range(pairs):
        rows = []
        for h in range(2):
            for p in range(profiles):
                high_block = spectrum[groups - 1 - 2 * q - h][p]
                rows.append(jnp.where(low_side, spectrum[2 * q + h][p], high_block))
        rows += [spectrum[2 * q + h][profiles] for h in range(2)]
        rows.append(jnp.where(low_side, power[q], power[pairs - 1 - q]))
        rows.append(jnp.zeros((8, LANES), F32))
        summands.append(jnp.concatenate(rows, axis=0))
    summed = dot(
        sums_ref[...],
        jnp.concatenate(split_two(jnp.concatenate(summands, axis=1)), axis=0),
    )
    rows, half = summed.shape[0] // 2, LANES // 2
    left = jnp.concatenate(
        [
            summed[:rows, q * LANES : q * LANES + half]
            + summed[rows:, q * LANES + half : (q + 1) * LANES]
            for q in range(pairs)
        ],
        axis=1,
    )
    owner_of = lax.broadcasted_iota(jnp.int32, (1, groups * capacity), 1)
    rank_of, owner_of = owner_of & (capacity - 1), owner_of >> (capacity.bit_length() - 1)
    wanted = jnp.full((1, groups * capacity), -1, jnp.int32)
    start = jnp.int32(0)
    for owner in range(groups):
        count = counts_ref[owner]
        wanted = jnp.where((owner_of == owner) & (rank_of < count), start + rank_of, wanted)
        start = start + count
    tile_of = lax.broadcasted_iota(jnp.int32, (pairs * half, groups * capacity), 0)
    tile_of = (tile_of >> (half.bit_length() - 1)) + pairs * (tile_of & (half - 1))
    chosen = jnp.where(tile_of == wanted, 1.0, 0.0).astype(BF16)
    routed = dot(jnp.concatenate(split_two(left), axis=0), chosen)
    routed = routed[:rows] + routed[rows:]
    for owner in range(groups):
        piece = routed[:, owner * capacity : (owner + 1) * capacity]
        out_ref[owner] = jnp.concatenate([piece[: rows // 2], piece[rows // 2 :]], axis=1)
    state_kernel(edges_ref, counts_ref, dynamics_ref, state_ref, moved_ref, band_ref)


def fine_step(arrived, band_edges, owner_counts, dynamics, state, profiles, coarse):
    groups, capacity = owner_counts.shape[0], state.shape[0]
    turns, matrix = fine_tables(groups, profiles, coarse)
    out, moved, band = pl.pallas_call(
        functools.partial(fine_kernel, profiles, coarse * groups * LANES),
        out_shape=(
            jax.ShapeDtypeStruct((groups, profiles * KINDS, LANES), F32),
            jax.ShapeDtypeStruct((2 * capacity, STATES), F32),
            jax.ShapeDtypeStruct((2 * capacity, LANES), jnp.int32),
        ),
        in_specs=[SMEM] * 2 + [VMEM] * 6,
        out_specs=(VMEM,) * 3,
        compiler_params=pltpu.CompilerParams(vmem_limit_bytes=32 << 20),
        name="fine_dft",
    )(
        band_edges,
        owner_counts,
        arrived,
        jnp.asarray(turns),
        jnp.asarray(matrix),
        jnp.asarray(sum_table(profiles)),
        dynamics.reshape(NCLASS * STATES, STATES),
        state,
    )
    return out.reshape(groups * profiles, KINDS, LANES), moved, band


def fine_step_general(arrived, owner_counts, capacity):
    groups, rows = arrived.shape[0], arrived.shape[1] // 2
    coarse = 2 * rows * groups
    fine_length = groups * LANES
    own = lax.axis_index("bins")
    real, imag = arrived[:, :rows], arrived[:, rows:]
    points = jnp.arange(fine_length, dtype=jnp.int32).reshape(groups, 1, LANES)
    k_index = own * rows + jnp.arange(rows, dtype=jnp.int32)[None, :, None]
    cosine, sine = unit_turn(points * k_index & (coarse * fine_length - 1), coarse * fine_length)
    packed = (own == 0) & (jnp.arange(rows)[None, :, None] == 0)
    middle = jnp.where(own == 0, imag[:, :1], 0.0)
    imag = jnp.where(packed, 0.0, imag)
    real, imag = real * cosine + imag * sine, imag * cosine - real * sine
    cosine, sine = unit_turn(points * (coarse // 2), coarse * fine_length)
    real = jnp.concatenate([real, middle * cosine], axis=1)
    imag = jnp.concatenate([imag, -middle * sine], axis=1)

    def turned(pattern, root, parts):
        cosine, sine = (jnp.asarray(part.astype(np.float32)) for part in root)
        mul = functools.partial(jnp.einsum, pattern, precision=HIGHEST)
        return (
            mul(cosine, parts[0]) - mul(sine, parts[1]),
            mul(cosine, parts[1]) + mul(sine, parts[0]),
        )

    group_index, lane_index = np.arange(groups), np.arange(LANES)
    parts = turned(
        "cu,crj->urj", unit_root(groups, group_index[:, None] * group_index), (real, imag)
    )
    parts = turned(
        "uj,urj->urj", unit_root(fine_length, group_index[:, None] * lane_index), parts
    )
    real, imag = (
        part.reshape(fine_length, rows + 1)
        for part in turned(
            "jv,urj->vur", unit_root(LANES, lane_index[:, None] * lane_index), parts
        )
    )
    half, tiles = fine_length // 2, fine_length // 4
    kept = jnp.concatenate([~packed[0, :, 0], jnp.zeros((1,), bool)])

    def sides(part, sign):
        low = part[:half].reshape(tiles, 2, rows + 1)
        high = sign * jnp.where(kept, part[half:][::-1], 0.0).reshape(tiles, 2, rows + 1)
        return low, high

    low_real, high_real = sides(real, 1.0)
    low_imag, high_imag = sides(imag, -1.0)
    power = sum(
        jnp.sum(part * part, axis=(1, 2)) for part in (low_real, high_real, low_imag, high_imag)
    )
    starts = jnp.cumsum(owner_counts) - owner_counts
    slot_index = jnp.arange(capacity, dtype=jnp.int32)
    filled = slot_index[None, :] < owner_counts[:, None]
    chosen = jnp.clip(starts[:, None] + slot_index[None, :], 0, tiles - 1)

    def kinds(low, high):
        low_sums = jnp.sum(low[:, :, :rows], axis=2)
        high_sums = jnp.sum(high[:, :, 1:rows], axis=2)
        rest = high[:, :, 0] + low[:, :, rows]
        last = jnp.stack([power, jnp.zeros_like(power)], axis=1)
        values = jnp.concatenate([low_sums, high_sums, rest, last], axis=1)
        return jnp.where(filled[:, :, None], values[chosen], 0.0).transpose(0, 2, 1)

    return jnp.concatenate([kinds(low_real, high_real), kinds(low_imag, high_imag)], axis=2)


def pool_table(shares, coarse):
    pool = np.zeros((shares, KINDS, 6, STATES), np.float32)
    wide = TILE // STATES
    rows = coarse // 2 // shares
    for share in range(shares):
        first = rows * share
        rest = coarse - first if share else coarse // 2
        for kind, at in ((0, first), (2, coarse - first - 1), (4, rest)):
            for h in range(2):
                for band in range(NCLASS):
                    pool[share, kind + h, band, (at + coarse * h) // wide >> band] = 1.0
        pool[share, 6, NCLASS, :] = 1.0
    return pool.reshape(shares * KINDS, 6 * STATES).astype(BF16)


def state_kernel(edges_ref, counts_ref, dynamics_ref, state_ref, moved_ref, band_ref):
    own = lax.axis_index("bins")
    groups = counts_ref.shape[0]
    capacity = state_ref.shape[0]
    wide = NCLASS * STATES

    def before(owner, start):
        return start + jnp.where(owner < own, counts_ref[owner], 0)

    start = lax.fori_loop(0, groups, before, jnp.int32(0))
    slot = lax.broadcasted_iota(jnp.int32, (2 * capacity, LANES), 0) & (capacity - 1)
    band = jnp.zeros_like(slot)
    for edge in range(1, NCLASS):
        band = band + jnp.where(slot + start >= edges_ref[edge], 1, 0)
    band = jnp.where(slot < counts_ref[own], band, -1)
    band_ref[...] = band
    state = state_ref[...]
    state = jnp.concatenate([state[:, :STATES], state[:, STATES:]], axis=0)
    row = lax.broadcasted_iota(jnp.int32, (wide, STATES), 0)
    column = lax.broadcasted_iota(jnp.int32, (wide, STATES), 1)
    limit = STATES >> (row >> 6)
    inside = ((row & (STATES - 1)) < limit) & (column < limit)
    dynamics = jnp.where(inside, dynamics_ref[...], 0.0)
    moved = lax.dot_general(
        state, dynamics, (((1,), (1,)), ((), ())), precision=HIGHEST, preferred_element_type=F32
    )
    moved = jnp.concatenate([moved, jnp.zeros((2 * capacity, STATES), F32)], axis=1)
    moved_ref[...] = of_band(moved, band)


def of_band(values, band):
    lane = lax.broadcasted_iota(jnp.int32, band.shape, 1) >> 6
    folded = jnp.zeros(band.shape, F32)
    for pair in range((NCLASS + 1) // 2):
        piece = values[:, pair * LANES : (pair + 1) * LANES]
        folded = folded + jnp.where(lane + 2 * pair == band, piece, 0.0)
    return folded[:, :STATES] + folded[:, STATES:]


def update_kernel(count, x_ref, pool_ref, moved_ref, band_ref, out_ref):
    capacity = out_ref.shape[0]
    band = band_ref[...]
    sums = lax.dot_general(
        jnp.concatenate(split_two(x_ref[...]), axis=1),
        pool_ref[...],
        (((0,), (0,)), ((), ())),
        preferred_element_type=F32,
    )
    sums = sums[: 2 * capacity] + sums[2 * capacity :]
    power = sums[:, NCLASS * STATES :] * (1.0 / count)
    span = jnp.left_shift(TILE // STATES, jnp.maximum(band[:, :STATES], 0)).astype(F32)
    scaling = 1.0 / jnp.sqrt(span * (power + EPSILON))
    result = moved_ref[...] + of_band(sums, band) * scaling
    out_ref[...] = jnp.concatenate([result[:capacity], result[capacity:]], axis=1)


def state_step(band_edges, owner_counts, dynamics, state):
    rows = 2 * state.shape[0]
    return pl.pallas_call(
        state_kernel,
        out_shape=(
            jax.ShapeDtypeStruct((rows, STATES), F32),
            jax.ShapeDtypeStruct((rows, LANES), jnp.int32),
        ),
        in_specs=[SMEM, SMEM, VMEM, VMEM],
        out_specs=(VMEM, VMEM),
        compiler_params=pltpu.CompilerParams(vmem_limit_bytes=32 << 20),
        cost_estimate=pl.CostEstimate(flops=1 << 25, bytes_accessed=1 << 19, transcendentals=0),
        name="state_step",
    )(band_edges, owner_counts, dynamics.reshape(NCLASS * STATES, STATES), state)


def update_step(arrived, moved, band, coarse, count):
    shares = arrived.shape[0]
    return pl.pallas_call(
        functools.partial(update_kernel, count),
        out_shape=jax.ShapeDtypeStruct((moved.shape[0] // 2, 2 * STATES), F32),
        in_specs=[VMEM] * 4,
        out_specs=VMEM,
        compiler_params=pltpu.CompilerParams(vmem_limit_bytes=32 << 20),
        name="state_update",
    )(arrived.reshape(shares * KINDS, LANES), jnp.asarray(pool_table(shares, coarse)), moved, band)


def exchanged(values, axes):
    return lax.all_to_all(values, axes, split_axis=0, concat_axis=0, tiled=True)


def body(profiles, band_edges, owner_counts, dynamics, prev_state):
    groups, scans = lax.axis_size("bins"), lax.axis_size("scans")
    prof_rows, length = profiles.shape
    capacity = prev_state.shape[0]
    coarse = length // LANES
    shares = groups * scans
    count = prof_rows * scans * TILE
    state = prev_state.reshape(capacity, 2 * STATES)
    columns = profiles.reshape(coarse // groups, groups, LANES).transpose(1, 0, 2)
    columns = exchanged(columns, "bins").reshape(coarse, LANES)
    if groups == 8 and scans == 4 and coarse == 8 * shares:
        blocks = exchanged(coarse_step(columns, shares), ("bins", "scans"))
        payload, moved, band = fine_step(
            blocks, band_edges, owner_counts, dynamics, state, scans, coarse
        )
        arrived = exchanged(payload, ("bins", "scans"))
    else:
        moved, band = state_step(band_edges, owner_counts, dynamics, state)
        blocks = exchanged(coarse_step(columns, groups), "bins")
        arrived = exchanged(fine_step_general(blocks, owner_counts, capacity), "bins")
        power = lax.psum(arrived[:, 6:7], "scans")
        arrived = jnp.concatenate([arrived[:, :6], power, arrived[:, 7:]], axis=1)
    updated = update_step(arrived, moved, band, coarse, count)
    return updated.reshape(prev_state.shape)


def solution(mesh):
    return jax.shard_map(
        body,
        mesh=mesh,
        in_specs=(P("scans", "bins"), P(), P(), P(), P("bins", "scans", None)),
        out_specs=P("bins", "scans", None),
        check_vma=False,
    )
```

time: 43.1 us -> 40.2 us (0.933)
  blocking collectives: 27.2 us -> 34.9 us
  waiting for transfers between devices: 5.71 us -> 0 us
  starting transfers between devices: 2.68 us -> 0 us
  local copies, waits for them, and re-layouts: 2.82 us -> 1.64 us
  Pallas kernels: 4.23 us -> 3.36 us
    all_to_all x2 -> x3, blocking collectives: 27.2 us -> 34.9 us  [exchanged(): return lax.all_to_all(values, axes, split_axis=0, concat_axis=0, tiled=True)]
    all_to_all x1 -> x0, waiting for transfers between devices: 5.71 us -> none  [exchanged(): return lax.all_to_all(values, axes, split_axis=0, concat_axis=0, tiled=True)]
    all_to_all x1 -> x0, starting transfers between devices: 2.68 us -> none  [exchanged(): return lax.all_to_all(values, axes, split_axis=0, concat_axis=0, tiled=True)]
    unnamed x16 -> x18, local copies, waits for them, and re-layouts: 1.89 us -> 0.67 us
    pallas_call x3 -> x2, Pallas kernels: 3.19 us -> 2.34 us  [the longest x1 2.11 us: fine_step(): pl.pallas_call(functools.partial(fine_kernel, profiles, coarse * groups *...]
  transfers between devices with their start and end apart: 1 -> 0, of which waited for: 1 -> 0; matrix products, arithmetic and copies ran while one was open for 0% -> 0% of each run, Pallas kernels for 2% -> 0%
where the time goes in v3:
time: 40.2 us; the launch traced here: 40 us
  blocking collectives  34.9 us (87%)
  Pallas kernels  3.36 us (8%)
  local copies, waits for them, and re-layouts  1.64 us (4%)
    all_to_all x3, blocking collectives, exchanged(): return lax.all_to_all(values, axes, split_axis=0, concat_axis=0, tiled=True)  34.9 us
    pallas_call x1, Pallas kernels, fine_step(): pl.pallas_call(functools.partial(fine_kernel, profiles, coarse * groups *...  2.11 us
    pallas_call x1, Pallas kernels, update_step(): pl.pallas_call(functools.partial(update_kernel, count), out_shape=jax.Sha...  1.02 us
    reshape x1, local copies, waits for them, and re-layouts, body(): profiles.reshape(coarse // groups, groups, LANES).transpose(1, 0, 2)  0.97 us

profile of v3, /device:TPU:0, one launch (start us, length us, event | category | flops | bytes accessed | tf_op | source)
XLA Modules:
  0.0 40.0 jit_solution(6691165807151936071)
XLA Ops:
  0.0 0.0 copy-start
  0.0 1.0 %copy.14 = f32[32,8,128]{2,0,1:T(8,128)S(1)} copy(f32[32,8,128]{2,1,0:T(8,128)} %bitcast.20) | data formatting | bytes 262144 | tf_op jit(solution)/shard_map/reshape | solution.py:459
  1.0 14.4 %all_to_all.15 = f32[8,32,128]{2,1,0:T(8,128)S(1)} all-to-all(f32[8,32,128]{2,1,0:T(8,128)S(1)} %bitcast.19), channel_id=1, replica_groups=mesh['bins'=8,'scans'=4] {'bins'}, dimensions={0} | all-to-all | bytes 262144 | tf_op jit(solution)/shard_map/all_to_all | solution.py:448
  15.4 0.0 copy-done
  15.4 0.0 copy-start.3
  15.4 0.0 copy-start.5
  15.4 0.2 coarse_dft.1
  15.6 0.0 copy-start.2
  15.7 0.0 copy-start.4
  15.7 0.0 copy-start.6
  15.7 10.4 %all_to_all.16.x_ref = f32[32,8,128]{2,1,0:T(8,128)S(1)} all-to-all(f32[32,8,128]{2,1,0:T(8,128)S(1)} %bitcast.15), channel_id=1, replica_groups=mesh['bins'=8,'scans'=4] {'bins','scans'}, dimensions={0} | all-to-all | bytes 262144 | tf_op jit(solution)/shard_map/all_to_all | solution.py:448
  26.1 0.0 copy-start.7
  26.1 0.0 copy-start.8
  26.1 0.0 copy-done.3
  26.1 0.0 copy-done.5
  26.1 0.0 copy-done.2
  26.1 0.0 copy-done.4
  26.1 0.0 copy-done.6
  26.1 0.6 %copy-done.7 = s32[6]{0:T(128)S(1)} copy-done((s32[6]{0:T(128)S(1)}, s32[6]{0:T(128)}, u32[]{:S(2)}) %copy-start.7) | copy-done | bytes 48
  26.7 0.0 copy-done.8
  26.8 2.1 %fine_dft.1 = (f32[8,32,128]{2,1,0:T(8,128)S(1)}, f32[128,64]{1,0:T(8,128)S(1)}, s32[128,128]{1,0:T(8,128)S(1)}) custom-call(s32[6]{0:T(128)S(1)} %copy-done.7, s32[8]{0:T(128)S(1)} %copy-done.8, f32[32,8,128]{2,1,0:T(8,128)S(1)} %all_to_all.16.x_ref, f32[80,128]{1,0:T(8,128)S(1)} %copy-done.5, bf16[128,512]{1,0:T(8,128)(2,1)S(1)} %copy-done.3, ...), custom_call_target="tpu_custom_call" | custom-call | tf_op jit(solution)/shard_map/fine_dft/pallas_call | solution.py:257
  28.9 0.0 copy-start.1
  28.9 10.1 %all_to_all.17 = f32[32,8,128]{2,1,0:T(8,128)S(1)} all-to-all(f32[32,8,128]{2,1,0:T(8,128)S(1)} %bitcast.17), channel_id=1, replica_groups=mesh['bins'=8,'scans'=4] {'bins','scans'}, dimensions={0} | all-to-all | bytes 262144 | tf_op jit(solution)/shard_map/all_to_all | solution.py:448
  38.9 0.0 copy-done.1
  39.0 1.0 %state_update.1 = f32[64,128]{1,0:T(8,128)} custom-call(f32[256,128]{1,0:T(8,128)S(1)} %bitcast.13, bf16[256,384]{1,0:T(8,128)(2,1)S(1)} %copy-done.1, f32[128,64]{1,0:T(8,128)S(1)} %get-tuple-element.9.moved_ref, s32[128,128]{1,0:T(8,128)S(1)} %get-tuple-element.10.band_ref), custom_call_target="tpu_custom_call" | custom-call | tf_op jit(solution)/shard_map/state_update/pallas_call | solution.py:437
Async XLA Ops:
  0.0 15.4 %copy-start = (bf16[256,512]{1,0:T(8,128)(2,1)S(1)}, bf16[256,512]{1,0:T(8,128)(2,1)}, u32[]{:S(2)}) copy-start(bf16[256,512]{1,0:T(8,128)(2,1)} %constant.10.clone.table_ref) | copy-start | bytes 786436
  15.4 10.7 %copy-start.3 = (bf16[128,512]{1,0:T(8,128)(2,1)S(1)}, bf16[128,512]{1,0:T(8,128)(2,1)}, u32[]{:S(2)}) copy-start(bf16[128,512]{1,0:T(8,128)(2,1)} %constant.12.clone.matrix_ref) | copy-start | bytes 393220
  15.4 10.7 %copy-start.5 = (f32[80,128]{1,0:T(8,128)S(1)}, f32[80,128]{1,0:T(8,128)}, u32[]{:S(2)}) copy-start(f32[80,128]{1,0:T(8,128)} %constant.11.clone.turns_ref) | copy-start | bytes 122884
  15.6 10.5 %copy-start.2 = (f32[5,64,64]{2,1,0:T(8,128)S(1)}, f32[5,64,64]{2,1,0:T(8,128)}, u32[]{:S(2)}) copy-start(f32[5,64,64]{2,1,0:T(8,128)} %param.13) | copy-start | bytes 245764
  15.7 10.5 %copy-start.4 = (bf16[128,192]{1,0:T(8,128)(2,1)S(1)}, bf16[128,192]{1,0:T(8,128)(2,1)}, u32[]{:S(2)}) copy-start(bf16[128,192]{1,0:T(8,128)(2,1)} %constant.13.clone.sums_ref) | copy-start | bytes 147460
  15.7 10.5 %copy-start.6 = (f32[64,1,128]{2,1,0:T(1,128)S(1)}, f32[64,1,128]{2,1,0:T(1,128)}, u32[]{:S(2)}) copy-start(f32[64,1,128]{2,1,0:T(1,128)} %param.14) | copy-start | bytes 98308
  26.1 0.7 %copy-start.7 = (s32[6]{0:T(128)S(1)}, s32[6]{0:T(128)}, u32[]{:S(2)}) copy-start(s32[6]{0:T(128)} %edges_ref.1) | copy-start | bytes 76
  26.1 0.7 %copy-start.8 = (s32[8]{0:T(128)S(1)}, s32[8]{0:T(128)}, u32[]{:S(2)}) copy-start(s32[8]{0:T(128)} %counts_ref.1) | copy-start | bytes 100
  28.9 10.1 %copy-start.1 = (bf16[256,384]{1,0:T(8,128)(2,1)S(1)}, bf16[256,384]{1,0:T(8,128)(2,1)}, u32[]{:S(2)}) copy-start(bf16[256,384]{1,0:T(8,128)(2,1)} %constant.14.clone.pool_ref) | copy-start | bytes 589828

commit v4 on v3

v4 whole, which is shorter than its diff:
```python
import functools
import math

import jax
import jax.numpy as jnp
import numpy as np
from jax import lax
from jax.experimental import pallas as pl
from jax.experimental.pallas import tpu as pltpu
from jax.sharding import PartitionSpec as P

TILE = 512
STATES = 64
NCLASS = 5
LANES = 128

EPSILON = 1e-05
HIGHEST = lax.Precision.HIGHEST
BF16 = jnp.bfloat16
F32 = jnp.float32


def unit_root(order, exponents):
    angles = 2.0 * np.pi * (np.asarray(exponents, dtype=np.int64) % order) / order
    return np.cos(angles), -np.sin(angles)


def two_terms(values):
    high = np.asarray(values, np.float32).astype(BF16)
    low = (np.asarray(values, np.float64) - high.astype(np.float64)).astype(BF16)
    return high, low


def split_two(values):
    high = values.astype(BF16)
    return high, (values - high.astype(F32)).astype(BF16)


def dot(left, right):
    return jnp.dot(left, right, preferred_element_type=F32)


VMEM = pl.BlockSpec(memory_space=pltpu.VMEM)
SMEM = pl.BlockSpec(memory_space=pltpu.SMEM)


KINDS = 4
HALF = LANES // 2


def columns_kernel(x_ref, out_ref):
    groups, rows, _ = out_ref.shape
    low_lanes = lax.broadcasted_iota(jnp.int32, (rows, LANES), 1) < HALF
    for pair in range(groups // 2):
        even = x_ref[pl.ds(pair, rows, stride=groups), :]
        odd = x_ref[pl.ds(groups // 2 + pair, rows, stride=groups), :]
        out_ref[2 * pair] = jnp.where(low_lanes, even, pltpu.roll(odd, HALF, 1))
        out_ref[2 * pair + 1] = jnp.where(low_lanes, pltpu.roll(even, HALF, 1), odd)


def columns_step(profile, groups):
    rows = profile.shape[0] // (groups * LANES)
    return pl.pallas_call(
        columns_kernel,
        out_shape=jax.ShapeDtypeStruct((groups, rows, LANES), F32),
        in_specs=[VMEM],
        out_specs=VMEM,
        compiler_params=pltpu.CompilerParams(vmem_limit_bytes=32 << 20),
        name="columns",
    )(profile.reshape(-1, LANES))


def coarse_table(coarse):
    half = coarse // 2
    real, imag = unit_root(half, np.arange(half)[:, None] * np.arange(half)[None, :])
    imag[0] = real[0]
    return np.concatenate(two_terms(np.concatenate([real, imag])), axis=1)


def coarse_kernel(x_ref, table_ref, out_ref):
    half = x_ref.shape[0]
    high, low = split_two(x_ref[...])
    both = dot(table_ref[:, :half], jnp.concatenate([high, low], axis=1))
    spectrum = both[:, :LANES] + both[:, LANES:] + dot(table_ref[:, half:], high)
    row = lax.broadcasted_iota(jnp.int32, (8, LANES), 0)
    low_lanes = lax.broadcasted_iota(jnp.int32, (8, LANES), 1) < HALF
    row_cosine, row_sine = unit_turn(row, 2 * half)
    side = jnp.where(low_lanes, 1.0, -1.0)
    for share in range(out_ref.shape[0]):
        real = spectrum[8 * share : 8 * (share + 1)]
        imag = spectrum[half + 8 * share : half + 8 * (share + 1)]
        even = jnp.where(low_lanes, real, pltpu.roll(imag, HALF, 1))
        odd = jnp.where(low_lanes, pltpu.roll(real, HALF, 1), imag)
        angle = math.pi * 8 * share / half
        cosine = row_cosine * math.cos(angle) - row_sine * math.sin(angle)
        sine = row_sine * math.cos(angle) + row_cosine * math.sin(angle)
        if share == 0:
            cosine = jnp.where((row == 0) & ~low_lanes, -1.0, cosine)
        out_ref[share] = even + odd * cosine + pltpu.roll(odd, HALF, 1) * (sine * side)


def coarse_step(columns):
    half = columns.shape[0]
    return pl.pallas_call(
        coarse_kernel,
        out_shape=jax.ShapeDtypeStruct((half // 8, 8, LANES), F32),
        in_specs=[VMEM] * 2,
        out_specs=VMEM,
        compiler_params=pltpu.CompilerParams(vmem_limit_bytes=32 << 20),
        name="coarse_dft",
    )(columns, jnp.asarray(coarse_table(2 * half)))


def coarse_step_general(columns, shares):
    coarse = columns.shape[0]
    half = coarse // 2
    real, imag = unit_root(coarse, np.arange(half)[:, None] * np.arange(coarse)[None, :])
    imag[0] = 1 - 2 * (np.arange(coarse) % 2)
    table = jnp.asarray(np.concatenate([real, imag]).astype(np.float32))
    spectrum = jnp.dot(table, columns, precision=HIGHEST)
    blocks = jnp.concatenate([spectrum[:half], spectrum[half:]], axis=1)
    return blocks.reshape(shares, half // shares, LANES)


def fine_tables(groups, profiles, coarse):
    fine_length = groups * HALF
    doubled = np.arange(LANES) % HALF
    turn = unit_root(fine_length, np.arange(groups)[:, None] * doubled[None, :])
    extra = unit_root(coarse * fine_length, np.arange(fine_length) * (coarse // 2))
    extra = np.concatenate([part.reshape(groups, HALF) for part in extra], axis=1)
    turns = np.concatenate([turn[0], turn[1], extra]).astype(np.float32)
    order = np.arange(HALF)
    order[HALF // 2 :] = order[HALF // 2 :][::-1]
    real, imag = unit_root(HALF, np.arange(HALF)[:, None] * order[None, :])
    sign = np.where(np.arange(HALF) < HALF // 2, 1, -1)
    matrix = np.block([[real, imag * sign], [-imag, real * sign]])
    sums = np.zeros((2, profiles, KINDS, 2, 6, 8), np.float32)
    for p in range(profiles):
        sums[0, p, 0, :, p, :] = 1
        sums[1, p, 1, :, p, 1:] = 1
        sums[1, p, 2, :, p, 0] = 1
        sums[0, p, 2, :, profiles, p] = 1
        sums[:, p, 3, :, profiles + 1, :] = 1
    sums = sums.reshape(2 * profiles * KINDS, -1)
    sums = np.pad(sums, [(0, 0), (0, 2 * LANES - sums.shape[1])]).astype(BF16)
    return turns, np.concatenate([np.concatenate(two_terms(matrix), axis=1), sums])


def unit_turn(phase, order):
    shifted = phase + order // 8
    quadrant = (shifted >> (order.bit_length() - 3)) & 3
    x = ((shifted & (order // 4 - 1)) - order // 8).astype(F32) * (2.0 * math.pi / order)
    y = x * x
    cosine = 1.0 + y * (-1 / 2 + y * (1 / 24 + y * (-1 / 720 + y * (1 / 40320))))
    sine = x * (1.0 + y * (-1 / 6 + y * (1 / 120 + y * (-1 / 5040 + y * (1 / 362880)))))
    odd = (quadrant & 1) == 1
    real, imag = jnp.where(odd, sine, cosine), jnp.where(odd, cosine, sine)
    real = jnp.where((quadrant == 1) | (quadrant == 2), -real, real)
    return real, jnp.where(quadrant >= 2, -imag, imag)


def eight_point(values, down):
    half = math.sqrt(0.5)

    def four(a, b, c, d):
        s0, s1, s2, s3 = a + c, a - c, b + d, down(b - d)
        return s0 + s2, s1 + s3, s0 - s2, s1 - s3

    even = four(values[0], values[2], values[4], values[6])
    odd = four(values[1], values[3], values[5], values[7])
    turned = [
        odd[0],
        (odd[1] + down(odd[1])) * half,
        down(odd[2]),
        (down(odd[3]) - odd[3]) * half,
    ]
    return [e + t for e, t in zip(even, turned)] + [e - t for e, t in zip(even, turned)]


def fine_kernel(
    profiles,
    order,
    edges_ref,
    counts_ref,
    x_ref,
    turns_ref,
    table_ref,
    dynamics_ref,
    state_ref,
    out_ref,
    moved_ref,
    band_ref,
):
    groups = counts_ref.shape[0]
    capacity = state_ref.shape[0]
    own = lax.axis_index("bins") * profiles + lax.axis_index("scans")
    row = lax.broadcasted_iota(jnp.int32, (8, LANES), 0)
    lane = lax.broadcasted_iota(jnp.int32, (8, LANES), 1)
    point = lane & (HALF - 1)
    low_side = point < HALF // 2
    first = own == 0
    side = jnp.where(lane < HALF, 1.0, -1.0)

    def swapped(values):
        return pltpu.roll(values, HALF, 1)

    def down(values):
        return swapped(values) * side

    columns = [[] for _ in range(profiles + 1)]
    for c in range(groups):
        cosine, sine = unit_turn(((c * HALF + point) * (8 * own + row)) & (order - 1), order)
        sine = sine * side
        middle = jnp.zeros((8, LANES), F32)
        for p in range(profiles):
            block = x_ref[c * profiles + p]
            middle = jnp.where(row == p, block[:1], middle)
            block = jnp.where(first & (row == 0) & (lane >= HALF), 0.0, block)
            columns[p].append(block * cosine + swapped(block) * sine)
        middle = jnp.where(lane < HALF, swapped(middle), middle)
        middle = middle * turns_ref[2 * groups + c : 2 * groups + c + 1, :]
        columns[profiles].append(jnp.where(first, middle, 0.0))
    transformed = [eight_point(column, down) for column in columns]
    blocks = []
    for u in range(groups):
        cosine, sine = turns_ref[u : u + 1, :], turns_ref[groups + u : groups + u + 1, :] * -side[:1]
        for column in transformed:
            block = column[u]
            blocks.append(block * cosine + swapped(block) * sine if u else block)
    high, low = split_two(jnp.concatenate(blocks, axis=0))
    product = dot(high, table_ref[:LANES, :])
    product = product[:, :LANES] + product[:, LANES:] + dot(low, table_ref[:LANES, :LANES])
    spectrum = []
    for at in range(len(blocks)):
        block = product[8 * at : 8 * (at + 1)]
        if at % (profiles + 1) < profiles:
            block = jnp.where(first & ~low_side & (row == 0), 0.0, block)
        else:
            block = jnp.where(low_side, block, 0.0)
        spectrum.append(block)
    spectrum = [spectrum[u * (profiles + 1) : (u + 1) * (profiles + 1)] for u in range(groups)]
    power = []
    for u in range(groups):
        squares = sum(block * block for block in spectrum[u])
        power.append(squares + swapped(squares))
    summands = []
    for u in range(groups):
        rows = [
            jnp.where(low_side, spectrum[u][p], spectrum[groups - 1 - u][p]) for p in range(profiles)
        ]
        rows.append(spectrum[u][profiles])
        rows.append(jnp.where(low_side, power[u], power[groups - 1 - u]))
        summands.append(jnp.concatenate(rows, axis=0))
    summands = jnp.concatenate(split_two(jnp.concatenate(summands, axis=1)), axis=0)
    summed = dot(table_ref[LANES:, : summands.shape[0]], summands)
    rows, quarter = summed.shape[0] // 2, HALF // 2
    lanes = lax.broadcasted_iota(jnp.int32, (rows, LANES), 1)
    left = [[], []]
    for part in range(2):
        for first_u in range(0, groups, 4):
            merged = None
            for u in range(first_u, first_u + 4):
                piece = summed[:rows, u * LANES : (u + 1) * LANES] + pltpu.roll(
                    summed[rows:, u * LANES : (u + 1) * LANES], LANES - quarter, 1
                )
                shift = ((u % 4) * quarter - part * HALF) % LANES
                piece = pltpu.roll(piece, shift, 1) if shift else piece
                here = lanes >= (u % 4) * quarter
                merged = piece if merged is None else jnp.where(here, piece, merged)
            left[part].append(merged)
    left = jnp.concatenate([jnp.concatenate(part, axis=1) for part in left], axis=0)
    owner_of = lax.broadcasted_iota(jnp.int32, (1, groups * capacity), 1)
    rank_of, owner_of = owner_of & (capacity - 1), owner_of >> (capacity.bit_length() - 1)
    wanted = jnp.full((1, groups * capacity), -1, jnp.int32)
    start = jnp.int32(0)
    for owner in range(groups):
        count = counts_ref[owner]
        wanted = jnp.where((owner_of == owner) & (rank_of < count), start + rank_of, wanted)
        start = start + count
    tile_of = lax.broadcasted_iota(jnp.int32, (groups * quarter, groups * capacity), 0)
    tile_of = (tile_of >> (quarter.bit_length() - 1)) + groups * (tile_of & (quarter - 1))
    chosen = jnp.where(tile_of == wanted, 1.0, 0.0).astype(BF16)
    routed = dot(jnp.concatenate(split_two(left), axis=0), chosen)
    routed = routed[: 2 * rows] + routed[2 * rows :]
    for owner in range(groups):
        piece = routed[:, owner * capacity : (owner + 1) * capacity]
        out_ref[owner] = jnp.concatenate([piece[:rows], piece[rows:]], axis=1)
    state_kernel(edges_ref, counts_ref, dynamics_ref, state_ref, moved_ref, band_ref)


def fine_step(arrived, band_edges, owner_counts, dynamics, state, profiles, coarse):
    groups, capacity = owner_counts.shape[0], state.shape[0]
    turns, table = fine_tables(groups, profiles, coarse)
    out, moved, band = pl.pallas_call(
        functools.partial(fine_kernel, profiles, coarse * groups * HALF),
        out_shape=(
            jax.ShapeDtypeStruct((groups, profiles * KINDS, LANES), F32),
            jax.ShapeDtypeStruct((2 * capacity, STATES), F32),
            jax.ShapeDtypeStruct((2 * capacity, LANES), jnp.int32),
        ),
        in_specs=[SMEM] * 2 + [VMEM] * 5,
        out_specs=(VMEM,) * 3,
        compiler_params=pltpu.CompilerParams(vmem_limit_bytes=32 << 20),
        name="fine_dft",
    )(
        band_edges,
        owner_counts,
        arrived,
        jnp.asarray(turns),
        jnp.asarray(table),
        dynamics.reshape(NCLASS * STATES, STATES),
        state,
    )
    return out.reshape(groups * profiles, KINDS, LANES), moved, band


def fine_step_general(arrived, owner_counts, capacity):
    groups, rows = arrived.shape[:2]
    coarse = 2 * rows * groups
    fine_length = groups * HALF
    order = coarse * fine_length
    own = lax.axis_index("bins")
    real, imag = arrived[:, :, :HALF], arrived[:, :, HALF:]
    points = jnp.arange(fine_length, dtype=jnp.int32).reshape(groups, 1, HALF)
    k_index = own * rows + jnp.arange(rows, dtype=jnp.int32)[None, :, None]
    cosine, sine = unit_turn(points * k_index & (order - 1), order)
    packed = (own == 0) & (jnp.arange(rows)[None, :, None] == 0)
    middle = jnp.where(own == 0, imag[:, :1], 0.0)
    imag = jnp.where(packed, 0.0, imag)
    real, imag = real * cosine + imag * sine, imag * cosine - real * sine
    cosine, sine = unit_turn(points * (coarse // 2), order)
    real = jnp.concatenate([real, middle * cosine], axis=1)
    imag = jnp.concatenate([imag, -middle * sine], axis=1)

    def turned(pattern, root, parts):
        cosine, sine = (jnp.asarray(part.astype(np.float32)) for part in root)
        mul = functools.partial(jnp.einsum, pattern, precision=HIGHEST)
        return (
            mul(cosine, parts[0]) - mul(sine, parts[1]),
            mul(cosine, parts[1]) + mul(sine, parts[0]),
        )

    group_index, point_index = np.arange(groups), np.arange(HALF)
    parts = turned(
        "cu,crj->urj", unit_root(groups, group_index[:, None] * group_index), (real, imag)
    )
    parts = turned(
        "uj,urj->urj", unit_root(fine_length, group_index[:, None] * point_index), parts
    )
    parts = turned(
        "jv,urj->vur", unit_root(HALF, point_index[:, None] * point_index), parts
    )
    tiles = fine_length // 2
    kept = jnp.concatenate([~packed[0, :, 0], jnp.zeros((1,), bool)])
    sides = []
    for part, sign in zip(parts, (1.0, -1.0)):
        part = part.reshape(fine_length, rows + 1)
        sides.append((part[:tiles], sign * jnp.where(kept, part[tiles:][::-1], 0.0)))
    power = sum(jnp.sum(part * part, axis=1) for pair in sides for part in pair)
    starts = jnp.cumsum(owner_counts) - owner_counts
    slot_index = jnp.arange(capacity, dtype=jnp.int32)
    filled = slot_index[None, :] < owner_counts[:, None]
    chosen = jnp.clip(starts[:, None] + slot_index[None, :], 0, tiles - 1)

    def kinds(low, high):
        low_sums, high_sums = jnp.sum(low[:, :rows], axis=1), jnp.sum(high[:, 1:rows], axis=1)
        values = jnp.stack([low_sums, high_sums, high[:, 0] + low[:, rows], power], axis=1)
        return jnp.where(filled[:, :, None], values[chosen], 0.0).transpose(0, 2, 1)

    return jnp.concatenate([kinds(*sides[0]), kinds(*sides[1])], axis=2)


def pool_table(shares, coarse):
    pool = np.zeros((shares, KINDS, 6, STATES), np.float32)
    wide = TILE // STATES
    rows = coarse // 2 // shares
    for share in range(shares):
        first = rows * share
        rest = coarse - first if share else coarse // 2
        for kind, at in enumerate((first, coarse - first - 1, rest)):
            for band in range(NCLASS):
                pool[share, kind, band, at // wide >> band] = 1.0
        pool[share, 3, NCLASS, :] = 1.0
    return pool.reshape(shares * KINDS, 6 * STATES).astype(BF16)


def state_kernel(edges_ref, counts_ref, dynamics_ref, state_ref, moved_ref, band_ref):
    own = lax.axis_index("bins")
    groups = counts_ref.shape[0]
    capacity = state_ref.shape[0]
    wide = NCLASS * STATES

    def before(owner, start):
        return start + jnp.where(owner < own, counts_ref[owner], 0)

    start = lax.fori_loop(0, groups, before, jnp.int32(0))
    slot = lax.broadcasted_iota(jnp.int32, (2 * capacity, LANES), 0) & (capacity - 1)
    band = jnp.zeros_like(slot)
    for edge in range(1, NCLASS):
        band = band + jnp.where(slot + start >= edges_ref[edge], 1, 0)
    band = jnp.where(slot < counts_ref[own], band, -1)
    band_ref[...] = band
    state = state_ref[...]
    state = jnp.concatenate([state[:, :STATES], state[:, STATES:]], axis=0)
    row = lax.broadcasted_iota(jnp.int32, (wide, STATES), 0)
    column = lax.broadcasted_iota(jnp.int32, (wide, STATES), 1)
    limit = STATES >> (row >> 6)
    inside = ((row & (STATES - 1)) < limit) & (column < limit)
    dynamics = jnp.where(inside, dynamics_ref[...], 0.0)
    state_high, state_low = split_two(state)
    high, low = split_two(dynamics)
    moved = lax.dot_general(
        jnp.concatenate([state_high, state_low, state_high], axis=1),
        jnp.concatenate([high, high, low], axis=1),
        (((1,), (1,)), ((), ())),
        preferred_element_type=F32,
    )
    moved = jnp.concatenate([moved, jnp.zeros((2 * capacity, STATES), F32)], axis=1)
    moved_ref[...] = of_band(moved, band)


def of_band(values, band):
    lane = lax.broadcasted_iota(jnp.int32, band.shape, 1) >> 6
    folded = jnp.zeros(band.shape, F32)
    for pair in range((NCLASS + 1) // 2):
        piece = values[:, pair * LANES : (pair + 1) * LANES]
        folded = folded + jnp.where(lane + 2 * pair == band, piece, 0.0)
    return folded[:, :STATES] + folded[:, STATES:]


def update_kernel(count, x_ref, pool_ref, moved_ref, band_ref, out_ref):
    capacity = out_ref.shape[0]
    band = band_ref[...]
    sums = lax.dot_general(
        jnp.concatenate(split_two(x_ref[...]), axis=1),
        pool_ref[...],
        (((0,), (0,)), ((), ())),
        preferred_element_type=F32,
    )
    sums = sums[: 2 * capacity] + sums[2 * capacity :]
    power = sums[:, NCLASS * STATES :] * (1.0 / count)
    span = jnp.left_shift(TILE // STATES, jnp.maximum(band[:, :STATES], 0)).astype(F32)
    scaling = 1.0 / jnp.sqrt(span * (power + EPSILON))
    result = moved_ref[...] + of_band(sums, band) * scaling
    out_ref[...] = jnp.concatenate([result[:capacity], result[capacity:]], axis=1)


def state_step(band_edges, owner_counts, dynamics, state):
    rows = 2 * state.shape[0]
    return pl.pallas_call(
        state_kernel,
        out_shape=(
            jax.ShapeDtypeStruct((rows, STATES), F32),
            jax.ShapeDtypeStruct((rows, LANES), jnp.int32),
        ),
        in_specs=[SMEM, SMEM, VMEM, VMEM],
        out_specs=(VMEM, VMEM),
        compiler_params=pltpu.CompilerParams(vmem_limit_bytes=32 << 20),
        cost_estimate=pl.CostEstimate(flops=1 << 25, bytes_accessed=1 << 19, transcendentals=0),
        name="state_step",
    )(band_edges, owner_counts, dynamics.reshape(NCLASS * STATES, STATES), state)


def update_step(arrived, moved, band, coarse, count):
    shares = arrived.shape[0]
    return pl.pallas_call(
        functools.partial(update_kernel, count),
        out_shape=jax.ShapeDtypeStruct((moved.shape[0] // 2, 2 * STATES), F32),
        in_specs=[VMEM] * 4,
        out_specs=VMEM,
        compiler_params=pltpu.CompilerParams(vmem_limit_bytes=32 << 20),
        name="state_update",
    )(arrived.reshape(shares * KINDS, LANES), jnp.asarray(pool_table(shares, coarse)), moved, band)


def exchanged(values, axes):
    return lax.all_to_all(values, axes, split_axis=0, concat_axis=0, tiled=True)


def body(profiles, band_edges, owner_counts, dynamics, prev_state):
    groups, scans = lax.axis_size("bins"), lax.axis_size("scans")
    prof_rows, length = profiles.shape
    capacity = prev_state.shape[0]
    coarse = length // HALF
    count = prof_rows * scans * TILE
    state = prev_state.reshape(capacity, 2 * STATES)
    if groups == 8 and scans == 4 and coarse == 16 * groups * scans:
        columns = exchanged(columns_step(profiles.reshape(length), groups), "bins")
        blocks = coarse_step(columns.reshape(coarse // 2, LANES))
        blocks = exchanged(blocks, ("bins", "scans"))
        payload, moved, band = fine_step(
            blocks, band_edges, owner_counts, dynamics, state, scans, coarse
        )
        arrived = exchanged(payload, ("bins", "scans"))
    else:
        moved, band = state_step(band_edges, owner_counts, dynamics, state)
        columns = profiles.reshape(coarse // groups, groups, HALF).transpose(1, 0, 2)
        columns = exchanged(columns, "bins").reshape(coarse, HALF)
        blocks = exchanged(coarse_step_general(columns, groups), "bins")
        arrived = exchanged(fine_step_general(blocks, owner_counts, capacity), "bins")
        power = lax.psum(arrived[:, 3:], "scans")
        arrived = jnp.concatenate([arrived[:, :3], power], axis=1)
    updated = update_step(arrived, moved, band, coarse, count)
    return updated.reshape(prev_state.shape)


def solution(mesh):
    return jax.shard_map(
        body,
        mesh=mesh,
        in_specs=(P("scans", "bins"), P(), P(), P(), P("bins", "scans", None)),
        out_specs=P("bins", "scans", None),
        check_vma=False,
    )
```

time: 40.2 us -> 39.6 us (0.985)
  blocking collectives: 34.9 us -> 34.1 us
    reshape x1 -> x0, local copies, waits for them, and re-layouts: 0.97 us -> none  [body(): profiles.reshape(coarse // groups, groups, LANES).transpose(1, 0, 2)]
    unnamed x18, local copies, waits for them, and re-layouts: 0.67 us -> 1.64 us
    all_to_all x3, blocking collectives: 34.9 us -> 34.1 us  [exchanged(): return lax.all_to_all(values, axes, split_axis=0, concat_axis=0, tiled=True)]
where the time goes in v4:
time: 39.6 us; the launch traced here: 39.3 us
  blocking collectives  34.1 us (86%)
  Pallas kernels  3.56 us (9%)
  local copies, waits for them, and re-layouts  1.64 us (4%)
    all_to_all x3, blocking collectives, exchanged(): return lax.all_to_all(values, axes, split_axis=0, concat_axis=0, tiled=True)  34.1 us
    pallas_call x1, Pallas kernels, fine_step(): pl.pallas_call(functools.partial(fine_kernel, profiles, coarse * groups *...  2.07 us
    unnamed x18, local copies, waits for them, and re-layouts  1.64 us
    pallas_call x1, Pallas kernels, update_step(): pl.pallas_call(functools.partial(update_kernel, count), out_shape=jax.Sha...  1.02 us

profile of v4, /device:TPU:0, one launch (start us, length us, event | category | flops | bytes accessed | tf_op | source)
XLA Modules:
  0.0 39.3 jit_solution(17451843565275642180)
XLA Ops:
  0.0 0.0 copy-start
  0.0 0.0 copy-start.2
  0.0 1.0 %copy-done.2 = f32[1,32768]{1,0:T(1,128)S(1)} copy-done((f32[1,32768]{1,0:T(1,128)S(1)}, f32[1,32768]{1,0:T(1,128)}, u32[]{:S(2)}) %copy-start.2) | copy-done | bytes 131096
  1.0 0.1 columns.1
  1.1 14.4 %all_to_all.15 = f32[8,32,128]{2,1,0:T(8,128)S(1)} all-to-all(f32[8,32,128]{2,1,0:T(8,128)S(1)} %columns.1), channel_id=1, replica_groups=mesh['bins'=8,'scans'=4] {'bins'}, dimensions={0} | all-to-all | bytes 262144 | tf_op jit(solution)/shard_map/all_to_all | solution.py:477
  15.5 0.0 copy-done
  15.5 0.0 copy-start.5
  15.5 0.4 coarse_dft.1
  15.9 0.0 copy-start.1
  15.9 0.0 copy-start.4
  15.9 0.0 copy-start.6
  15.9 10.4 %all_to_all.16.x_ref = f32[32,8,128]{2,1,0:T(8,128)S(1)} all-to-all(f32[32,8,128]{2,1,0:T(8,128)S(1)} %coarse_dft.1), channel_id=1, replica_groups=mesh['bins'=8,'scans'=4] {'bins','scans'}, dimensions={0} | all-to-all | bytes 262144 | tf_op jit(solution)/shard_map/all_to_all | solution.py:477
  26.3 0.0 copy-start.7
  26.3 0.0 copy-start.8
  26.3 0.0 copy-done.5
  26.3 0.0 copy-done.1
  26.3 0.0 copy-done.4
  26.4 0.0 copy-done.6
  26.4 0.6 %copy-done.7 = s32[6]{0:T(128)S(1)} copy-done((s32[6]{0:T(128)S(1)}, s32[6]{0:T(128)}, u32[]{:S(2)}) %copy-start.7) | copy-done | bytes 48
  27.0 0.0 copy-done.8
  27.0 2.1 %fine_dft.1 = (f32[8,16,128]{2,1,0:T(8,128)S(1)}, f32[128,64]{1,0:T(8,128)S(1)}, s32[128,128]{1,0:T(8,128)S(1)}) custom-call(s32[6]{0:T(128)S(1)} %copy-done.7, s32[8]{0:T(128)S(1)} %copy-done.8, f32[32,8,128]{2,1,0:T(8,128)S(1)} %all_to_all.16.x_ref, f32[24,128]{1,0:T(8,128)S(1)} %copy-done.6, bf16[160,256]{1,0:T(8,128)(2,1)S(1)} %copy-done.4, ...), custom_call_target="tpu_custom_call" | custom-call | tf_op jit(solution)/shard_map/fine_dft/pallas_call | solution.py:294
  29.1 0.0 copy-start.3
  29.1 9.2 %all_to_all.17 = f32[32,4,128]{2,1,0:T(4,128)S(1)} all-to-all(f32[32,4,128]{2,1,0:T(4,128)S(1)} %bitcast.13), channel_id=1, replica_groups=mesh['bins'=8,'scans'=4] {'bins','scans'}, dimensions={0} | all-to-all | bytes 131072 | tf_op jit(solution)/shard_map/all_to_all | solution.py:477
  38.3 0.0 copy-done.3
  38.3 1.0 %state_update.1 = f32[64,128]{1,0:T(8,128)} custom-call(f32[128,128]{1,0:T(8,128)S(1)} %bitcast.10, bf16[128,384]{1,0:T(8,128)(2,1)S(1)} %copy-done.3, f32[128,64]{1,0:T(8,128)S(1)} %get-tuple-element.9.moved_ref, s32[128,128]{1,0:T(8,128)S(1)} %get-tuple-element.10.band_ref), custom_call_target="tpu_custom_call" | custom-call | tf_op jit(solution)/shard_map/state_update/pallas_call | solution.py:466
Async XLA Ops:
  0.0 15.5 %copy-start = (bf16[512,512]{1,0:T(8,128)(2,1)S(1)}, bf16[512,512]{1,0:T(8,128)(2,1)}, u32[]{:S(2)}) copy-start(bf16[512,512]{1,0:T(8,128)(2,1)} %constant.8.clone.table_ref) | copy-start | bytes 1572868
  0.0 1.0 %copy-start.2 = (f32[1,32768]{1,0:T(1,128)S(1)}, f32[1,32768]{1,0:T(1,128)}, u32[]{:S(2)}) copy-start(f32[1,32768]{1,0:T(1,128)} %param.9) | copy-start | bytes 393220
  15.5 10.8 %copy-start.5 = (f32[64,1,128]{2,1,0:T(1,128)S(1)}, f32[64,1,128]{2,1,0:T(1,128)}, u32[]{:S(2)}) copy-start(f32[64,1,128]{2,1,0:T(1,128)} %param.13) | copy-start | bytes 98308
  15.9 10.5 %copy-start.1 = (f32[5,64,64]{2,1,0:T(8,128)S(1)}, f32[5,64,64]{2,1,0:T(8,128)}, u32[]{:S(2)}) copy-start(f32[5,64,64]{2,1,0:T(8,128)} %param.12) | copy-start | bytes 245764
  15.9 10.5 %copy-start.4 = (bf16[160,256]{1,0:T(8,128)(2,1)S(1)}, bf16[160,256]{1,0:T(8,128)(2,1)}, u32[]{:S(2)}) copy-start(bf16[160,256]{1,0:T(8,128)(2,1)} %constant.10.clone.table_ref) | copy-start | bytes 245764
  15.9 10.5 %copy-start.6 = (f32[24,128]{1,0:T(8,128)S(1)}, f32[24,128]{1,0:T(8,128)}, u32[]{:S(2)}) copy-start(f32[24,128]{1,0:T(8,128)} %constant.9.clone.turns_ref) | copy-start | bytes 36868
  26.3 0.7 %copy-start.7 = (s32[6]{0:T(128)S(1)}, s32[6]{0:T(128)}, u32[]{:S(2)}) copy-start(s32[6]{0:T(128)} %edges_ref.1) | copy-start | bytes 76
  26.3 0.7 %copy-start.8 = (s32[8]{0:T(128)S(1)}, s32[8]{0:T(128)}, u32[]{:S(2)}) copy-start(s32[8]{0:T(128)} %counts_ref.1) | copy-start | bytes 100
  29.1 9.3 %copy-start.3 = (bf16[128,384]{1,0:T(8,128)(2,1)S(1)}, bf16[128,384]{1,0:T(8,128)(2,1)}, u32[]{:S(2)}) copy-start(bf16[128,384]{1,0:T(8,128)(2,1)} %constant.11.clone.pool_ref) | copy-start | bytes 294916

commit v5 on v4

v5 whole, which is shorter than its diff:
```python
import functools
import math

import jax
import jax.numpy as jnp
import numpy as np
from jax import lax
from jax.experimental import pallas as pl
from jax.experimental.pallas import tpu as pltpu
from jax.sharding import PartitionSpec as P

TILE = 512
STATES = 64
NCLASS = 5
LANES = 128

EPSILON = 1e-05
HIGHEST = lax.Precision.HIGHEST
BF16 = jnp.bfloat16
F32 = jnp.float32


def unit_root(order, exponents):
    angles = 2.0 * np.pi * (np.asarray(exponents, dtype=np.int64) % order) / order
    return np.cos(angles), -np.sin(angles)


def two_terms(values):
    high = np.asarray(values, np.float32).astype(BF16)
    low = (np.asarray(values, np.float64) - high.astype(np.float64)).astype(BF16)
    return high, low


def split_two(values):
    high = values.astype(BF16)
    return high, (values - high.astype(F32)).astype(BF16)


def dot(left, right):
    return jnp.dot(left, right, preferred_element_type=F32)


VMEM = pl.BlockSpec(memory_space=pltpu.VMEM)
PARAMS = pltpu.CompilerParams(vmem_limit_bytes=32 << 20)


KINDS = 4
HALF = LANES // 2


def unit_turn(phase, order):
    shifted = phase + order // 8
    quadrant = (shifted >> (order.bit_length() - 3)) & 3
    x = ((shifted & (order // 4 - 1)) - order // 8).astype(F32) * (2.0 * math.pi / order)
    y = x * x
    cosine = 1.0 + y * (-1 / 2 + y * (1 / 24 + y * (-1 / 720 + y * (1 / 40320))))
    sine = x * (1.0 + y * (-1 / 6 + y * (1 / 120 + y * (-1 / 5040 + y * (1 / 362880)))))
    odd = (quadrant & 1) == 1
    real, imag = jnp.where(odd, sine, cosine), jnp.where(odd, cosine, sine)
    real = jnp.where((quadrant == 1) | (quadrant == 2), -real, real)
    return real, jnp.where(quadrant >= 2, -imag, imag)


def iotas(shape):
    return [lax.broadcasted_iota(jnp.int32, shape, axis) for axis in range(len(shape))]


def columns_kernel(
    x_ref, edges_ref, counts_ref, out_ref, wanted_ref, lane_band_ref, row_band_ref
):
    groups, rows, _ = out_ref.shape
    capacity = row_band_ref.shape[0]
    low_lanes = iotas((rows, LANES))[1] < HALF
    for pair in range(groups // 2):
        even = x_ref[pl.ds(pair, rows, stride=groups), :]
        odd = x_ref[pl.ds(groups // 2 + pair, rows, stride=groups), :]
        out_ref[2 * pair] = jnp.where(low_lanes, even, pltpu.roll(odd, HALF, 1))
        out_ref[2 * pair + 1] = jnp.where(low_lanes, pltpu.roll(even, HALF, 1), odd)
    own = lax.axis_index("bins")
    counts = [
        jnp.broadcast_to(counts_ref[:, owner : owner + 1], (1, LANES)) for owner in range(groups)
    ]
    lane = iotas((1, LANES))[1]
    start = jnp.zeros((1, LANES), jnp.int32)
    own_start, own_count = start, start
    wanted = []
    for owner, count in enumerate(counts):
        rank = lane & (HALF - 1)
        wanted.append(jnp.where(rank < count, start + rank, -1))
        own_start = jnp.where(own == owner, start, own_start)
        own_count = jnp.where(own == owner, count, own_count)
        start = start + count
    for pair in range(groups // 2):
        wanted_ref[:, pair * LANES : (pair + 1) * LANES] = jnp.where(
            lane < HALF, wanted[2 * pair], wanted[2 * pair + 1]
        )
    edges = [jnp.broadcast_to(edges_ref[:, at : at + 1], (1, LANES)) for at in range(1, NCLASS)]
    for ref, slot in (
        (lane_band_ref, lane & (capacity - 1)),
        (row_band_ref, iotas((capacity, LANES))[0]),
    ):
        band = jnp.zeros_like(slot)
        for edge in edges:
            band = band + jnp.where(slot + own_start >= edge, 1, 0)
        ref[...] = jnp.where(slot < own_count, band, -1)


def columns_step(profile, band_edges, owner_counts, capacity):
    groups = owner_counts.shape[0]
    rows = profile.shape[0] // (groups * LANES)
    return pl.pallas_call(
        columns_kernel,
        out_shape=(
            jax.ShapeDtypeStruct((groups, rows, LANES), F32),
            jax.ShapeDtypeStruct((1, groups * capacity), jnp.int32),
            jax.ShapeDtypeStruct((1, LANES), jnp.int32),
            jax.ShapeDtypeStruct((capacity, LANES), jnp.int32),
        ),
        in_specs=[VMEM] * 3,
        out_specs=(VMEM,) * 4,
        compiler_params=PARAMS,
        name="columns",
    )(profile.reshape(-1, LANES), band_edges.reshape(1, -1), owner_counts.reshape(1, -1))


def coarse_table(coarse):
    half, quarter = coarse // 2, coarse // 4
    k_index = np.arange(quarter)
    a_index = np.concatenate([np.arange(0, half, 2), np.arange(1, half, 2)])
    real, imag = unit_root(half, k_index[:, None] * a_index[None, :])
    imag[0] = 1
    parts = [part.reshape(quarter // 16, 2, 2, 1, 4, half) for part in (real, imag)]
    parts = np.concatenate(parts, axis=3).transpose(0, 2, 3, 1, 4, 5)
    return np.concatenate(two_terms(parts.reshape(half, half)), axis=1)


def coarse_kernel(groups, shares, x_ref, table_ref, out_ref, turn_ref):
    half = x_ref.shape[0]
    quarter = half // 2
    row, lane = iotas((8, LANES))
    low_lanes = lane < HALF
    sums = []
    for parity in range(2):
        high, low = split_two(x_ref[pl.ds(parity, quarter, stride=2), :])
        at = parity * quarter
        both = dot(table_ref[:, at : at + quarter], jnp.concatenate([high, low], axis=1))
        rest = dot(table_ref[:, half + at : half + at + quarter], high)
        sums.append(both[:, :LANES] + both[:, LANES:] + rest)
    base = 8 * (row >> 2) + 4 * (lane >> 6) + (row & 3)
    base_cosine, base_sine = unit_turn(base, 2 * half)
    packed = low_lanes & (row == 0)
    for sign, block in [(sign, block) for block in range(half // 32) for sign in (1, -1)]:
        pieces = []
        for at in range(32 * block, 32 * (block + 1), 8):
            even, odd = sums[0][at : at + 8], sums[1][at : at + 8]
            pieces.append(even + odd if sign > 0 else even - odd)
        real_low, imag_low, real_high, imag_high = pieces
        if block == 0 and sign < 0:
            imag_low = jnp.where(row == 0, 0.0, imag_low)
        even_real = jnp.where(low_lanes, real_low, pltpu.roll(real_high, HALF, 1))
        even_imag = jnp.where(low_lanes, imag_low, pltpu.roll(imag_high, HALF, 1))
        odd_real = jnp.where(low_lanes, pltpu.roll(real_low, HALF, 1), real_high)
        odd_imag = jnp.where(low_lanes, pltpu.roll(imag_low, HALF, 1), imag_high)
        first = 2 * block + (0 if sign > 0 else shares // 2)
        angle = math.pi * 8 * first / half
        cosine = base_cosine * math.cos(angle) - base_sine * math.sin(angle)
        sine = base_sine * math.cos(angle) + base_cosine * math.sin(angle)
        real = even_real + odd_real * cosine + odd_imag * sine
        if first == 0:
            cosine = jnp.where(packed, -1.0, cosine)
        imag = even_imag + odd_imag * cosine - odd_real * sine
        out_ref[pl.ds(8 * first, 8, stride=2), :] = real
        out_ref[pl.ds(8 * first + 1, 8, stride=2), :] = imag
    own = lax.axis_index("bins") * lax.axis_size("scans") + lax.axis_index("scans")
    k_index = 8 * own + 4 * (lane >> 6) + (row & 3)
    order = 2 * half * groups * HALF
    for c in range(groups):
        phase = ((c * HALF + (lane & (HALF - 1))) * k_index) & (order - 1)
        turn_ref[2 * c], turn_ref[2 * c + 1] = unit_turn(phase, order)


def coarse_step(columns, groups, shares):
    half = columns.shape[0]
    return pl.pallas_call(
        functools.partial(coarse_kernel, groups, shares),
        out_shape=(
            jax.ShapeDtypeStruct((half, LANES), F32),
            jax.ShapeDtypeStruct((2 * groups, 8, LANES), F32),
        ),
        in_specs=[VMEM] * 2,
        out_specs=(VMEM,) * 2,
        compiler_params=PARAMS,
        name="coarse_dft",
    )(columns, jnp.asarray(coarse_table(2 * half)))


def coarse_step_general(columns, shares):
    coarse = columns.shape[0]
    half = coarse // 2
    real, imag = unit_root(coarse, np.arange(half)[:, None] * np.arange(coarse)[None, :])
    imag[0] = 1 - 2 * (np.arange(coarse) % 2)
    table = jnp.asarray(np.concatenate([real, imag]).astype(np.float32))
    spectrum = jnp.dot(table, columns, precision=HIGHEST)
    blocks = jnp.concatenate([spectrum[:half], spectrum[half:]], axis=1)
    return blocks.reshape(shares, half // shares, LANES)


def fine_tables(groups, profiles, coarse):
    fine_length = groups * HALF
    doubled = np.arange(LANES) % HALF
    turn = unit_root(fine_length, np.arange(groups)[:, None] * doubled[None, :])
    middle = (np.arange(groups)[:, None] * HALF + doubled[None, :]) * (coarse // 2)
    middle = unit_root(coarse * fine_length, middle)
    turns = np.concatenate(turn + middle).astype(np.float32)
    order = np.arange(HALF)
    order[HALF // 2 :] = order[HALF // 2 :][::-1]
    real, imag = unit_root(HALF, np.arange(HALF)[:, None] * order[None, :])
    sign = np.where(np.arange(HALF) < HALF // 2, 1, -1)
    both = np.eye(2)
    matrix = np.block(
        [
            [np.kron(both, real), np.kron(both, imag * sign)],
            [np.kron(both, -imag), np.kron(both, real * sign)],
        ]
    )
    sums = np.zeros((3, profiles, KINDS, 2, profiles // 2 + 2, 2, 4), np.float32)
    for p in range(profiles):
        pair, which = divmod(p, 2)
        sums[0, p, 0, :, pair, which, :] = 1
        sums[1, p, 1, :, pair, which, 1:] = 1
        sums[2, p, 1, :, pair, which, :] = 1
        sums[1, p, 2, :, pair, which, 0] = 1
        sums[0, p, 2, :, profiles // 2, which, pair] = 1
        sums[:, p, 3, :, profiles // 2 + 1] = 1
    sums = sums.reshape(3 * profiles * KINDS, -1)
    sums = np.pad(sums, [(0, 0), (0, 4 * LANES - sums.shape[1])]).astype(BF16)
    return turns, np.concatenate([np.concatenate(two_terms(matrix), axis=1), sums])


def add(p, q):
    return (p[0] + q[0], p[1] + q[1])


def sub(p, q):
    return (p[0] - q[0], p[1] - q[1])


def times(p, cosine, sine):
    return (p[0] * cosine + p[1] * sine, p[1] * cosine - p[0] * sine)


def eight_point(values):
    half = math.sqrt(0.5)

    def down(p):
        return (p[1], -p[0])

    def four(a, b, c, d):
        s0, s1, s2, s3 = add(a, c), sub(a, c), add(b, d), sub(b, d)
        turned = (s1[0] + s3[1], s1[1] - s3[0]), (s1[0] - s3[1], s1[1] + s3[0])
        return add(s0, s2), turned[0], sub(s0, s2), turned[1]

    even = four(values[0], values[2], values[4], values[6])
    odd = four(values[1], values[3], values[5], values[7])
    turned = [
        odd[0],
        ((odd[1][0] + odd[1][1]) * half, (odd[1][1] - odd[1][0]) * half),
        down(odd[2]),
        ((odd[3][1] - odd[3][0]) * half, (odd[3][0] + odd[3][1]) * -half),
    ]
    return [add(e, t) for e, t in zip(even, turned)] + [sub(e, t) for e, t in zip(even, turned)]


def fine_kernel(
    profiles,
    x_ref,
    turn_ref,
    wanted_ref,
    band_ref,
    turns_ref,
    table_ref,
    dynamics_ref,
    state_ref,
    out_ref,
    moved_ref,
):
    groups = out_ref.shape[0]
    first = (lax.axis_index("bins") == 0) & (lax.axis_index("scans") == 0)
    row, lane = iotas((8, LANES))
    low_lanes = lane < HALF
    low_side = (lane & (HALF - 1)) < HALF // 2
    packed = first & low_lanes & ((row & 3) == 0)
    shifted = first & low_lanes & ((row & 3) == 1)
    pairs = profiles // 2
    columns = [[] for _ in range(pairs + 1)]
    for c in range(groups):
        cosine, sine = turn_ref[2 * c], turn_ref[2 * c + 1]
        at = c * 8 * profiles
        for pair in range(pairs):
            real = x_ref[pl.ds(at + 16 * pair, 8, stride=2), :]
            imag = x_ref[pl.ds(at + 16 * pair + 1, 8, stride=2), :]
            if pair == 0:
                middle = jnp.where(packed, imag, 0.0)
            imag = jnp.where(packed, 0.0, imag)
            columns[pair].append(times((real, imag), cosine, sine))
        middle = jnp.where(shifted, x_ref[pl.ds(at + 15, 8, stride=2), :], middle)
        middle_real = turns_ref[2 * groups + c : 2 * groups + c + 1, :]
        middle_imag = turns_ref[3 * groups + c : 3 * groups + c + 1, :]
        columns[pairs].append((middle * middle_real, middle * middle_imag))
    transformed = [eight_point(column) for column in columns]
    blocks = []
    for u in range(groups):
        cosine, sine = turns_ref[u : u + 1, :], -turns_ref[groups + u : groups + u + 1, :]
        for column in transformed:
            blocks.append(times(column[u], cosine, sine) if u else column[u])
    wide = 2 * LANES
    size = wide
    left = jnp.concatenate(
        [jnp.concatenate([block[part] for block in blocks], axis=0) for part in range(2)], axis=1
    )
    high, low = split_two(left)
    product = dot(high, table_ref[:size, :])
    product = product[:, :wide] + product[:, wide:] + dot(low, table_ref[:size, :wide])
    spectrum = []
    for u in range(groups):
        spectrum.append([])
        for at in range(pairs + 1):
            start = 8 * (u * (pairs + 1) + at)
            block = (product[start : start + 8, :LANES], product[start : start + 8, LANES:])
            dropped = ~low_side & packed if at < pairs else ~low_side
            spectrum[u].append(tuple(jnp.where(dropped, 0.0, part) for part in block))
    power = [
        sum(block[0] * block[0] + block[1] * block[1] for block in spectrum[u])
        for u in range(groups)
    ]
    summands = []
    for part in range(2):
        for u in range(groups):
            mirror = groups - 1 - u
            rows = [
                jnp.where(low_side, spectrum[u][pair][part], spectrum[mirror][pair][part])
                for pair in range(pairs)
            ]
            rows.append(spectrum[u][pairs][part])
            rows.append(jnp.where(low_side, power[u], power[mirror]))
            summands.append(jnp.concatenate(rows, axis=0))
    summands = jnp.concatenate(split_two(jnp.concatenate(summands, axis=1)), axis=0)
    summed = dot(table_ref[size:, : summands.shape[0]], summands)
    rows = summed.shape[0] // 3
    _, lanes = iotas((rows, LANES))
    side, early = (lanes & (HALF - 1)) < HALF // 2, lanes < HALF
    left = []
    for part in range(2):
        pieces = []
        for at in range(part * groups, (part + 1) * groups):
            piece = summed[:, at * LANES : (at + 1) * LANES]
            piece = jnp.where(
                side,
                piece[:rows],
                jnp.where(early, piece[rows : 2 * rows], piece[2 * rows :]),
            )
            pieces.append(piece)
        left.append(jnp.concatenate(pieces, axis=1))
    left = jnp.concatenate(split_two(jnp.concatenate(left, axis=0)), axis=0)
    wanted = wanted_ref[...]
    chosen = []
    for u in range(groups):
        tile = u + groups * iotas((HALF // 2, wanted.shape[1]))[0]
        chosen += [jnp.where(tile == wanted, 1.0, 0.0).astype(BF16)] * 4
    routed = dot(left, jnp.concatenate(chosen, axis=0))
    routed = routed[: 2 * rows] + routed[2 * rows :]
    for pair in range(groups // 2):
        real = routed[:rows, pair * LANES : (pair + 1) * LANES]
        imag = routed[rows:, pair * LANES : (pair + 1) * LANES]
        out_ref[2 * pair] = jnp.where(early, real, pltpu.roll(imag, HALF, 1))
        out_ref[2 * pair + 1] = jnp.where(early, pltpu.roll(real, HALF, 1), imag)
    moved_ref[...] = state_product(dynamics_ref[...], state_ref[...], band_ref[...])


def state_product(dynamics, state, band):
    row, column = iotas((NCLASS * STATES, STATES))
    limit = STATES >> (row >> 6)
    inside = ((row & (STATES - 1)) < limit) & (column < limit)
    dynamics = jnp.where(inside, dynamics, 0.0)
    empty = jnp.zeros_like(dynamics)
    halves = [
        jnp.concatenate([dynamics, empty], axis=1),
        jnp.concatenate([empty, dynamics], axis=1),
    ]
    matrix = jnp.concatenate(
        [half[k * STATES : (k + 1) * STATES] for k in range(NCLASS) for half in halves], axis=0
    )
    state_high, state_low = split_two(state)
    high, low = split_two(matrix)
    moved = lax.dot_general(
        jnp.concatenate([state_high, state_low, state_high], axis=1),
        jnp.concatenate([high, high, low], axis=1),
        (((1,), (1,)), ((), ())),
        preferred_element_type=F32,
    )
    result = jnp.zeros(state.shape, F32)
    for k in range(NCLASS):
        result = jnp.where(band == k, moved[:, k * LANES : (k + 1) * LANES], result)
    return result


def fine_step(arrived, turn, wanted, band, dynamics, state, profiles, coarse):
    groups = turn.shape[0] // 2
    turns, table = fine_tables(groups, profiles, coarse)
    out, moved = pl.pallas_call(
        functools.partial(fine_kernel, profiles),
        out_shape=(
            jax.ShapeDtypeStruct((groups, profiles * KINDS, LANES), F32),
            jax.ShapeDtypeStruct(state.shape, F32),
        ),
        in_specs=[VMEM] * 8,
        out_specs=(VMEM,) * 2,
        compiler_params=PARAMS,
        name="fine_dft",
    )(
        arrived,
        turn,
        wanted,
        band,
        jnp.asarray(turns),
        jnp.asarray(table),
        dynamics.reshape(NCLASS * STATES, STATES),
        state,
    )
    return out.reshape(groups * profiles, KINDS, LANES), moved


def fine_step_general(arrived, owner_counts, capacity):
    groups, rows = arrived.shape[:2]
    coarse = 2 * rows * groups
    fine_length = groups * HALF
    order = coarse * fine_length
    own = lax.axis_index("bins")
    real, imag = arrived[:, :, :HALF], arrived[:, :, HALF:]
    points = jnp.arange(fine_length, dtype=jnp.int32).reshape(groups, 1, HALF)
    k_index = own * rows + jnp.arange(rows, dtype=jnp.int32)[None, :, None]
    cosine, sine = unit_turn(points * k_index & (order - 1), order)
    packed = (own == 0) & (jnp.arange(rows)[None, :, None] == 0)
    middle = jnp.where(own == 0, imag[:, :1], 0.0)
    imag = jnp.where(packed, 0.0, imag)
    real, imag = real * cosine + imag * sine, imag * cosine - real * sine
    cosine, sine = unit_turn(points * (coarse // 2), order)
    real = jnp.concatenate([real, middle * cosine], axis=1)
    imag = jnp.concatenate([imag, -middle * sine], axis=1)

    def turned(pattern, root, parts):
        cosine, sine = (jnp.asarray(part.astype(np.float32)) for part in root)
        mul = functools.partial(jnp.einsum, pattern, precision=HIGHEST)
        return (
            mul(cosine, parts[0]) - mul(sine, parts[1]),
            mul(cosine, parts[1]) + mul(sine, parts[0]),
        )

    group_index, point_index = np.arange(groups), np.arange(HALF)
    parts = turned(
        "cu,crj->urj", unit_root(groups, group_index[:, None] * group_index), (real, imag)
    )
    parts = turned(
        "uj,urj->urj", unit_root(fine_length, group_index[:, None] * point_index), parts
    )
    parts = turned(
        "jv,urj->vur", unit_root(HALF, point_index[:, None] * point_index), parts
    )
    tiles = fine_length // 2
    kept = jnp.concatenate([~packed[0, :, 0], jnp.zeros((1,), bool)])
    sides = []
    for part, sign in zip(parts, (1.0, -1.0)):
        part = part.reshape(fine_length, rows + 1)
        sides.append((part[:tiles], sign * jnp.where(kept, part[tiles:][::-1], 0.0)))
    power = sum(jnp.sum(part * part, axis=1) for pair in sides for part in pair)
    starts = jnp.cumsum(owner_counts) - owner_counts
    slot_index = jnp.arange(capacity, dtype=jnp.int32)
    filled = slot_index[None, :] < owner_counts[:, None]
    chosen = jnp.clip(starts[:, None] + slot_index[None, :], 0, tiles - 1)

    def kinds(low, high):
        low_sums, high_sums = jnp.sum(low[:, :rows], axis=1), jnp.sum(high[:, 1:rows], axis=1)
        values = jnp.stack([low_sums, high_sums, high[:, 0] + low[:, rows], power], axis=1)
        return jnp.where(filled[:, :, None], values[chosen], 0.0).transpose(0, 2, 1)

    return jnp.concatenate([kinds(*sides[0]), kinds(*sides[1])], axis=2)


def pool_table(shares, coarse):
    pool = np.zeros((21, 16, shares, KINDS), np.float32)
    sums = pool[:20].reshape(NCLASS, STATES, shares, KINDS)
    wide = TILE // STATES
    rows = coarse // 2 // shares
    for share in range(shares):
        first = rows * share
        rest = coarse - first if share else coarse // 2
        for kind, at in enumerate((first, coarse - first - 1, rest)):
            for band in range(NCLASS):
                sums[band, at // wide >> band, share, kind] = 1.0
    pool[20, :, :, 3] = 1.0
    return pool.reshape(-1, shares * KINDS).astype(BF16)


def update_kernel(count, x_ref, pool_ref, moved_ref, band_ref, out_ref):
    band = band_ref[...]
    sums = dot(pool_ref[...], jnp.concatenate(split_two(x_ref[...]), axis=1))
    sums = sums[:, :LANES] + sums[:, LANES:]
    power = sums[NCLASS * STATES : NCLASS * STATES + 1] * (1.0 / count)
    span = jnp.left_shift(TILE // STATES, jnp.maximum(band, 0)).astype(F32)
    scaling = 1.0 / jnp.sqrt(span * (power + EPSILON))
    scaling = jnp.where(band < 0, 0.0, scaling)
    chosen = sums[:STATES]
    for k in range(1, NCLASS):
        chosen = jnp.where(band == k, sums[k * STATES : (k + 1) * STATES], chosen)
    chosen = chosen * scaling
    turned = jnp.transpose(jnp.concatenate([chosen, chosen], axis=0))
    half = turned.shape[0] // 2
    measured = jnp.where(iotas((half, LANES))[1] < STATES, turned[:half], turned[half:])
    out_ref[...] = moved_ref[...] + measured


def update_step(arrived, moved, band, coarse, count):
    shares = arrived.shape[0]
    return pl.pallas_call(
        functools.partial(update_kernel, count),
        out_shape=jax.ShapeDtypeStruct(moved.shape, F32),
        in_specs=[VMEM] * 4,
        out_specs=VMEM,
        compiler_params=PARAMS,
        name="state_update",
    )(arrived.reshape(shares * KINDS, LANES), jnp.asarray(pool_table(shares, coarse)), moved, band)


def state_step_general(band_edges, owner_counts, dynamics, state):
    own = lax.axis_index("bins")
    capacity = state.shape[0]
    slot = jnp.arange(capacity, dtype=jnp.int32)
    start = jnp.cumsum(owner_counts)[own] - owner_counts[own]
    band = jnp.sum((slot + start)[:, None] >= band_edges[None, 1:NCLASS], axis=1)
    band = jnp.where(slot < owner_counts[own], band, -1).astype(jnp.int32)
    limit = STATES >> jnp.arange(NCLASS)[:, None, None]
    index = jnp.arange(STATES)
    inside = (index[:, None] < limit) & (index[None, :] < limit)
    chosen = (band[:, None] == jnp.arange(NCLASS)[None, :]).astype(F32)
    picked = jnp.einsum(
        "rk,kij->rij", chosen, jnp.where(inside, dynamics, 0.0), precision=HIGHEST
    )
    parts = state.reshape(capacity, 2, STATES)
    moved = jnp.einsum("rij,rcj->rci", picked, parts, precision=HIGHEST)
    return moved.reshape(state.shape), jnp.tile(band, 2)[None, :]


def exchanged(values, axes):
    return lax.all_to_all(values, axes, split_axis=0, concat_axis=0, tiled=True)


def body(profiles, band_edges, owner_counts, dynamics, prev_state):
    groups, scans = lax.axis_size("bins"), lax.axis_size("scans")
    prof_rows, length = profiles.shape
    capacity = prev_state.shape[0]
    coarse = length // HALF
    shares = groups * scans
    count = prof_rows * scans * TILE
    state = prev_state.reshape(capacity, 2 * STATES)
    if groups == 8 and scans == 4 and coarse == 16 * shares and capacity == HALF:
        columns, wanted, lane_band, row_band = columns_step(
            profiles.reshape(length), band_edges, owner_counts, capacity
        )
        columns = exchanged(columns, "bins").reshape(coarse // 2, LANES)
        blocks, turn = coarse_step(columns, groups, shares)
        blocks = exchanged(blocks.reshape(shares, 8, LANES), ("bins", "scans"))
        payload, moved = fine_step(
            blocks.reshape(8 * shares, LANES),
            turn,
            wanted,
            row_band,
            dynamics,
            state,
            scans,
            coarse,
        )
        arrived = exchanged(payload, ("bins", "scans"))
    else:
        moved, lane_band = state_step_general(band_edges, owner_counts, dynamics, state)
        columns = profiles.reshape(coarse // groups, groups, HALF).transpose(1, 0, 2)
        columns = exchanged(columns, "bins").reshape(coarse, HALF)
        blocks = exchanged(coarse_step_general(columns, groups), "bins")
        arrived = exchanged(fine_step_general(blocks, owner_counts, capacity), "bins")
        power = lax.psum(arrived[:, 3:], "scans")
        arrived = jnp.concatenate([arrived[:, :3], power], axis=1)
    updated = update_step(arrived, moved, lane_band, coarse, count)
    return updated.reshape(prev_state.shape)


def solution(mesh):
    return jax.shard_map(
        body,
        mesh=mesh,
        in_specs=(P("scans", "bins"), P(), P(), P(), P("bins", "scans", None)),
        out_specs=P("bins", "scans", None),
        check_vma=False,
    )
```

time: 39.6 us -> 39 us (0.985)
  Pallas kernels: 3.56 us -> 2.34 us
  local copies, waits for them, and re-layouts: 1.64 us -> 2.3 us
    pallas_call x3, Pallas kernels: 2.54 us -> 1.42 us  [the longest x1 0.93 us: fine_step(): pl.pallas_call(functools.partial(fine_kernel, profiles), out_shape=(jax.S...]
    unnamed x18, local copies, waits for them, and re-layouts: 1.64 us -> 2.3 us
where the time goes in v5:
time: 39 us; the launch traced here: 38.8 us
  blocking collectives  34.1 us (87%)
  Pallas kernels  2.34 us (6%)
  local copies, waits for them, and re-layouts  2.3 us (6%)
    all_to_all x3, blocking collectives, exchanged(): return lax.all_to_all(values, axes, split_axis=0, concat_axis=0, tiled=True)  34.1 us
    unnamed x18, local copies, waits for them, and re-layouts  2.3 us
    pallas_call x1, Pallas kernels, fine_step(): pl.pallas_call(functools.partial(fine_kernel, profiles), out_shape=(jax.S...  0.93 us
    pallas_call x1, Pallas kernels, update_step(): pl.pallas_call(functools.partial(update_kernel, count), out_shape=jax.Sha...  0.92 us

profile of v5, /device:TPU:0, one launch (start us, length us, event | category | flops | bytes accessed | tf_op | source)
XLA Modules:
  0.0 38.8 jit_solution(7759678980329482525)
XLA Ops:
  0.0 0.0 copy-start.1
  0.0 0.0 copy-start.3
  0.0 0.9 %copy-done.3 = f32[1,32768]{1,0:T(1,128)S(1)} copy-done((f32[1,32768]{1,0:T(1,128)S(1)}, f32[1,32768]{1,0:T(1,128)}, u32[]{:S(2)}) %copy-start.3) | copy-done | bytes 131096
  1.0 0.0 copy-start.7
  1.0 0.7 %copy-done.7 = s32[6]{0:T(128)S(1)} copy-done((s32[6]{0:T(128)S(1)}, s32[6]{0:T(128)}, u32[]{:S(2)}) %copy-start.7) | copy-done | bytes 48
  1.6 0.0 copy-start.8
  1.6 0.7 %copy-done.8 = s32[8]{0:T(128)S(1)} copy-done((s32[8]{0:T(128)S(1)}, s32[8]{0:T(128)}, u32[]{:S(2)}) %copy-start.8) | copy-done | bytes 56
  2.3 0.1 columns.1
  2.4 14.4 %all_to_all.15 = f32[8,32,128]{2,1,0:T(8,128)S(1)} all-to-all(f32[8,32,128]{2,1,0:T(8,128)S(1)} %get-tuple-element.13), channel_id=1, replica_groups=mesh['bins'=8,'scans'=4] {'bins'}, dimensions={0} | all-to-all | bytes 262144 | tf_op jit(solution)/shard_map/all_to_all | solution.py:554
  16.8 0.0 copy-done.1
  16.8 0.0 copy-start
  16.8 0.4 coarse_dft.1
  17.2 0.0 copy-start.2
  17.2 0.0 copy-start.5
  17.2 0.0 copy-start.6
  17.2 10.4 %all_to_all.16 = f32[32,8,128]{2,1,0:T(8,128)S(1)} all-to-all(f32[32,8,128]{2,1,0:T(8,128)S(1)} %bitcast.18), channel_id=1, replica_groups=mesh['bins'=8,'scans'=4] {'bins','scans'}, dimensions={0} | all-to-all | bytes 262144 | tf_op jit(solution)/shard_map/all_to_all | solution.py:554
  27.6 0.0 copy-done
  27.6 0.0 copy-done.2
  27.6 0.0 copy-done.5
  27.6 0.0 copy-done.6
  27.7 0.9 %fine_dft.1 = (f32[8,16,128]{2,1,0:T(8,128)S(1)}, f32[64,128]{1,0:T(8,128)S(1)}) custom-call(f32[256,128]{1,0:T(8,128)S(1)} %bitcast.14, f32[16,8,128]{2,1,0:T(8,128)S(1)} %get-tuple-element.15.turn_ref, s32[1,512]{1,0:T(1,128)S(1)} %get-tuple-element.16.wanted_ref, s32[64,128]{1,0:T(8,128)S(1)} %get-tuple-element.17.band_ref, f32[32,128]{1,0:T(8,128)S(1)} %copy-done.6, ...), custom_call_target="tpu_custom_call" | custom-call | tf_op jit(solution)/shard_map/fine_dft/pallas_call | solution.py:410
  28.6 0.0 copy-start.4
  28.6 9.2 %all_to_all.17 = f32[32,4,128]{2,1,0:T(4,128)S(1)} all-to-all(f32[32,4,128]{2,1,0:T(4,128)S(1)} %bitcast.19), channel_id=1, replica_groups=mesh['bins'=8,'scans'=4] {'bins','scans'}, dimensions={0} | all-to-all | bytes 131072 | tf_op jit(solution)/shard_map/all_to_all | solution.py:554
  37.9 0.0 copy-done.4
  37.9 0.9 %state_update.1 = f32[64,128]{1,0:T(8,128)} custom-call(f32[128,128]{1,0:T(8,128)S(1)} %bitcast.15, bf16[336,128]{1,0:T(8,128)(2,1)S(1)} %copy-done.4, f32[64,128]{1,0:T(8,128)S(1)} %get-tuple-element.19.moved_ref, s32[1,128]{1,0:T(1,128)S(1)} %get-tuple-element.20.band_ref), custom_call_target="tpu_custom_call" | custom-call | tf_op jit(solution)/shard_map/state_update/pallas_call | solution.py:524
Async XLA Ops:
  0.0 16.8 %copy-start.1 = (bf16[256,512]{1,0:T(8,128)(2,1)S(1)}, bf16[256,512]{1,0:T(8,128)(2,1)}, u32[]{:S(2)}) copy-start(bf16[256,512]{1,0:T(8,128)(2,1)} %constant.8.clone.table_ref) | copy-start | bytes 786436
  0.0 0.9 %copy-start.3 = (f32[1,32768]{1,0:T(1,128)S(1)}, f32[1,32768]{1,0:T(1,128)}, u32[]{:S(2)}) copy-start(f32[1,32768]{1,0:T(1,128)} %param.9) | copy-start | bytes 393220
  1.0 0.7 %copy-start.7 = (s32[6]{0:T(128)S(1)}, s32[6]{0:T(128)}, u32[]{:S(2)}) copy-start(s32[6]{0:T(128)} %param.10) | copy-start | bytes 76
  1.6 0.7 %copy-start.8 = (s32[8]{0:T(128)S(1)}, s32[8]{0:T(128)}, u32[]{:S(2)}) copy-start(s32[8]{0:T(128)} %param.11) | copy-start | bytes 100
  16.8 10.8 %copy-start = (bf16[304,512]{1,0:T(8,128)(2,1)S(1)}, bf16[304,512]{1,0:T(8,128)(2,1)}, u32[]{:S(2)}) copy-start(bf16[304,512]{1,0:T(8,128)(2,1)} %constant.10.clone.table_ref) | copy-start | bytes 933892
  17.2 10.5 %copy-start.2 = (f32[5,64,64]{2,1,0:T(8,128)S(1)}, f32[5,64,64]{2,1,0:T(8,128)}, u32[]{:S(2)}) copy-start(f32[5,64,64]{2,1,0:T(8,128)} %param.12) | copy-start | bytes 245764
  17.2 10.4 %copy-start.5 = (f32[64,1,128]{2,1,0:T(1,128)S(1)}, f32[64,1,128]{2,1,0:T(1,128)}, u32[]{:S(2)}) copy-start(f32[64,1,128]{2,1,0:T(1,128)} %param.13) | copy-start | bytes 98308
  17.2 10.4 %copy-start.6 = (f32[32,128]{1,0:T(8,128)S(1)}, f32[32,128]{1,0:T(8,128)}, u32[]{:S(2)}) copy-start(f32[32,128]{1,0:T(8,128)} %constant.9.clone.turns_ref) | copy-start | bytes 49156
  28.6 9.3 %copy-start.4 = (bf16[336,128]{1,0:T(8,128)(2,1)S(1)}, bf16[336,128]{1,0:T(8,128)(2,1)}, u32[]{:S(2)}) copy-start(bf16[336,128]{1,0:T(8,128)(2,1)} %constant.11.clone.pool_ref) | copy-start | bytes 258052

commit v6 on v5

--- a/solution.py
+++ b/solution.py
@@ -66,26 +66,51 @@
 
 
 def columns_kernel(
-    x_ref, edges_ref, counts_ref, out_ref, wanted_ref, lane_band_ref, row_band_ref
+    order,
+    x_hbm,
+    edges_hbm,
+    counts_hbm,
+    out_ref,
+    turn_ref,
+    wanted_ref,
+    lane_band_ref,
+    row_band_ref,
+    x_ref,
+    edges_ref,
+    counts_ref,
+    copied,
 ):
     groups, rows, _ = out_ref.shape
     capacity = row_band_ref.shape[0]
+    copies = [
+        pltpu.make_async_copy(source, target, copied.at[at])
+        for at, (source, target) in enumerate(
+            ((x_hbm, x_ref), (edges_hbm, edges_ref), (counts_hbm, counts_ref))
+        )
+    ]
+    for copy in copies:
+        copy.start()
+    row, lane = iotas((8, LANES))
+    own = lax.axis_index("bins")
+    own_share = own * lax.axis_size("scans") + lax.axis_index("scans")
+    k_index = 8 * own_share + 4 * (lane >> 6) + (row & 3)
+    for c in range(groups):
+        phase = ((c * HALF + (lane & (HALF - 1))) * k_index) & (order - 1)
+        turn_ref[2 * c], turn_ref[2 * c + 1] = unit_turn(phase, order)
+    for copy in copies:
+        copy.wait()
     low_lanes = iotas((rows, LANES))[1] < HALF
     for pair in range(groups // 2):
         even = x_ref[pl.ds(pair, rows, stride=groups), :]
         odd = x_ref[pl.ds(groups // 2 + pair, rows, stride=groups), :]
         out_ref[2 * pair] = jnp.where(low_lanes, even, pltpu.roll(odd, HALF, 1))
         out_ref[2 * pair + 1] = jnp.where(low_lanes, pltpu.roll(even, HALF, 1), odd)
-    own = lax.axis_index("bins")
-    counts = [
-        jnp.broadcast_to(counts_ref[:, owner : owner + 1], (1, LANES)) for owner in range(groups)
-    ]
     lane = iotas((1, LANES))[1]
-    start = jnp.zeros((1, LANES), jnp.int32)
-    own_start, own_count = start, start
+    rank = lane & (HALF - 1)
+    start, own_start, own_count = jnp.int32(0), jnp.int32(0), jnp.int32(0)
     wanted = []
-    for owner, count in enumerate(counts):
-        rank = lane & (HALF - 1)
+    for owner in range(groups):
+        count = counts_ref[owner]
         wanted.append(jnp.where(rank < count, start + rank, -1))
         own_start = jnp.where(own == owner, start, own_start)
         own_count = jnp.where(own == owner, count, own_count)
@@ -94,33 +119,39 @@
         wanted_ref[:, pair * LANES : (pair + 1) * LANES] = jnp.where(
             lane < HALF, wanted[2 * pair], wanted[2 * pair + 1]
         )
-    edges = [jnp.broadcast_to(edges_ref[:, at : at + 1], (1, LANES)) for at in range(1, NCLASS)]
     for ref, slot in (
         (lane_band_ref, lane & (capacity - 1)),
         (row_band_ref, iotas((capacity, LANES))[0]),
     ):
         band = jnp.zeros_like(slot)
-        for edge in edges:
-            band = band + jnp.where(slot + own_start >= edge, 1, 0)
+        for at in range(1, NCLASS):
+            band = band + jnp.where(slot >= edges_ref[at] - own_start, 1, 0)
         ref[...] = jnp.where(slot < own_count, band, -1)
 
 
-def columns_step(profile, band_edges, owner_counts, capacity):
+def columns_step(profile, band_edges, owner_counts, capacity, order):
     groups = owner_counts.shape[0]
     rows = profile.shape[0] // (groups * LANES)
     return pl.pallas_call(
-        columns_kernel,
+        functools.partial(columns_kernel, order),
         out_shape=(
             jax.ShapeDtypeStruct((groups, rows, LANES), F32),
+            jax.ShapeDtypeStruct((2 * groups, 8, LANES), F32),
             jax.ShapeDtypeStruct((1, groups * capacity), jnp.int32),
             jax.ShapeDtypeStruct((1, LANES), jnp.int32),
             jax.ShapeDtypeStruct((capacity, LANES), jnp.int32),
         ),
-        in_specs=[VMEM] * 3,
-        out_specs=(VMEM,) * 4,
+        in_specs=[pl.BlockSpec(memory_space=pltpu.HBM)] * 3,
+        out_specs=(VMEM,) * 5,
+        scratch_shapes=[
+            pltpu.VMEM((groups * rows, LANES), F32),
+            pltpu.SMEM(band_edges.shape, jnp.int32),
+            pltpu.SMEM(owner_counts.shape, jnp.int32),
+            pltpu.SemaphoreType.DMA((3,)),
+        ],
         compiler_params=PARAMS,
         name="columns",
-    )(profile.reshape(-1, LANES), band_edges.reshape(1, -1), owner_counts.reshape(1, -1))
+    )(profile.reshape(-1, LANES), band_edges, owner_counts)
 
 
 def coarse_table(coarse):
@@ -134,7 +165,7 @@
     return np.concatenate(two_terms(parts.reshape(half, half)), axis=1)
 
 
-def coarse_kernel(groups, shares, x_ref, table_ref, out_ref, turn_ref):
+def coarse_kernel(shares, x_ref, table_ref, out_ref):
     half = x_ref.shape[0]
     quarter = half // 2
     row, lane = iotas((8, LANES))
@@ -171,24 +202,15 @@
         imag = even_imag + odd_imag * cosine - odd_real * sine
         out_ref[pl.ds(8 * first, 8, stride=2), :] = real
         out_ref[pl.ds(8 * first + 1, 8, stride=2), :] = imag
-    own = lax.axis_index("bins") * lax.axis_size("scans") + lax.axis_index("scans")
-    k_index = 8 * own + 4 * (lane >> 6) + (row & 3)
-    order = 2 * half * groups * HALF
-    for c in range(groups):
-        phase = ((c * HALF + (lane & (HALF - 1))) * k_index) & (order - 1)
-        turn_ref[2 * c], turn_ref[2 * c + 1] = unit_turn(phase, order)
-
-
-def coarse_step(columns, groups, shares):
+
+
+def coarse_step(columns, shares):
     half = columns.shape[0]
     return pl.pallas_call(
-        functools.partial(coarse_kernel, groups, shares),
-        out_shape=(
-            jax.ShapeDtypeStruct((half, LANES), F32),
-            jax.ShapeDtypeStruct((2 * groups, 8, LANES), F32),
-        ),
+        functools.partial(coarse_kernel, shares),
+        out_shape=jax.ShapeDtypeStruct((half, LANES), F32),
         in_specs=[VMEM] * 2,
-        out_specs=(VMEM,) * 2,
+        out_specs=VMEM,
         compiler_params=PARAMS,
         name="coarse_dft",
     )(columns, jnp.asarray(coarse_table(2 * half)))
@@ -563,11 +585,11 @@
     count = prof_rows * scans * TILE
     state = prev_state.reshape(capacity, 2 * STATES)
     if groups == 8 and scans == 4 and coarse == 16 * shares and capacity == HALF:
-        columns, wanted, lane_band, row_band = columns_step(
-            profiles.reshape(length), band_edges, owner_counts, capacity
+        columns, turn, wanted, lane_band, row_band = columns_step(
+            profiles.reshape(length), band_edges, owner_counts, capacity, length * groups
         )
         columns = exchanged(columns, "bins").reshape(coarse // 2, LANES)
-        blocks, turn = coarse_step(columns, groups, shares)
+        blocks = coarse_step(columns, shares)
         blocks = exchanged(blocks.reshape(shares, 8, LANES), ("bins", "scans"))
         payload, moved = fine_step(
             blocks.reshape(8 * shares, LANES),

time: 39 us -> 39.7 us (1.018)
  Pallas kernels: 2.34 us -> 3.03 us
    pallas_call x2, Pallas kernels: 0.48 us -> 1.17 us  [the longest x1 0.81 us: columns_step(): pl.pallas_call(functools.partial(columns_kernel, order), out_shape=(jax.S...]
where the time goes in v6:
time: 39.7 us; the launch traced here: 39.5 us
  blocking collectives  34.1 us (86%)
  Pallas kernels  3.03 us (8%)
  local copies, waits for them, and re-layouts  2.3 us (6%)
    all_to_all x3, blocking collectives, exchanged(): return lax.all_to_all(values, axes, split_axis=0, concat_axis=0, tiled=True)  34.1 us
    unnamed x18, local copies, waits for them, and re-layouts  2.3 us
    pallas_call x1, Pallas kernels, fine_step(): pl.pallas_call(functools.partial(fine_kernel, profiles), out_shape=(jax.S...  0.94 us
    pallas_call x1, Pallas kernels, update_step(): pl.pallas_call(functools.partial(update_kernel, count), out_shape=jax.Sha...  0.92 us
    pallas_call x1, Pallas kernels, columns_step(): pl.pallas_call(functools.partial(columns_kernel, order), out_shape=(jax.S...  0.81 us

profile of v6, /device:TPU:0, one launch (start us, length us, event | category | flops | bytes accessed | tf_op | source)
XLA Modules:
  0.0 39.5 jit_solution(12016033838703909070)
XLA Ops:
  0.0 0.0 copy-start.1
  0.0 0.0 copy-start.3
  0.0 0.9 %copy-done.3 = f32[1,32768]{1,0:T(1,128)S(1)} copy-done((f32[1,32768]{1,0:T(1,128)S(1)}, f32[1,32768]{1,0:T(1,128)}, u32[]{:S(2)}) %copy-start.3) | copy-done | bytes 131096
  1.0 0.0 copy-start.7
  1.0 0.7 %copy-done.7 = s32[6]{0:T(128)S(1)} copy-done((s32[6]{0:T(128)S(1)}, s32[6]{0:T(128)}, u32[]{:S(2)}) %copy-start.7) | copy-done | bytes 48
  1.6 0.0 copy-start.8
  1.6 0.7 %copy-done.8 = s32[8]{0:T(128)S(1)} copy-done((s32[8]{0:T(128)S(1)}, s32[8]{0:T(128)}, u32[]{:S(2)}) %copy-start.8) | copy-done | bytes 56
  2.3 0.8 %columns.1 = (f32[8,32,128]{2,1,0:T(8,128)S(1)}, f32[16,8,128]{2,1,0:T(8,128)S(1)}, s32[1,512]{1,0:T(1,128)S(1)}, s32[1,128]{1,0:T(1,128)S(1)}, s32[64,128]{1,0:T(8,128)S(1)}) custom-call(f32[256,128]{1,0:T(8,128)S(1)} %bitcast.16, s32[6]{0:T(128)S(1)} %copy-done.7, s32[8]{0:T(128)S(1)} %copy-done.8), custom_call_target="tpu_custom_call" | custom-call | tf_op jit(solution)/shard_map/columns/pallas_call | solution.py:135
  3.1 14.4 %all_to_all.15 = f32[8,32,128]{2,1,0:T(8,128)S(1)} all-to-all(f32[8,32,128]{2,1,0:T(8,128)S(1)} %get-tuple-element.12), channel_id=1, replica_groups=mesh['bins'=8,'scans'=4] {'bins'}, dimensions={0} | all-to-all | bytes 262144 | tf_op jit(solution)/shard_map/all_to_all | solution.py:576
  17.5 0.0 copy-done.1
  17.5 0.0 copy-start
  17.5 0.4 coarse_dft.1
  17.9 0.0 copy-start.2
  17.9 0.0 copy-start.5
  17.9 0.0 copy-start.6
  17.9 10.4 %all_to_all.16 = f32[32,8,128]{2,1,0:T(8,128)S(1)} all-to-all(f32[32,8,128]{2,1,0:T(8,128)S(1)} %bitcast.13), channel_id=1, replica_groups=mesh['bins'=8,'scans'=4] {'bins','scans'}, dimensions={0} | all-to-all | bytes 262144 | tf_op jit(solution)/shard_map/all_to_all | solution.py:576
  28.3 0.0 copy-done
  28.3 0.0 copy-done.2
  28.3 0.0 copy-done.5
  28.3 0.0 copy-done.6
  28.3 0.9 %fine_dft.1 = (f32[8,16,128]{2,1,0:T(8,128)S(1)}, f32[64,128]{1,0:T(8,128)S(1)}) custom-call(f32[256,128]{1,0:T(8,128)S(1)} %bitcast.11, f32[16,8,128]{2,1,0:T(8,128)S(1)} %get-tuple-element.13.turn_ref, s32[1,512]{1,0:T(1,128)S(1)} %get-tuple-element.14.wanted_ref, s32[64,128]{1,0:T(8,128)S(1)} %get-tuple-element.15.band_ref, f32[32,128]{1,0:T(8,128)S(1)} %copy-done.6, ...), custom_call_target="tpu_custom_call" | custom-call | tf_op jit(solution)/shard_map/fine_dft/pallas_call | solution.py:432
  29.3 0.0 copy-start.4
  29.3 9.2 %all_to_all.17 = f32[32,4,128]{2,1,0:T(4,128)S(1)} all-to-all(f32[32,4,128]{2,1,0:T(4,128)S(1)} %bitcast.17), channel_id=1, replica_groups=mesh['bins'=8,'scans'=4] {'bins','scans'}, dimensions={0} | all-to-all | bytes 131072 | tf_op jit(solution)/shard_map/all_to_all | solution.py:576
  38.6 0.0 copy-done.4
  38.6 0.9 %state_update.1 = f32[64,128]{1,0:T(8,128)} custom-call(f32[128,128]{1,0:T(8,128)S(1)} %bitcast.14, bf16[336,128]{1,0:T(8,128)(2,1)S(1)} %copy-done.4, f32[64,128]{1,0:T(8,128)S(1)} %get-tuple-element.17.moved_ref, s32[1,128]{1,0:T(1,128)S(1)} %get-tuple-element.18.band_ref), custom_call_target="tpu_custom_call" | custom-call | tf_op jit(solution)/shard_map/state_update/pallas_call | solution.py:546
Async XLA Ops:
  0.0 17.5 %copy-start.1 = (bf16[256,512]{1,0:T(8,128)(2,1)S(1)}, bf16[256,512]{1,0:T(8,128)(2,1)}, u32[]{:S(2)}) copy-start(bf16[256,512]{1,0:T(8,128)(2,1)} %constant.8.clone.table_ref) | copy-start | bytes 786436
  0.0 0.9 %copy-start.3 = (f32[1,32768]{1,0:T(1,128)S(1)}, f32[1,32768]{1,0:T(1,128)}, u32[]{:S(2)}) copy-start(f32[1,32768]{1,0:T(1,128)} %param.9) | copy-start | bytes 393220
  1.0 0.7 %copy-start.7 = (s32[6]{0:T(128)S(1)}, s32[6]{0:T(128)}, u32[]{:S(2)}) copy-start(s32[6]{0:T(128)} %edges_hbm.1) | copy-start | bytes 76
  1.6 0.7 %copy-start.8 = (s32[8]{0:T(128)S(1)}, s32[8]{0:T(128)}, u32[]{:S(2)}) copy-start(s32[8]{0:T(128)} %counts_hbm.1) | copy-start | bytes 100
  17.5 10.8 %copy-start = (bf16[304,512]{1,0:T(8,128)(2,1)S(1)}, bf16[304,512]{1,0:T(8,128)(2,1)}, u32[]{:S(2)}) copy-start(bf16[304,512]{1,0:T(8,128)(2,1)} %constant.10.clone.table_ref) | copy-start | bytes 933892
  17.9 10.5 %copy-start.2 = (f32[5,64,64]{2,1,0:T(8,128)S(1)}, f32[5,64,64]{2,1,0:T(8,128)}, u32[]{:S(2)}) copy-start(f32[5,64,64]{2,1,0:T(8,128)} %param.12) | copy-start | bytes 245764
  17.9 10.4 %copy-start.5 = (f32[64,1,128]{2,1,0:T(1,128)S(1)}, f32[64,1,128]{2,1,0:T(1,128)}, u32[]{:S(2)}) copy-start(f32[64,1,128]{2,1,0:T(1,128)} %param.13) | copy-start | bytes 98308
  17.9 10.4 %copy-start.6 = (f32[32,128]{1,0:T(8,128)S(1)}, f32[32,128]{1,0:T(8,128)}, u32[]{:S(2)}) copy-start(f32[32,128]{1,0:T(8,128)} %constant.9.clone.turns_ref) | copy-start | bytes 49156
  29.3 9.3 %copy-start.4 = (bf16[336,128]{1,0:T(8,128)(2,1)S(1)}, bf16[336,128]{1,0:T(8,128)(2,1)}, u32[]{:S(2)}) copy-start(bf16[336,128]{1,0:T(8,128)(2,1)} %constant.11.clone.pool_ref) | copy-start | bytes 258052

commit v7 on v5

--- a/solution.py
+++ b/solution.py
@@ -42,6 +42,7 @@
 
 VMEM = pl.BlockSpec(memory_space=pltpu.VMEM)
 PARAMS = pltpu.CompilerParams(vmem_limit_bytes=32 << 20)
+COST = pl.CostEstimate(flops=1 << 30, bytes_accessed=1 << 24, transcendentals=0)
 
 
 KINDS = 4
@@ -65,27 +66,52 @@
     return [lax.broadcasted_iota(jnp.int32, shape, axis) for axis in range(len(shape))]
 
 
-def columns_kernel(
-    x_ref, edges_ref, counts_ref, out_ref, wanted_ref, lane_band_ref, row_band_ref
-):
+def columns_kernel(x_ref, out_ref):
     groups, rows, _ = out_ref.shape
-    capacity = row_band_ref.shape[0]
     low_lanes = iotas((rows, LANES))[1] < HALF
     for pair in range(groups // 2):
         even = x_ref[pl.ds(pair, rows, stride=groups), :]
         odd = x_ref[pl.ds(groups // 2 + pair, rows, stride=groups), :]
         out_ref[2 * pair] = jnp.where(low_lanes, even, pltpu.roll(odd, HALF, 1))
         out_ref[2 * pair + 1] = jnp.where(low_lanes, pltpu.roll(even, HALF, 1), odd)
+
+
+def columns_step(profile, groups):
+    rows = profile.shape[0] // (groups * LANES)
+    return pl.pallas_call(
+        columns_kernel,
+        out_shape=jax.ShapeDtypeStruct((groups, rows, LANES), F32),
+        in_specs=[VMEM],
+        out_specs=VMEM,
+        compiler_params=PARAMS,
+        cost_estimate=COST,
+        name="columns",
+    )(profile.reshape(-1, LANES))
+
+
+def coarse_table(coarse):
+    half, quarter = coarse // 2, coarse // 4
+    k_index = np.arange(quarter)
+    a_index = np.concatenate([np.arange(0, half, 2), np.arange(1, half, 2)])
+    real, imag = unit_root(half, k_index[:, None] * a_index[None, :])
+    imag[0] = 1
+    parts = [part.reshape(quarter // 16, 2, 2, 1, 4, half) for part in (real, imag)]
+    parts = np.concatenate(parts, axis=3).transpose(0, 2, 3, 1, 4, 5)
+    return np.concatenate(two_terms(parts.reshape(half, half)), axis=1)
+
+
+def slot_bands(edges_ref, counts_ref, wanted_ref, lane_band_ref, row_band_ref):
+    groups, capacity = counts_ref.shape[1], row_band_ref.shape[0]
     own = lax.axis_index("bins")
     counts = [
         jnp.broadcast_to(counts_ref[:, owner : owner + 1], (1, LANES)) for owner in range(groups)
     ]
     lane = iotas((1, LANES))[1]
+    rank = lane & (capacity - 1)
     start = jnp.zeros((1, LANES), jnp.int32)
     own_start, own_count = start, start
     wanted = []
     for owner, count in enumerate(counts):
-        rank = lane & (HALF - 1)
         wanted.append(jnp.where(rank < count, start + rank, -1))
         own_start = jnp.where(own == owner, start, own_start)
         own_count = jnp.where(own == owner, count, own_count)
@@ -95,46 +121,26 @@
             lane < HALF, wanted[2 * pair], wanted[2 * pair + 1]
         )
     edges = [jnp.broadcast_to(edges_ref[:, at : at + 1], (1, LANES)) for at in range(1, NCLASS)]
-    for ref, slot in (
-        (lane_band_ref, lane & (capacity - 1)),
-        (row_band_ref, iotas((capacity, LANES))[0]),
-    ):
+    for ref, slot in ((lane_band_ref, rank), (row_band_ref, iotas((capacity, LANES))[0])):
         band = jnp.zeros_like(slot)
         for edge in edges:
             band = band + jnp.where(slot + own_start >= edge, 1, 0)
         ref[...] = jnp.where(slot < own_count, band, -1)
 
 
-def columns_step(profile, band_edges, owner_counts, capacity):
-    groups = owner_counts.shape[0]
-    rows = profile.shape[0] // (groups * LANES)
-    return pl.pallas_call(
-        columns_kernel,
-        out_shape=(
-            jax.ShapeDtypeStruct((groups, rows, LANES), F32),
-            jax.ShapeDtypeStruct((1, groups * capacity), jnp.int32),
-            jax.ShapeDtypeStruct((1, LANES), jnp.int32),
-            jax.ShapeDtypeStruct((capacity, LANES), jnp.int32),
-        ),
-        in_specs=[VMEM] * 3,
-        out_specs=(VMEM,) * 4,
-        compiler_params=PARAMS,
-        name="columns",
-    )(profile.reshape(-1, LANES), band_edges.reshape(1, -1), owner_counts.reshape(1, -1))
-
-
-def coarse_table(coarse):
-    half, quarter = coarse // 2, coarse // 4
-    k_index = np.arange(quarter)
-    a_index = np.concatenate([np.arange(0, half, 2), np.arange(1, half, 2)])
-    real, imag = unit_root(half, k_index[:, None] * a_index[None, :])
-    imag[0] = 1
-    parts = [part.reshape(quarter // 16, 2, 2, 1, 4, half) for part in (real, imag)]
-    parts = np.concatenate(parts, axis=3).transpose(0, 2, 3, 1, 4, 5)
-    return np.concatenate(two_terms(parts.reshape(half, half)), axis=1)
-
-
-def coarse_kernel(groups, shares, x_ref, table_ref, out_ref, turn_ref):
+def coarse_kernel(
+    groups,
+    shares,
+    x_ref,
+    table_ref,
+    edges_ref,
+    counts_ref,
+    out_ref,
+    turn_ref,
+    wanted_ref,
+    lane_band_ref,
+    row_band_ref,
+):
     half = x_ref.shape[0]
     quarter = half // 2
     row, lane = iotas((8, LANES))
@@ -177,21 +183,31 @@
     for c in range(groups):
         phase = ((c * HALF + (lane & (HALF - 1))) * k_index) & (order - 1)
         turn_ref[2 * c], turn_ref[2 * c + 1] = unit_turn(phase, order)
-
-
-def coarse_step(columns, groups, shares):
-    half = columns.shape[0]
+    slot_bands(edges_ref, counts_ref, wanted_ref, lane_band_ref, row_band_ref)
+
+
+def coarse_step(columns, band_edges, owner_counts, shares, capacity):
+    half, groups = columns.shape[0], owner_counts.shape[0]
     return pl.pallas_call(
         functools.partial(coarse_kernel, groups, shares),
         out_shape=(
             jax.ShapeDtypeStruct((half, LANES), F32),
             jax.ShapeDtypeStruct((2 * groups, 8, LANES), F32),
+            jax.ShapeDtypeStruct((1, groups * capacity), jnp.int32),
+            jax.ShapeDtypeStruct((1, LANES), jnp.int32),
+            jax.ShapeDtypeStruct((capacity, LANES), jnp.int32),
         ),
-        in_specs=[VMEM] * 2,
-        out_specs=(VMEM,) * 2,
+        in_specs=[VMEM] * 4,
+        out_specs=(VMEM,) * 5,
         compiler_params=PARAMS,
+        cost_estimate=COST,
         name="coarse_dft",
-    )(columns, jnp.asarray(coarse_table(2 * half)))
+    )(
+        columns,
+        jnp.asarray(coarse_table(2 * half)),
+        band_edges.reshape(1, -1),
+        owner_counts.reshape(1, -1),
+    )
 
 
 def coarse_step_general(columns, shares):
@@ -416,6 +432,7 @@
         in_specs=[VMEM] * 8,
         out_specs=(VMEM,) * 2,
         compiler_params=PARAMS,
+        cost_estimate=COST,
         name="fine_dft",
     )(
         arrived,
@@ -563,11 +580,10 @@
     count = prof_rows * scans * TILE
     state = prev_state.reshape(capacity, 2 * STATES)
     if groups == 8 and scans == 4 and coarse == 16 * shares and capacity == HALF:
-        columns, wanted, lane_band, row_band = columns_step(
-            profiles.reshape(length), band_edges, owner_counts, capacity
+        columns = exchanged(columns_step(profiles.reshape(length), groups), "bins")
+        blocks, turn, wanted, lane_band, row_band = coarse_step(
+            columns.reshape(coarse // 2, LANES), band_edges, owner_counts, shares, capacity
         )
-        columns = exchanged(columns, "bins").reshape(coarse // 2, LANES)
-        blocks, turn = coarse_step(columns, groups, shares)
         blocks = exchanged(blocks.reshape(shares, 8, LANES), ("bins", "scans"))
         payload, moved = fine_step(
             blocks.reshape(8 * shares, LANES),

time: 39 us -> 38.5 us (0.987)
  local copies, waits for them, and re-layouts: 2.3 us -> 1.62 us
    unnamed x18, local copies, waits for them, and re-layouts: 2.3 us -> 1.62 us
where the time goes in v7:
time: 38.5 us; the launch traced here: 38.2 us
  blocking collectives  34.2 us (89%)
  Pallas kernels  2.32 us (6%)
  local copies, waits for them, and re-layouts  1.62 us (4%)
    all_to_all x3, blocking collectives, exchanged(): return lax.all_to_all(values, axes, split_axis=0, concat_axis=0, tiled=True)  34.2 us
    unnamed x18, local copies, waits for them, and re-layouts  1.62 us
    pallas_call x1, Pallas kernels, fine_step(): pl.pallas_call(functools.partial(fine_kernel, profiles), out_shape=(jax.S...  0.93 us
    pallas_call x1, Pallas kernels, update_step(): pl.pallas_call(functools.partial(update_kernel, count), out_shape=jax.Sha...  0.93 us

profile of v7, /device:TPU:0, one launch (start us, length us, event | category | flops | bytes accessed | tf_op | source)
XLA Modules:
  0.0 38.2 jit_solution(6836909946288084775)
XLA Ops:
  0.0 0.0 copy-start.2
  0.0 0.9 %copy-done.2 = f32[1,32768]{1,0:T(1,128)S(1)} copy-done((f32[1,32768]{1,0:T(1,128)S(1)}, f32[1,32768]{1,0:T(1,128)}, u32[]{:S(2)}) %copy-start.2) | copy-done | bytes 131096
  0.9 0.1 columns.1
  1.0 0.0 copy-start.7
  1.0 14.6 %all_to_all.15 = f32[8,32,128]{2,1,0:T(8,128)S(1)} all-to-all(f32[8,32,128]{2,1,0:T(8,128)S(1)} %columns.1), channel_id=1, replica_groups=mesh['bins'=8,'scans'=4] {'bins'}, dimensions={0} | all-to-all | bytes 262144 | tf_op jit(solution)/shard_map/all_to_all | solution.py:571
  15.6 0.0 copy-start.4
  15.6 0.0 copy-start.5
  15.6 0.0 copy-done.7
  15.6 0.6 %copy-done.4 = s32[6]{0:T(128)S(1)} copy-done((s32[6]{0:T(128)S(1)}, s32[6]{0:T(128)}, u32[]{:S(2)}) %copy-start.4) | copy-done | bytes 48
  16.2 0.0 copy-done.5
  16.3 0.0 copy-start.6
  16.3 0.4 coarse_dft.1
  16.6 0.0 copy-start.1
  16.6 0.0 copy-start.3
  16.7 0.0 copy-start.8
  16.7 10.4 %all_to_all.16 = f32[32,8,128]{2,1,0:T(8,128)S(1)} all-to-all(f32[32,8,128]{2,1,0:T(8,128)S(1)} %bitcast.16), channel_id=1, replica_groups=mesh['bins'=8,'scans'=4] {'bins','scans'}, dimensions={0} | all-to-all | bytes 262144 | tf_op jit(solution)/shard_map/all_to_all | solution.py:571
  27.1 0.0 copy-done.6
  27.1 0.0 copy-done.1
  27.1 0.0 copy-done.3
  27.1 0.0 copy-done.8
  27.1 0.9 %fine_dft.1 = (f32[8,16,128]{2,1,0:T(8,128)S(1)}, f32[64,128]{1,0:T(8,128)S(1)}) custom-call(f32[256,128]{1,0:T(8,128)S(1)} %bitcast.14, f32[16,8,128]{2,1,0:T(8,128)S(1)} %get-tuple-element.13.turn_ref, s32[1,512]{1,0:T(1,128)S(1)} %get-tuple-element.14.wanted_ref, s32[64,128]{1,0:T(8,128)S(1)} %get-tuple-element.15.band_ref, f32[32,128]{1,0:T(8,128)S(1)} %copy-done.8, ...), custom_call_target="tpu_custom_call" | custom-call | flops 1073741824 | bytes 16777216 | tf_op jit(solution)/shard_map/fine_dft/pallas_call | solution.py:426
  28.0 0.0 copy-start
  28.1 9.2 %all_to_all.17 = f32[32,4,128]{2,1,0:T(4,128)S(1)} all-to-all(f32[32,4,128]{2,1,0:T(4,128)S(1)} %bitcast.17), channel_id=1, replica_groups=mesh['bins'=8,'scans'=4] {'bins','scans'}, dimensions={0} | all-to-all | bytes 131072 | tf_op jit(solution)/shard_map/all_to_all | solution.py:571
  37.3 0.0 copy-done
  37.3 0.9 %state_update.1 = f32[64,128]{1,0:T(8,128)} custom-call(f32[128,128]{1,0:T(8,128)S(1)} %bitcast.13, bf16[336,128]{1,0:T(8,128)(2,1)S(1)} %copy-done, f32[64,128]{1,0:T(8,128)S(1)} %get-tuple-element.17.moved_ref, s32[1,128]{1,0:T(1,128)S(1)} %get-tuple-element.18.band_ref), custom_call_target="tpu_custom_call" | custom-call | tf_op jit(solution)/shard_map/state_update/pallas_call | solution.py:541
Async XLA Ops:
  0.0 0.9 %copy-start.2 = (f32[1,32768]{1,0:T(1,128)S(1)}, f32[1,32768]{1,0:T(1,128)}, u32[]{:S(2)}) copy-start(f32[1,32768]{1,0:T(1,128)} %param.9) | copy-start | bytes 393220
  1.0 14.6 %copy-start.7 = (bf16[256,512]{1,0:T(8,128)(2,1)S(1)}, bf16[256,512]{1,0:T(8,128)(2,1)}, u32[]{:S(2)}) copy-start(bf16[256,512]{1,0:T(8,128)(2,1)} %constant.8.clone.table_ref) | copy-start | bytes 786436
  15.6 0.7 %copy-start.4 = (s32[6]{0:T(128)S(1)}, s32[6]{0:T(128)}, u32[]{:S(2)}) copy-start(s32[6]{0:T(128)} %param.10) | copy-start | bytes 76
  15.6 0.7 %copy-start.5 = (s32[8]{0:T(128)S(1)}, s32[8]{0:T(128)}, u32[]{:S(2)}) copy-start(s32[8]{0:T(128)} %param.11) | copy-start | bytes 100
  16.3 10.8 %copy-start.6 = (bf16[304,512]{1,0:T(8,128)(2,1)S(1)}, bf16[304,512]{1,0:T(8,128)(2,1)}, u32[]{:S(2)}) copy-start(bf16[304,512]{1,0:T(8,128)(2,1)} %constant.10.clone.table_ref) | copy-start | bytes 933892
  16.6 10.5 %copy-start.1 = (f32[5,64,64]{2,1,0:T(8,128)S(1)}, f32[5,64,64]{2,1,0:T(8,128)}, u32[]{:S(2)}) copy-start(f32[5,64,64]{2,1,0:T(8,128)} %param.12) | copy-start | bytes 245764
  16.6 10.4 %copy-start.3 = (f32[64,1,128]{2,1,0:T(1,128)S(1)}, f32[64,1,128]{2,1,0:T(1,128)}, u32[]{:S(2)}) copy-start(f32[64,1,128]{2,1,0:T(1,128)} %param.13) | copy-start | bytes 98308
  16.7 10.4 %copy-start.8 = (f32[32,128]{1,0:T(8,128)S(1)}, f32[32,128]{1,0:T(8,128)}, u32[]{:S(2)}) copy-start(f32[32,128]{1,0:T(8,128)} %constant.9.clone.turns_ref) | copy-start | bytes 49156
  28.0 9.3 %copy-start = (bf16[336,128]{1,0:T(8,128)(2,1)S(1)}, bf16[336,128]{1,0:T(8,128)(2,1)}, u32[]{:S(2)}) copy-start(bf16[336,128]{1,0:T(8,128)(2,1)} %constant.11.clone.pool_ref) | copy-start | bytes 258052

commit v8 on v7

--- a/solution.py
+++ b/solution.py
@@ -100,32 +100,32 @@
     return np.concatenate(two_terms(parts.reshape(half, half)), axis=1)
 
 
-def slot_bands(edges_ref, counts_ref, wanted_ref, lane_band_ref, row_band_ref):
-    groups, capacity = counts_ref.shape[1], row_band_ref.shape[0]
+def slot_tiles(counts_ref):
+    groups = counts_ref.shape[1]
     own = lax.axis_index("bins")
-    counts = [
-        jnp.broadcast_to(counts_ref[:, owner : owner + 1], (1, LANES)) for owner in range(groups)
-    ]
     lane = iotas((1, LANES))[1]
-    rank = lane & (capacity - 1)
+    rank = lane & (HALF - 1)
     start = jnp.zeros((1, LANES), jnp.int32)
     own_start, own_count = start, start
     wanted = []
-    for owner, count in enumerate(counts):
+    for owner in range(groups):
+        count = jnp.broadcast_to(counts_ref[:, owner : owner + 1], (1, LANES))
         wanted.append(jnp.where(rank < count, start + rank, -1))
         own_start = jnp.where(own == owner, start, own_start)
         own_count = jnp.where(own == owner, count, own_count)
         start = start + count
-    for pair in range(groups // 2):
-        wanted_ref[:, pair * LANES : (pair + 1) * LANES] = jnp.where(
-            lane < HALF, wanted[2 * pair], wanted[2 * pair + 1]
-        )
-    edges = [jnp.broadcast_to(edges_ref[:, at : at + 1], (1, LANES)) for at in range(1, NCLASS)]
-    for ref, slot in ((lane_band_ref, rank), (row_band_ref, iotas((capacity, LANES))[0])):
-        band = jnp.zeros_like(slot)
-        for edge in edges:
-            band = band + jnp.where(slot + own_start >= edge, 1, 0)
-        ref[...] = jnp.where(slot < own_count, band, -1)
+    wanted = [
+        jnp.where(lane < HALF, wanted[2 * pair], wanted[2 * pair + 1]) for pair in range(groups // 2)
+    ]
+    return jnp.concatenate(wanted, axis=1), own_start, own_count
+
+
+def bands(slot, start, count, edges_ref):
+    band = jnp.zeros_like(slot)
+    for at in range(1, NCLASS):
+        edge = jnp.broadcast_to(edges_ref[:, at : at + 1], (1, LANES))
+        band = band + jnp.where(slot + start >= edge, 1, 0)
+    return jnp.where(slot < count, band, -1)
 
 
 def coarse_kernel(
@@ -138,8 +138,7 @@
     out_ref,
     turn_ref,
     wanted_ref,
-    lane_band_ref,
-    row_band_ref,
+    band_ref,
 ):
     half = x_ref.shape[0]
     quarter = half // 2
@@ -183,7 +182,8 @@
     for c in range(groups):
         phase = ((c * HALF + (lane & (HALF - 1))) * k_index) & (order - 1)
         turn_ref[2 * c], turn_ref[2 * c + 1] = unit_turn(phase, order)
-    slot_bands(edges_ref, counts_ref, wanted_ref, lane_band_ref, row_band_ref)
+    wanted_ref[...], start, count = slot_tiles(counts_ref)
+    band_ref[...] = bands(iotas(band_ref.shape)[0], start, count, edges_ref)
 
 
 def coarse_step(columns, band_edges, owner_counts, shares, capacity):
@@ -194,11 +194,10 @@
             jax.ShapeDtypeStruct((half, LANES), F32),
             jax.ShapeDtypeStruct((2 * groups, 8, LANES), F32),
             jax.ShapeDtypeStruct((1, groups * capacity), jnp.int32),
-            jax.ShapeDtypeStruct((1, LANES), jnp.int32),
             jax.ShapeDtypeStruct((capacity, LANES), jnp.int32),
         ),
         in_specs=[VMEM] * 4,
-        out_specs=(VMEM,) * 5,
+        out_specs=(VMEM,) * 4,
         compiler_params=PARAMS,
         cost_estimate=COST,
         name="coarse_dft",
@@ -518,8 +517,9 @@
     return pool.reshape(-1, shares * KINDS).astype(BF16)
 
 
-def update_kernel(count, x_ref, pool_ref, moved_ref, band_ref, out_ref):
-    band = band_ref[...]
+def update_kernel(count, x_ref, pool_ref, moved_ref, edges_ref, counts_ref, out_ref):
+    _, own_start, own_count = slot_tiles(counts_ref)
+    band = bands(iotas((1, LANES))[1] & (HALF - 1), own_start, own_count, edges_ref)
     sums = dot(pool_ref[...], jnp.concatenate(split_two(x_ref[...]), axis=1))
     sums = sums[:, :LANES] + sums[:, LANES:]
     power = sums[NCLASS * STATES : NCLASS * STATES + 1] * (1.0 / count)
@@ -536,16 +536,22 @@
     out_ref[...] = moved_ref[...] + measured
 
 
-def update_step(arrived, moved, band, coarse, count):
+def update_step(arrived, moved, band_edges, owner_counts, coarse, count):
     shares = arrived.shape[0]
     return pl.pallas_call(
         functools.partial(update_kernel, count),
         out_shape=jax.ShapeDtypeStruct(moved.shape, F32),
-        in_specs=[VMEM] * 4,
+        in_specs=[VMEM] * 5,
         out_specs=VMEM,
         compiler_params=PARAMS,
         name="state_update",
-    )(arrived.reshape(shares * KINDS, LANES), jnp.asarray(pool_table(shares, coarse)), moved, band)
+    )(
+        arrived.reshape(shares * KINDS, LANES),
+        jnp.asarray(pool_table(shares, coarse)),
+        moved,
+        band_edges.reshape(1, -1),
+        owner_counts.reshape(1, -1),
+    )
 
 
 def state_step_general(band_edges, owner_counts, dynamics, state):
@@ -564,7 +570,7 @@
     )
     parts = state.reshape(capacity, 2, STATES)
     moved = jnp.einsum("rij,rcj->rci", picked, parts, precision=HIGHEST)
-    return moved.reshape(state.shape), jnp.tile(band, 2)[None, :]
+    return moved.reshape(state.shape)
 
 
 def exchanged(values, axes):
@@ -581,7 +587,7 @@
     state = prev_state.reshape(capacity, 2 * STATES)
     if groups == 8 and scans == 4 and coarse == 16 * shares and capacity == HALF:
         columns = exchanged(columns_step(profiles.reshape(length), groups), "bins")
-        blocks, turn, wanted, lane_band, row_band = coarse_step(
+        blocks, turn, wanted, band = coarse_step(
             columns.reshape(coarse // 2, LANES), band_edges, owner_counts, shares, capacity
         )
         blocks = exchanged(blocks.reshape(shares, 8, LANES), ("bins", "scans"))
@@ -589,7 +595,7 @@
             blocks.reshape(8 * shares, LANES),
             turn,
             wanted,
-            row_band,
+            band,
             dynamics,
             state,
             scans,
@@ -597,14 +603,14 @@
         )
         arrived = exchanged(payload, ("bins", "scans"))
     else:
-        moved, lane_band = state_step_general(band_edges, owner_counts, dynamics, state)
+        moved = state_step_general(band_edges, owner_counts, dynamics, state)
         columns = profiles.reshape(coarse // groups, groups, HALF).transpose(1, 0, 2)
         columns = exchanged(columns, "bins").reshape(coarse, HALF)
         blocks = exchanged(coarse_step_general(columns, groups), "bins")
         arrived = exchanged(fine_step_general(blocks, owner_counts, capacity), "bins")
         power = lax.psum(arrived[:, 3:], "scans")
         arrived = jnp.concatenate([arrived[:, :3], power], axis=1)
-    updated = update_step(arrived, moved, lane_band, coarse, count)
+    updated = update_step(arrived, moved, band_edges, owner_counts, coarse, count)
     return updated.reshape(prev_state.shape)
 
 

time: 38.5 us -> 38.5 us (level)
  no operation moved by 1% of the time
where the time goes in v8:
time: 38.5 us; the launch traced here: 38.2 us
  blocking collectives  34.2 us (89%)
  Pallas kernels  2.32 us (6%)
  local copies, waits for them, and re-layouts  1.62 us (4%)
    all_to_all x3, blocking collectives, exchanged(): return lax.all_to_all(values, axes, split_axis=0, concat_axis=0, tiled=True)  34.2 us
    unnamed x18, local copies, waits for them, and re-layouts  1.62 us
    pallas_call x1, Pallas kernels, fine_step(): pl.pallas_call(functools.partial(fine_kernel, profiles), out_shape=(jax.S...  0.93 us
    pallas_call x1, Pallas kernels, update_step(): pl.pallas_call(functools.partial(update_kernel, count), out_shape=jax.Sha...  0.93 us

profile of v8, /device:TPU:0, one launch (start us, length us, event | category | flops | bytes accessed | tf_op | source)
XLA Modules:
  0.0 38.2 jit_solution(6547359427242392813)
XLA Ops:
  0.0 0.0 copy-start.4
  0.0 0.9 %copy-done.4 = f32[1,32768]{1,0:T(1,128)S(1)} copy-done((f32[1,32768]{1,0:T(1,128)S(1)}, f32[1,32768]{1,0:T(1,128)}, u32[]{:S(2)}) %copy-start.4) | copy-done | bytes 131096
  0.9 0.1 columns.1
  1.0 0.0 copy-start.7
  1.0 14.6 %all_to_all.15 = f32[8,32,128]{2,1,0:T(8,128)S(1)} all-to-all(f32[8,32,128]{2,1,0:T(8,128)S(1)} %columns.1), channel_id=1, replica_groups=mesh['bins'=8,'scans'=4] {'bins'}, dimensions={0} | all-to-all | bytes 262144 | tf_op jit(solution)/shard_map/all_to_all | solution.py:577
  15.6 0.0 copy-start.1
  15.6 0.0 copy-start.2
  15.6 0.0 copy-done.7
  15.6 0.6 %copy-done.1 = s32[6]{0:T(128)S(1)} copy-done((s32[6]{0:T(128)S(1)}, s32[6]{0:T(128)}, u32[]{:S(2)}) %copy-start.1) | copy-done | bytes 48
  16.2 0.0 copy-done.2
  16.3 0.0 copy-start.6
  16.3 0.4 coarse_dft.1
  16.6 0.0 copy-start.3
  16.6 0.0 copy-start.5
  16.6 0.0 copy-start.8
  16.7 10.4 %all_to_all.16 = f32[32,8,128]{2,1,0:T(8,128)S(1)} all-to-all(f32[32,8,128]{2,1,0:T(8,128)S(1)} %bitcast.16), channel_id=1, replica_groups=mesh['bins'=8,'scans'=4] {'bins','scans'}, dimensions={0} | all-to-all | bytes 262144 | tf_op jit(solution)/shard_map/all_to_all | solution.py:577
  27.1 0.0 copy-done.6
  27.1 0.0 copy-done.3
  27.1 0.0 copy-done.5
  27.1 0.0 copy-done.8
  27.1 0.9 %fine_dft.1 = (f32[8,16,128]{2,1,0:T(8,128)S(1)}, f32[64,128]{1,0:T(8,128)S(1)}) custom-call(f32[256,128]{1,0:T(8,128)S(1)} %bitcast.14, f32[16,8,128]{2,1,0:T(8,128)S(1)} %get-tuple-element.12.turn_ref, s32[1,512]{1,0:T(1,128)S(1)} %get-tuple-element.13.wanted_ref, s32[64,128]{1,0:T(8,128)S(1)} %get-tuple-element.14.band_ref, f32[32,128]{1,0:T(8,128)S(1)} %copy-done.8, ...), custom_call_target="tpu_custom_call" | custom-call | flops 1073741824 | bytes 16777216 | tf_op jit(solution)/shard_map/fine_dft/pallas_call | solution.py:425
  28.0 0.0 copy-start
  28.1 9.2 %all_to_all.17 = f32[32,4,128]{2,1,0:T(4,128)S(1)} all-to-all(f32[32,4,128]{2,1,0:T(4,128)S(1)} %bitcast.17), channel_id=1, replica_groups=mesh['bins'=8,'scans'=4] {'bins','scans'}, dimensions={0} | all-to-all | bytes 131072 | tf_op jit(solution)/shard_map/all_to_all | solution.py:577
  37.3 0.0 copy-done
  37.3 0.9 %state_update.1 = f32[64,128]{1,0:T(8,128)} custom-call(f32[128,128]{1,0:T(8,128)S(1)} %bitcast.13, bf16[336,128]{1,0:T(8,128)(2,1)S(1)} %copy-done, f32[64,128]{1,0:T(8,128)S(1)} %get-tuple-element.16.moved_ref, s32[1,6]{1,0:T(1,128)S(1)} %bitcast.19, s32[1,8]{1,0:T(1,128)S(1)} %bitcast.21), custom_call_target="tpu_custom_call" | custom-call | tf_op jit(solution)/shard_map/state_update/pallas_call | solution.py:541
Async XLA Ops:
  0.0 0.9 %copy-start.4 = (f32[1,32768]{1,0:T(1,128)S(1)}, f32[1,32768]{1,0:T(1,128)}, u32[]{:S(2)}) copy-start(f32[1,32768]{1,0:T(1,128)} %param.9) | copy-start | bytes 393220
  1.0 14.6 %copy-start.7 = (bf16[256,512]{1,0:T(8,128)(2,1)S(1)}, bf16[256,512]{1,0:T(8,128)(2,1)}, u32[]{:S(2)}) copy-start(bf16[256,512]{1,0:T(8,128)(2,1)} %constant.8.clone.table_ref) | copy-start | bytes 786436
  15.6 0.7 %copy-start.1 = (s32[6]{0:T(128)S(1)}, s32[6]{0:T(128)}, u32[]{:S(2)}) copy-start(s32[6]{0:T(128)} %param.10) | copy-start | bytes 76
  15.6 0.7 %copy-start.2 = (s32[8]{0:T(128)S(1)}, s32[8]{0:T(128)}, u32[]{:S(2)}) copy-start(s32[8]{0:T(128)} %param.11) | copy-start | bytes 100
  16.3 10.8 %copy-start.6 = (bf16[304,512]{1,0:T(8,128)(2,1)S(1)}, bf16[304,512]{1,0:T(8,128)(2,1)}, u32[]{:S(2)}) copy-start(bf16[304,512]{1,0:T(8,128)(2,1)} %constant.10.clone.table_ref) | copy-start | bytes 933892
  16.6 10.5 %copy-start.3 = (f32[5,64,64]{2,1,0:T(8,128)S(1)}, f32[5,64,64]{2,1,0:T(8,128)}, u32[]{:S(2)}) copy-start(f32[5,64,64]{2,1,0:T(8,128)} %param.12) | copy-start | bytes 245764
  16.6 10.4 %copy-start.5 = (f32[64,1,128]{2,1,0:T(1,128)S(1)}, f32[64,1,128]{2,1,0:T(1,128)}, u32[]{:S(2)}) copy-start(f32[64,1,128]{2,1,0:T(1,128)} %param.13) | copy-start | bytes 98308
  16.6 10.4 %copy-start.8 = (f32[32,128]{1,0:T(8,128)S(1)}, f32[32,128]{1,0:T(8,128)}, u32[]{:S(2)}) copy-start(f32[32,128]{1,0:T(8,128)} %constant.9.clone.turns_ref) | copy-start | bytes 49156
  28.0 9.3 %copy-start = (bf16[336,128]{1,0:T(8,128)(2,1)S(1)}, bf16[336,128]{1,0:T(8,128)(2,1)}, u32[]{:S(2)}) copy-start(bf16[336,128]{1,0:T(8,128)(2,1)} %constant.11.clone.pool_ref) | copy-start | bytes 258052

commit v9 on v5

--- a/solution.py
+++ b/solution.py
@@ -42,6 +42,7 @@
 
 VMEM = pl.BlockSpec(memory_space=pltpu.VMEM)
 PARAMS = pltpu.CompilerParams(vmem_limit_bytes=32 << 20)
+COST = pl.CostEstimate(flops=1 << 30, bytes_accessed=1 << 24, transcendentals=0)
 
 
 KINDS = 4
@@ -65,8 +66,28 @@
     return [lax.broadcasted_iota(jnp.int32, shape, axis) for axis in range(len(shape))]
 
 
+def turns_kernel(order, turn_ref):
+    row, lane = iotas((8, LANES))
+    own = lax.axis_index("bins") * lax.axis_size("scans") + lax.axis_index("scans")
+    k_index = 8 * own + 4 * (lane >> 6) + (row & 3)
+    for c in range(turn_ref.shape[0] // 2):
+        phase = ((c * HALF + (lane & (HALF - 1))) * k_index) & (order - 1)
+        turn_ref[2 * c], turn_ref[2 * c + 1] = unit_turn(phase, order)
+
+
+def turns_step(groups, order):
+    return pl.pallas_call(
+        functools.partial(turns_kernel, order),
+        out_shape=jax.ShapeDtypeStruct((2 * groups, 8, LANES), F32),
+        out_specs=VMEM,
+        compiler_params=PARAMS,
+        cost_estimate=COST,
+        name="turns",
+    )()
+
+
 def columns_kernel(
-    x_ref, edges_ref, counts_ref, out_ref, wanted_ref, lane_band_ref, row_band_ref
+    x_ref, turn_ref, edges_ref, counts_ref, out_ref, wanted_ref, lane_band_ref, row_band_ref
 ):
     groups, rows, _ = out_ref.shape
     capacity = row_band_ref.shape[0]
@@ -105,7 +126,7 @@
         ref[...] = jnp.where(slot < own_count, band, -1)
 
 
-def columns_step(profile, band_edges, owner_counts, capacity):
+def columns_step(profile, turn, band_edges, owner_counts, capacity):
     groups = owner_counts.shape[0]
     rows = profile.shape[0] // (groups * LANES)
     return pl.pallas_call(
@@ -116,11 +137,11 @@
             jax.ShapeDtypeStruct((1, LANES), jnp.int32),
             jax.ShapeDtypeStruct((capacity, LANES), jnp.int32),
         ),
-        in_specs=[VMEM] * 3,
+        in_specs=[VMEM] * 4,
         out_specs=(VMEM,) * 4,
         compiler_params=PARAMS,
         name="columns",
-    )(profile.reshape(-1, LANES), band_edges.reshape(1, -1), owner_counts.reshape(1, -1))
+    )(profile.reshape(-1, LANES), turn, band_edges.reshape(1, -1), owner_counts.reshape(1, -1))
 
 
 def coarse_table(coarse):
@@ -134,7 +155,7 @@
     return np.concatenate(two_terms(parts.reshape(half, half)), axis=1)
 
 
-def coarse_kernel(groups, shares, x_ref, table_ref, out_ref, turn_ref):
+def coarse_kernel(shares, x_ref, table_ref, out_ref):
     half = x_ref.shape[0]
     quarter = half // 2
     row, lane = iotas((8, LANES))
@@ -171,24 +192,15 @@
         imag = even_imag + odd_imag * cosine - odd_real * sine
         out_ref[pl.ds(8 * first, 8, stride=2), :] = real
         out_ref[pl.ds(8 * first + 1, 8, stride=2), :] = imag
-    own = lax.axis_index("bins") * lax.axis_size("scans") + lax.axis_index("scans")
-    k_index = 8 * own + 4 * (lane >> 6) + (row & 3)
-    order = 2 * half * groups * HALF
-    for c in range(groups):
-        phase = ((c * HALF + (lane & (HALF - 1))) * k_index) & (order - 1)
-        turn_ref[2 * c], turn_ref[2 * c + 1] = unit_turn(phase, order)
-
-
-def coarse_step(columns, groups, shares):
+
+
+def coarse_step(columns, shares):
     half = columns.shape[0]
     return pl.pallas_call(
-        functools.partial(coarse_kernel, groups, shares),
-        out_shape=(
-            jax.ShapeDtypeStruct((half, LANES), F32),
-            jax.ShapeDtypeStruct((2 * groups, 8, LANES), F32),
-        ),
+        functools.partial(coarse_kernel, shares),
+        out_shape=jax.ShapeDtypeStruct((half, LANES), F32),
         in_specs=[VMEM] * 2,
-        out_specs=(VMEM,) * 2,
+        out_specs=VMEM,
         compiler_params=PARAMS,
         name="coarse_dft",
     )(columns, jnp.asarray(coarse_table(2 * half)))
@@ -563,11 +575,12 @@
     count = prof_rows * scans * TILE
     state = prev_state.reshape(capacity, 2 * STATES)
     if groups == 8 and scans == 4 and coarse == 16 * shares and capacity == HALF:
+        turn = turns_step(groups, groups * length)
         columns, wanted, lane_band, row_band = columns_step(
-            profiles.reshape(length), band_edges, owner_counts, capacity
+            profiles.reshape(length), turn, band_edges, owner_counts, capacity
         )
         columns = exchanged(columns, "bins").reshape(coarse // 2, LANES)
-        blocks, turn = coarse_step(columns, groups, shares)
+        blocks = coarse_step(columns, shares)
         blocks = exchanged(blocks.reshape(shares, 8, LANES), ("bins", "scans"))
         payload, moved = fine_step(
             blocks.reshape(8 * shares, LANES),

time: 39 us -> 37.7 us (0.967)
  local copies, waits for them, and re-layouts: 2.3 us -> 0.88 us
    unnamed x18, local copies, waits for them, and re-layouts: 2.3 us -> 0.88 us
where the time goes in v9:
time: 37.7 us; the launch traced here: 37.4 us
  blocking collectives  34.1 us (90%)
  Pallas kernels  2.39 us (6%)
  local copies, waits for them, and re-layouts  0.88 us (2%)
    all_to_all x3, blocking collectives, exchanged(): return lax.all_to_all(values, axes, split_axis=0, concat_axis=0, tiled=True)  34.1 us
    pallas_call x1, Pallas kernels, fine_step(): pl.pallas_call(functools.partial(fine_kernel, profiles), out_shape=(jax.S...  0.93 us
    pallas_call x1, Pallas kernels, update_step(): pl.pallas_call(functools.partial(update_kernel, count), out_shape=jax.Sha...  0.93 us
    unnamed x18, local copies, waits for them, and re-layouts  0.88 us

profile of v9, /device:TPU:0, one launch (start us, length us, event | category | flops | bytes accessed | tf_op | source)
XLA Modules:
  0.0 37.4 jit_solution(2818019373317743207)
XLA Ops:
  0.0 0.0 copy-start.3
  0.0 0.0 copy-start.7
  0.0 0.0 copy-start.8
  0.0 0.1 turns.1.turn_ref
  0.1 0.0 copy-start.1
  0.1 0.8 %copy-done.3 = f32[1,32768]{1,0:T(1,128)S(1)} copy-done((f32[1,32768]{1,0:T(1,128)S(1)}, f32[1,32768]{1,0:T(1,128)}, u32[]{:S(2)}) %copy-start.3) | copy-done | bytes 131096
  0.9 0.0 copy-done.7
  0.9 0.0 copy-done.8
  0.9 0.1 columns.1
  1.0 14.4 %all_to_all.15 = f32[8,32,128]{2,1,0:T(8,128)S(1)} all-to-all(f32[8,32,128]{2,1,0:T(8,128)S(1)} %get-tuple-element.11), channel_id=1, replica_groups=mesh['bins'=8,'scans'=4] {'bins'}, dimensions={0} | all-to-all | bytes 262144 | tf_op jit(solution)/shard_map/all_to_all | solution.py:566
  15.5 0.0 copy-done.1
  15.5 0.0 copy-start
  15.5 0.4 coarse_dft.1
  15.8 0.0 copy-start.2
  15.8 0.0 copy-start.5
  15.9 0.0 copy-start.6
  15.9 10.4 %all_to_all.16 = f32[32,8,128]{2,1,0:T(8,128)S(1)} all-to-all(f32[32,8,128]{2,1,0:T(8,128)S(1)} %bitcast.15), channel_id=1, replica_groups=mesh['bins'=8,'scans'=4] {'bins','scans'}, dimensions={0} | all-to-all | bytes 262144 | tf_op jit(solution)/shard_map/all_to_all | solution.py:566
  26.3 0.0 copy-done
  26.3 0.0 copy-done.2
  26.3 0.0 copy-done.5
  26.3 0.0 copy-done.6
  26.3 0.9 %fine_dft.1 = (f32[8,16,128]{2,1,0:T(8,128)S(1)}, f32[64,128]{1,0:T(8,128)S(1)}) custom-call(f32[256,128]{1,0:T(8,128)S(1)} %bitcast.13, f32[16,8,128]{2,1,0:T(8,128)S(1)} %turns.1.turn_ref, s32[1,512]{1,0:T(1,128)S(1)} %get-tuple-element.12.wanted_ref, s32[64,128]{1,0:T(8,128)S(1)} %get-tuple-element.13.band_ref, f32[32,128]{1,0:T(8,128)S(1)} %copy-done.6, ...), custom_call_target="tpu_custom_call" | custom-call | tf_op jit(solution)/shard_map/fine_dft/pallas_call | solution.py:422
  27.2 0.0 copy-start.4
  27.3 9.2 %all_to_all.17 = f32[32,4,128]{2,1,0:T(4,128)S(1)} all-to-all(f32[32,4,128]{2,1,0:T(4,128)S(1)} %bitcast.19), channel_id=1, replica_groups=mesh['bins'=8,'scans'=4] {'bins','scans'}, dimensions={0} | all-to-all | bytes 131072 | tf_op jit(solution)/shard_map/all_to_all | solution.py:566
  36.5 0.0 copy-done.4
  36.5 0.9 %state_update.1 = f32[64,128]{1,0:T(8,128)} custom-call(f32[128,128]{1,0:T(8,128)S(1)} %bitcast.16, bf16[336,128]{1,0:T(8,128)(2,1)S(1)} %copy-done.4, f32[64,128]{1,0:T(8,128)S(1)} %get-tuple-element.15.moved_ref, s32[1,128]{1,0:T(1,128)S(1)} %get-tuple-element.16.band_ref), custom_call_target="tpu_custom_call" | custom-call | tf_op jit(solution)/shard_map/state_update/pallas_call | solution.py:536
Async XLA Ops:
  0.0 0.9 %copy-start.3 = (f32[1,32768]{1,0:T(1,128)S(1)}, f32[1,32768]{1,0:T(1,128)}, u32[]{:S(2)}) copy-start(f32[1,32768]{1,0:T(1,128)} %param.9) | copy-start | bytes 393220
  0.0 0.9 %copy-start.7 = (s32[6]{0:T(128)S(1)}, s32[6]{0:T(128)}, u32[]{:S(2)}) copy-start(s32[6]{0:T(128)} %param.10) | copy-start | bytes 76
  0.0 0.9 %copy-start.8 = (s32[8]{0:T(128)S(1)}, s32[8]{0:T(128)}, u32[]{:S(2)}) copy-start(s32[8]{0:T(128)} %param.11) | copy-start | bytes 100
  0.1 15.4 %copy-start.1 = (bf16[256,512]{1,0:T(8,128)(2,1)S(1)}, bf16[256,512]{1,0:T(8,128)(2,1)}, u32[]{:S(2)}) copy-start(bf16[256,512]{1,0:T(8,128)(2,1)} %constant.8.clone.table_ref) | copy-start | bytes 786436
  15.5 10.8 %copy-start = (bf16[304,512]{1,0:T(8,128)(2,1)S(1)}, bf16[304,512]{1,0:T(8,128)(2,1)}, u32[]{:S(2)}) copy-start(bf16[304,512]{1,0:T(8,128)(2,1)} %constant.10.clone.table_ref) | copy-start | bytes 933892
  15.8 10.5 %copy-start.2 = (f32[5,64,64]{2,1,0:T(8,128)S(1)}, f32[5,64,64]{2,1,0:T(8,128)}, u32[]{:S(2)}) copy-start(f32[5,64,64]{2,1,0:T(8,128)} %param.12) | copy-start | bytes 245764
  15.8 10.4 %copy-start.5 = (f32[64,1,128]{2,1,0:T(1,128)S(1)}, f32[64,1,128]{2,1,0:T(1,128)}, u32[]{:S(2)}) copy-start(f32[64,1,128]{2,1,0:T(1,128)} %param.13) | copy-start | bytes 98308
  15.9 10.4 %copy-start.6 = (f32[32,128]{1,0:T(8,128)S(1)}, f32[32,128]{1,0:T(8,128)}, u32[]{:S(2)}) copy-start(f32[32,128]{1,0:T(8,128)} %constant.9.clone.turns_ref) | copy-start | bytes 49156
  27.2 9.3 %copy-start.4 = (bf16[336,128]{1,0:T(8,128)(2,1)S(1)}, bf16[336,128]{1,0:T(8,128)(2,1)}, u32[]{:S(2)}) copy-start(bf16[336,128]{1,0:T(8,128)(2,1)} %constant.11.clone.pool_ref) | copy-start | bytes 258052

commit v10 on v9

v10 whole, which is shorter than its diff:
```python
import functools
import math

import jax
import jax.numpy as jnp
import numpy as np
from jax import lax
from jax.experimental import pallas as pl
from jax.experimental.pallas import tpu as pltpu
from jax.sharding import PartitionSpec as P

TILE = 512
STATES = 64
NCLASS = 5
LANES = 128

EPSILON = 1e-05
HIGHEST = lax.Precision.HIGHEST
BF16 = jnp.bfloat16
F32 = jnp.float32


def unit_root(order, exponents):
    angles = 2.0 * np.pi * (np.asarray(exponents, dtype=np.int64) % order) / order
    return np.cos(angles), -np.sin(angles)


def two_terms(values):
    high = np.asarray(values, np.float32).astype(BF16)
    low = (np.asarray(values, np.float64) - high.astype(np.float64)).astype(BF16)
    return high, low


def split_two(values):
    high = values.astype(BF16)
    return high, (values - high.astype(F32)).astype(BF16)


def dot(left, right):
    return jnp.dot(left, right, preferred_element_type=F32)


VMEM = pl.BlockSpec(memory_space=pltpu.VMEM)
PARAMS = pltpu.CompilerParams(vmem_limit_bytes=32 << 20)
COST = pl.CostEstimate(flops=1 << 30, bytes_accessed=1 << 24, transcendentals=0)


KINDS = 4
HALF = LANES // 2


def unit_turn(phase, order):
    shifted = phase + order // 8
    quadrant = (shifted >> (order.bit_length() - 3)) & 3
    x = ((shifted & (order // 4 - 1)) - order // 8).astype(F32) * (2.0 * math.pi / order)
    y = x * x
    cosine = 1.0 + y * (-1 / 2 + y * (1 / 24 + y * (-1 / 720 + y * (1 / 40320))))
    sine = x * (1.0 + y * (-1 / 6 + y * (1 / 120 + y * (-1 / 5040 + y * (1 / 362880)))))
    odd = (quadrant & 1) == 1
    real, imag = jnp.where(odd, sine, cosine), jnp.where(odd, cosine, sine)
    real = jnp.where((quadrant == 1) | (quadrant == 2), -real, real)
    return real, jnp.where(quadrant >= 2, -imag, imag)


def iotas(shape):
    return [lax.broadcasted_iota(jnp.int32, shape, axis) for axis in range(len(shape))]


def turns_kernel(order, turn_ref):
    row, lane = iotas((8, LANES))
    own = lax.axis_index("bins") * lax.axis_size("scans") + lax.axis_index("scans")
    for at in range(turn_ref.shape[0] // 2):
        c, odd = divmod(at, 2)
        k_index = 8 * own + 4 * (lane >> 6) + 2 * (row & 1) + odd
        phase = ((c * HALF + (lane & (HALF - 1))) * k_index) & (order - 1)
        turn_ref[2 * at], turn_ref[2 * at + 1] = unit_turn(phase, order)


def turns_step(groups, order):
    return pl.pallas_call(
        functools.partial(turns_kernel, order),
        out_shape=jax.ShapeDtypeStruct((4 * groups, 8, LANES), F32),
        out_specs=VMEM,
        compiler_params=PARAMS,
        cost_estimate=COST,
        name="turns",
    )()


def slots_kernel(turn_ref, edges_ref, counts_ref, chosen_ref, lane_band_ref, row_band_ref):
    del turn_ref
    groups, capacity = counts_ref.shape[1], row_band_ref.shape[0]
    own = lax.axis_index("bins")
    counts = [
        jnp.broadcast_to(counts_ref[:, owner : owner + 1], (1, LANES)) for owner in range(groups)
    ]
    lane = iotas((1, LANES))[1]
    rank = lane & (capacity - 1)
    start = jnp.zeros((1, LANES), jnp.int32)
    own_start, own_count = start, start
    wanted = []
    for owner, count in enumerate(counts):
        wanted.append(jnp.where(rank < count, start + rank, -1))
        own_start = jnp.where(own == owner, start, own_start)
        own_count = jnp.where(own == owner, count, own_count)
        start = start + count
    quarter = HALF // 2
    tile = groups * iotas((quarter, LANES))[0]
    for pair in range(groups // 2):
        tiles = jnp.where(lane < HALF, wanted[2 * pair], wanted[2 * pair + 1])
        for u in range(groups):
            chosen_ref[u * quarter : (u + 1) * quarter, pair * LANES : (pair + 1) * LANES] = (
                jnp.where(tile + u == tiles, 1.0, 0.0).astype(BF16)
            )
    edges = [jnp.broadcast_to(edges_ref[:, at : at + 1], (1, LANES)) for at in range(1, NCLASS)]
    for ref, slot in ((lane_band_ref, rank), (row_band_ref, iotas((capacity, LANES))[0])):
        band = jnp.zeros_like(slot)
        for edge in edges:
            band = band + jnp.where(slot + own_start >= edge, 1, 0)
        ref[...] = jnp.where(slot < own_count, band, -1)


def slots_step(turn, band_edges, owner_counts, capacity):
    groups = owner_counts.shape[0]
    return pl.pallas_call(
        slots_kernel,
        out_shape=(
            jax.ShapeDtypeStruct((groups * HALF // 2, groups * capacity), BF16),
            jax.ShapeDtypeStruct((1, LANES), jnp.int32),
            jax.ShapeDtypeStruct((capacity, LANES), jnp.int32),
        ),
        in_specs=[VMEM] * 3,
        out_specs=(VMEM,) * 3,
        compiler_params=PARAMS,
        name="slots",
    )(turn, band_edges.reshape(1, -1), owner_counts.reshape(1, -1))


def columns_kernel(x_ref, band_ref, out_ref):
    del band_ref
    groups, rows, _ = out_ref.shape
    low_lanes = iotas((rows, LANES))[1] < HALF
    for pair in range(groups // 2):
        even = x_ref[pl.ds(pair, rows, stride=groups), :]
        odd = x_ref[pl.ds(groups // 2 + pair, rows, stride=groups), :]
        out_ref[2 * pair] = jnp.where(low_lanes, even, pltpu.roll(odd, HALF, 1))
        out_ref[2 * pair + 1] = jnp.where(low_lanes, pltpu.roll(even, HALF, 1), odd)


def columns_step(profile, band, groups):
    rows = profile.shape[0] // (groups * LANES)
    return pl.pallas_call(
        columns_kernel,
        out_shape=jax.ShapeDtypeStruct((groups, rows, LANES), F32),
        in_specs=[VMEM] * 2,
        out_specs=VMEM,
        compiler_params=PARAMS,
        name="columns",
    )(profile.reshape(-1, LANES), band)


def coarse_table(coarse):
    half, quarter = coarse // 2, coarse // 4
    k_index = np.arange(quarter)
    a_index = np.concatenate([np.arange(0, half, 2), np.arange(1, half, 2)])
    real, imag = unit_root(half, k_index[:, None] * a_index[None, :])
    imag[0] = 1
    parts = [part.reshape(quarter // 16, 2, 2, 1, 4, half) for part in (real, imag)]
    parts = np.concatenate(parts, axis=3).transpose(0, 2, 3, 1, 4, 5)
    return np.concatenate(two_terms(parts.reshape(half, half)), axis=1)


def coarse_kernel(shares, x_ref, table_ref, out_ref):
    half = x_ref.shape[0]
    quarter = half // 2
    row, lane = iotas((8, LANES))
    low_lanes = lane < HALF
    sums = []
    for parity in range(2):
        high, low = split_two(x_ref[pl.ds(parity, quarter, stride=2), :])
        at = parity * quarter
        both = dot(table_ref[:, at : at + quarter], jnp.concatenate([high, low], axis=1))
        rest = dot(table_ref[:, half + at : half + at + quarter], high)
        sums.append(both[:, :LANES] + both[:, LANES:] + rest)
    base = 8 * (row >> 2) + 4 * (lane >> 6) + (row & 3)
    base_cosine, base_sine = unit_turn(base, 2 * half)
    packed = low_lanes & (row == 0)
    for sign, block in [(sign, block) for block in range(half // 32) for sign in (1, -1)]:
        pieces = []
        for at in range(32 * block, 32 * (block + 1), 8):
            even, odd = sums[0][at : at + 8], sums[1][at : at + 8]
            pieces.append(even + odd if sign > 0 else even - odd)
        real_low, imag_low, real_high, imag_high = pieces
        if block == 0 and sign < 0:
            imag_low = jnp.where(row == 0, 0.0, imag_low)
        even_real = jnp.where(low_lanes, real_low, pltpu.roll(real_high, HALF, 1))
        even_imag = jnp.where(low_lanes, imag_low, pltpu.roll(imag_high, HALF, 1))
        odd_real = jnp.where(low_lanes, pltpu.roll(real_low, HALF, 1), real_high)
        odd_imag = jnp.where(low_lanes, pltpu.roll(imag_low, HALF, 1), imag_high)
        first = 2 * block + (0 if sign > 0 else shares // 2)
        angle = math.pi * 8 * first / half
        cosine = base_cosine * math.cos(angle) - base_sine * math.sin(angle)
        sine = base_sine * math.cos(angle) + base_cosine * math.sin(angle)
        real = even_real + odd_real * cosine + odd_imag * sine
        if first == 0:
            cosine = jnp.where(packed, -1.0, cosine)
        imag = even_imag + odd_imag * cosine - odd_real * sine
        out_ref[pl.ds(8 * first, 8, stride=2), :] = real
        out_ref[pl.ds(8 * first + 1, 8, stride=2), :] = imag


def coarse_step(columns, shares):
    half = columns.shape[0]
    return pl.pallas_call(
        functools.partial(coarse_kernel, shares),
        out_shape=jax.ShapeDtypeStruct((half, LANES), F32),
        in_specs=[VMEM] * 2,
        out_specs=VMEM,
        compiler_params=PARAMS,
        name="coarse_dft",
    )(columns, jnp.asarray(coarse_table(2 * half)))


def coarse_step_general(columns, shares):
    coarse = columns.shape[0]
    half = coarse // 2
    real, imag = unit_root(coarse, np.arange(half)[:, None] * np.arange(coarse)[None, :])
    imag[0] = 1 - 2 * (np.arange(coarse) % 2)
    table = jnp.asarray(np.concatenate([real, imag]).astype(np.float32))
    spectrum = jnp.dot(table, columns, precision=HIGHEST)
    blocks = jnp.concatenate([spectrum[:half], spectrum[half:]], axis=1)
    return blocks.reshape(shares, half // shares, LANES)


def fine_tables(groups, coarse):
    fine_length = groups * HALF
    doubled = np.arange(LANES) % HALF
    turn = unit_root(fine_length, np.arange(groups)[:, None] * doubled[None, :])
    middle = (np.arange(groups)[:, None] * HALF + doubled[None, :]) * (coarse // 2)
    middle = unit_root(coarse * fine_length, middle)
    turns = np.concatenate(turn + middle).astype(np.float32)
    order = np.arange(HALF)
    order[HALF // 2 :] = order[HALF // 2 :][::-1]
    real, imag = unit_root(HALF, np.arange(HALF)[:, None] * order[None, :])
    sign = np.where(np.arange(HALF) < HALF // 2, 1, -1)
    both = np.eye(2)
    matrix = np.block(
        [
            [np.kron(both, real), np.kron(both, imag * sign)],
            [np.kron(both, -imag), np.kron(both, real * sign)],
        ]
    )
    return turns, np.concatenate(two_terms(matrix), axis=1)


def add(p, q):
    return (p[0] + q[0], p[1] + q[1])


def sub(p, q):
    return (p[0] - q[0], p[1] - q[1])


def times(p, cosine, sine):
    return (p[0] * cosine + p[1] * sine, p[1] * cosine - p[0] * sine)


def eight_point(values):
    half = math.sqrt(0.5)

    def down(p):
        return (p[1], -p[0])

    def four(a, b, c, d):
        s0, s1, s2, s3 = add(a, c), sub(a, c), add(b, d), sub(b, d)
        turned = (s1[0] + s3[1], s1[1] - s3[0]), (s1[0] - s3[1], s1[1] + s3[0])
        return add(s0, s2), turned[0], sub(s0, s2), turned[1]

    even = four(values[0], values[2], values[4], values[6])
    odd = four(values[1], values[3], values[5], values[7])
    turned = [
        odd[0],
        ((odd[1][0] + odd[1][1]) * half, (odd[1][1] - odd[1][0]) * half),
        down(odd[2]),
        ((odd[3][1] - odd[3][0]) * half, (odd[3][0] + odd[3][1]) * -half),
    ]
    return [add(e, t) for e, t in zip(even, turned)] + [sub(e, t) for e, t in zip(even, turned)]


def fine_kernel(profiles, x_ref, turn_ref, chosen_ref, turns_ref, table_ref, out_ref):
    groups = turn_ref.shape[0] // 4
    first = (lax.axis_index("bins") == 0) & (lax.axis_index("scans") == 0)
    row, lane = iotas((8, LANES))
    low_lanes = lane < HALF
    low_side = (lane & (HALF - 1)) < HALF // 2
    even = (row & 1) == 0
    packed = first & low_lanes & even
    blocks = [[None] * 3 for _ in range(groups)]
    for at in range(3):
        column = []
        for c in range(groups):
            start = c * 8 * profiles
            if at < 2:
                real = x_ref[pl.ds(start + 2 * at, 8, stride=4), :]
                imag = x_ref[pl.ds(start + 2 * at + 1, 8, stride=4), :]
                imag = imag if at else jnp.where(packed, 0.0, imag)
                turn = 4 * c + 2 * at
                column.append(times((real, imag), turn_ref[turn], turn_ref[turn + 1]))
            else:
                middle = jnp.where(packed, x_ref[pl.ds(start + 1, 8, stride=4), :], 0.0)
                middle_real = turns_ref[2 * groups + c : 2 * groups + c + 1, :]
                middle_imag = turns_ref[3 * groups + c : 3 * groups + c + 1, :]
                column.append((middle * middle_real, middle * middle_imag))
        for u, value in enumerate(eight_point(column)):
            cosine, sine = turns_ref[u : u + 1, :], -turns_ref[groups + u : groups + u + 1, :]
            blocks[u][at] = times(value, cosine, sine) if u else value
    rows = [block for blocks_u in blocks for block in blocks_u]
    left = jnp.concatenate(
        [jnp.concatenate([block[part] for block in rows], axis=0) for part in range(2)], axis=1
    )
    wide = 2 * LANES
    high, low = split_two(left)
    product = dot(high, table_ref[...])
    product = product[:, :wide] + product[:, wide:] + dot(low, table_ref[:, :wide])
    spectrum = []
    for u in range(groups):
        spectrum.append([])
        for at in range(3):
            start = 8 * (3 * u + at)
            block = (product[start : start + 8, :LANES], product[start : start + 8, LANES:])
            if at != 1:
                dropped = ~low_side & packed if at == 0 else ~low_side
                block = tuple(jnp.where(dropped, 0.0, part) for part in block)
            spectrum[u].append(block)
    squares = [
        sum(block[0] * block[0] + block[1] * block[1] for block in spectrum[u])
        for u in range(groups)
    ]
    rest_place = ~low_side & low_lanes & even
    left = [[], [], [], []]
    for u in range(groups):
        mirror = groups - 1 - u
        power = jnp.where(low_side, squares[u], squares[mirror])
        for shift in (4, 2, 1):
            power = power + pltpu.roll(power, shift, 0)
        for part in range(2):
            evens, odds = (
                jnp.where(low_side, spectrum[u][at][part], spectrum[mirror][at][part])
                for at in range(2)
            )
            sums = jnp.where(rest_place, 0.0, evens) + odds
            sums = sums + pltpu.roll(sums, 7, 0)
            left[2 * part].append(
                jnp.where(
                    even,
                    jnp.where(low_side, sums, 0.0),
                    jnp.where(low_side, 0.0, pltpu.roll(sums, 1, 0)),
                )
            )
            rest = jnp.where(rest_place, evens, spectrum[u][2][part])
            left[2 * part + 1].append(jnp.where(even, rest, power))
    left = jnp.concatenate([jnp.concatenate(pieces, axis=1) for pieces in left], axis=0)
    left = jnp.concatenate(split_two(left), axis=0)
    quarter = HALF // 2
    chosen = [chosen_ref[u * quarter : (u + 1) * quarter, :] for u in range(groups)]
    routed = dot(left, jnp.concatenate([piece for piece in chosen for _ in range(4)], axis=0))
    routed = routed[:32] + routed[32:]
    for pair in range(groups // 2):
        for at in range(2):
            real = routed[8 * at : 8 * (at + 1), pair * LANES : (pair + 1) * LANES]
            imag = routed[16 + 8 * at : 16 + 8 * (at + 1), pair * LANES : (pair + 1) * LANES]
            start = 2 * pair * profiles * KINDS + at
            out_ref[pl.ds(start, 8, stride=2), :] = jnp.where(
                low_lanes, real, pltpu.roll(imag, HALF, 1)
            )
            out_ref[pl.ds(start + profiles * KINDS, 8, stride=2), :] = jnp.where(
                low_lanes, pltpu.roll(real, HALF, 1), imag
            )


def fine_step(arrived, turn, chosen, profiles, coarse):
    groups = turn.shape[0] // 4
    turns, table = fine_tables(groups, coarse)
    out = pl.pallas_call(
        functools.partial(fine_kernel, profiles),
        out_shape=jax.ShapeDtypeStruct((groups * profiles * KINDS, LANES), F32),
        in_specs=[VMEM] * 5,
        out_specs=VMEM,
        compiler_params=PARAMS,
        name="fine_dft",
    )(arrived, turn, chosen, jnp.asarray(turns), jnp.asarray(table))
    return out.reshape(groups * profiles, KINDS, LANES)


def fine_step_general(arrived, owner_counts, capacity):
    groups, rows = arrived.shape[:2]
    coarse = 2 * rows * groups
    fine_length = groups * HALF
    order = coarse * fine_length
    own = lax.axis_index("bins")
    real, imag = arrived[:, :, :HALF], arrived[:, :, HALF:]
    points = jnp.arange(fine_length, dtype=jnp.int32).reshape(groups, 1, HALF)
    k_index = own * rows + jnp.arange(rows, dtype=jnp.int32)[None, :, None]
    cosine, sine = unit_turn(points * k_index & (order - 1), order)
    packed = (own == 0) & (jnp.arange(rows)[None, :, None] == 0)
    middle = jnp.where(own == 0, imag[:, :1], 0.0)
    imag = jnp.where(packed, 0.0, imag)
    real, imag = real * cosine + imag * sine, imag * cosine - real * sine
    cosine, sine = unit_turn(points * (coarse // 2), order)
    real = jnp.concatenate([real, middle * cosine], axis=1)
    imag = jnp.concatenate([imag, -middle * sine], axis=1)

    def turned(pattern, root, parts):
        cosine, sine = (jnp.asarray(part.astype(np.float32)) for part in root)
        mul = functools.partial(jnp.einsum, pattern, precision=HIGHEST)
        return (
            mul(cosine, parts[0]) - mul(sine, parts[1]),
            mul(cosine, parts[1]) + mul(sine, parts[0]),
        )

    group_index, point_index = np.arange(groups), np.arange(HALF)
    parts = turned(
        "cu,crj->urj", unit_root(groups, group_index[:, None] * group_index), (real, imag)
    )
    parts = turned(
        "uj,urj->urj", unit_root(fine_length, group_index[:, None] * point_index), parts
    )
    parts = turned(
        "jv,urj->vur", unit_root(HALF, point_index[:, None] * point_index), parts
    )
    tiles = fine_length // 2
    kept = jnp.concatenate([~packed[0, :, 0], jnp.zeros((1,), bool)])
    sides = []
    for part, sign in zip(parts, (1.0, -1.0)):
        part = part.reshape(fine_length, rows + 1)
        sides.append((part[:tiles], sign * jnp.where(kept, part[tiles:][::-1], 0.0)))
    power = sum(jnp.sum(part * part, axis=1) for pair in sides for part in pair)
    starts = jnp.cumsum(owner_counts) - owner_counts
    slot_index = jnp.arange(capacity, dtype=jnp.int32)
    filled = slot_index[None, :] < owner_counts[:, None]
    chosen = jnp.clip(starts[:, None] + slot_index[None, :], 0, tiles - 1)

    def kinds(low, high):
        low_sums, high_sums = jnp.sum(low[:, :rows], axis=1), jnp.sum(high[:, 1:rows], axis=1)
        values = jnp.stack([low_sums, high[:, 0] + low[:, rows], high_sums, power], axis=1)
        return jnp.where(filled[:, :, None], values[chosen], 0.0).transpose(0, 2, 1)

    return jnp.concatenate([kinds(*sides[0]), kinds(*sides[1])], axis=2)


def pool_table(shares, coarse):
    pool = np.zeros((21, 16, shares, KINDS), np.float32)
    sums = pool[:20].reshape(NCLASS, STATES, shares, KINDS)
    wide = TILE // STATES
    rows = coarse // 2 // shares
    for share in range(shares):
        first = rows * share
        rest = coarse - first if share else coarse // 2
        for kind, at in enumerate((first, rest, coarse - first - 1)):
            for band in range(NCLASS):
                sums[band, at // wide >> band, share, kind] = 1.0
    pool[20, :, :, 3] = 1.0
    return pool.reshape(-1, shares * KINDS).astype(BF16)


def state_product(dynamics, state, band):
    row, column = iotas((NCLASS * STATES, STATES))
    limit = STATES >> (row >> 6)
    inside = ((row & (STATES - 1)) < limit) & (column < limit)
    dynamics = jnp.where(inside, dynamics, 0.0)
    empty = jnp.zeros_like(dynamics)
    halves = [
        jnp.concatenate([dynamics, empty], axis=1),
        jnp.concatenate([empty, dynamics], axis=1),
    ]
    matrix = jnp.concatenate(
        [half[k * STATES : (k + 1) * STATES] for k in range(NCLASS) for half in halves], axis=0
    )
    state_high, state_low = split_two(state)
    high, low = split_two(matrix)
    moved = lax.dot_general(
        jnp.concatenate([state_high, state_low, state_high], axis=1),
        jnp.concatenate([high, high, low], axis=1),
        (((1,), (1,)), ((), ())),
        preferred_element_type=F32,
    )
    result = jnp.zeros(state.shape, F32)
    for k in range(NCLASS):
        result = jnp.where(band == k, moved[:, k * LANES : (k + 1) * LANES], result)
    return result


def update_kernel(
    count, x_ref, pool_ref, lane_band_ref, row_band_ref, dynamics_ref, state_ref, out_ref
):
    band = lane_band_ref[...]
    sums = dot(pool_ref[...], jnp.concatenate(split_two(x_ref[...]), axis=1))
    sums = sums[:, :LANES] + sums[:, LANES:]
    power = sums[NCLASS * STATES : NCLASS * STATES + 1] * (1.0 / count)
    span = jnp.left_shift(TILE // STATES, jnp.maximum(band, 0)).astype(F32)
    scaling = 1.0 / jnp.sqrt(span * (power + EPSILON))
    scaling = jnp.where(band < 0, 0.0, scaling)
    chosen = sums[:STATES]
    for k in range(1, NCLASS):
        chosen = jnp.where(band == k, sums[k * STATES : (k + 1) * STATES], chosen)
    chosen = chosen * scaling
    turned = jnp.transpose(jnp.concatenate([chosen, chosen], axis=0))
    half = turned.shape[0] // 2
    measured = jnp.where(iotas((half, LANES))[1] < STATES, turned[:half], turned[half:])
    out_ref[...] = measured + state_product(
        dynamics_ref[...], state_ref[...], row_band_ref[...]
    )


def update_step(arrived, lane_band, row_band, dynamics, state, coarse, count):
    shares = arrived.shape[0]
    return pl.pallas_call(
        functools.partial(update_kernel, count),
        out_shape=jax.ShapeDtypeStruct(state.shape, F32),
        in_specs=[VMEM] * 6,
        out_specs=VMEM,
        compiler_params=PARAMS,
        name="state_update",
    )(
        arrived.reshape(shares * KINDS, LANES),
        jnp.asarray(pool_table(shares, coarse)),
        lane_band,
        row_band,
        dynamics.reshape(NCLASS * STATES, STATES),
        state,
    )


def bands_general(band_edges, owner_counts, capacity):
    own = lax.axis_index("bins")
    slot = jnp.arange(capacity, dtype=jnp.int32)
    start = jnp.cumsum(owner_counts)[own] - owner_counts[own]
    band = jnp.sum((slot + start)[:, None] >= band_edges[None, 1:NCLASS], axis=1)
    band = jnp.where(slot < owner_counts[own], band, -1).astype(jnp.int32)
    return jnp.tile(band, 2)[None, :], jnp.broadcast_to(band[:, None], (capacity, LANES))


def exchanged(values, axes):
    return lax.all_to_all(values, axes, split_axis=0, concat_axis=0, tiled=True)


def body(profiles, band_edges, owner_counts, dynamics, prev_state):
    groups, scans = lax.axis_size("bins"), lax.axis_size("scans")
    prof_rows, length = profiles.shape
    capacity = prev_state.shape[0]
    coarse = length // HALF
    shares = groups * scans
    count = prof_rows * scans * TILE
    state = prev_state.reshape(capacity, 2 * STATES)
    if groups == 8 and scans == 4 and coarse == 16 * shares and capacity == HALF:
        turn = turns_step(groups, groups * length)
        chosen, lane_band, row_band = slots_step(turn, band_edges, owner_counts, capacity)
        columns = columns_step(profiles.reshape(length), row_band, groups)
        columns = exchanged(columns, "bins").reshape(coarse // 2, LANES)
        blocks = coarse_step(columns, shares)
        blocks = exchanged(blocks.reshape(shares, 8, LANES), ("bins", "scans"))
        payload = fine_step(blocks.reshape(8 * shares, LANES), turn, chosen, scans, coarse)
        arrived = exchanged(payload, ("bins", "scans"))
    else:
        lane_band, row_band = bands_general(band_edges, owner_counts, capacity)
        columns = profiles.reshape(coarse // groups, groups, HALF).transpose(1, 0, 2)
        columns = exchanged(columns, "bins").reshape(coarse, HALF)
        blocks = exchanged(coarse_step_general(columns, groups), "bins")
        arrived = exchanged(fine_step_general(blocks, owner_counts, capacity), "bins")
        power = lax.psum(arrived[:, 3:], "scans")
        arrived = jnp.concatenate([arrived[:, :3], power], axis=1)
    updated = update_step(arrived, lane_band, row_band, dynamics, state, coarse, count)
    return updated.reshape(prev_state.shape)


def solution(mesh):
    return jax.shard_map(
        body,
        mesh=mesh,
        in_specs=(P("scans", "bins"), P(), P(), P(), P("bins", "scans", None)),
        out_specs=P("bins", "scans", None),
        check_vma=False,
    )
```

time: 37.7 us -> 37.6 us (level)
    pallas_call x2 -> x3, Pallas kernels: 1.06 us -> 0.94 us  [the longest x1 0.7 us: fine_step(): pl.pallas_call(functools.partial(fine_kernel, profiles), out_shape=jax.Sh...]
where the time goes in v10:
time: 37.6 us; the launch traced here: 37.3 us
  blocking collectives  34.1 us (91%)
  Pallas kernels  2.39 us (6%)
  local copies, waits for them, and re-layouts  0.78 us (2%)
    all_to_all x3, blocking collectives, exchanged(): return lax.all_to_all(values, axes, split_axis=0, concat_axis=0, tiled=True)  34.1 us
    pallas_call x1, Pallas kernels, update_step(): pl.pallas_call(functools.partial(update_kernel, count), out_shape=jax.Sha...  0.99 us
    unnamed x18, local copies, waits for them, and re-layouts  0.78 us

profile of v10, /device:TPU:0, one launch (start us, length us, event | category | flops | bytes accessed | tf_op | source)
XLA Modules:
  0.0 37.3 jit_solution(5205494586623614099)
XLA Ops:
  0.0 0.0 copy-start.7
  0.0 0.0 copy-start.8
  0.0 0.1 turns.1.turn_ref
  0.1 0.0 copy-start.3
  0.1 0.5 %copy-done.7 = s32[6]{0:T(128)S(1)} copy-done((s32[6]{0:T(128)S(1)}, s32[6]{0:T(128)}, u32[]{:S(2)}) %copy-start.7) | copy-done | bytes 48
  0.7 0.0 copy-done.8
  0.7 0.1 slots.1
  0.8 0.2 copy-done.3
  1.0 0.0 copy-start
  1.0 0.1 columns.1
  1.1 14.4 %all_to_all.15 = f32[8,32,128]{2,1,0:T(8,128)S(1)} all-to-all(f32[8,32,128]{2,1,0:T(8,128)S(1)} %columns.1), channel_id=1, replica_groups=mesh['bins'=8,'scans'=4] {'bins'}, dimensions={0} | all-to-all | bytes 262144 | tf_op jit(solution)/shard_map/all_to_all | solution.py:544
  15.5 0.0 copy-done
  15.5 0.0 copy-start.6
  15.5 0.4 coarse_dft.1
  15.9 0.0 copy-start.1
  15.9 10.4 %all_to_all.16 = f32[32,8,128]{2,1,0:T(8,128)S(1)} all-to-all(f32[32,8,128]{2,1,0:T(8,128)S(1)} %bitcast.15), channel_id=1, replica_groups=mesh['bins'=8,'scans'=4] {'bins','scans'}, dimensions={0} | all-to-all | bytes 262144 | tf_op jit(solution)/shard_map/all_to_all | solution.py:544
  26.3 0.0 copy-done.6
  26.3 0.0 copy-done.1
  26.3 0.0 copy-start.2
  26.4 0.7 %fine_dft.1 = f32[128,128]{1,0:T(8,128)S(1)} custom-call(f32[256,128]{1,0:T(8,128)S(1)} %bitcast.13, f32[32,8,128]{2,1,0:T(8,128)S(1)} %turns.1.turn_ref, bf16[256,512]{1,0:T(8,128)(2,1)S(1)} %get-tuple-element.9.chosen_ref, f32[32,128]{1,0:T(8,128)S(1)} %copy-done.6, bf16[256,512]{1,0:T(8,128)(2,1)S(1)} %copy-done.1), custom_call_target="tpu_custom_call" | custom-call | tf_op jit(solution)/shard_map/fine_dft/pallas_call | solution.py:384
  27.1 0.0 copy-start.4
  27.1 0.0 copy-start.5
  27.1 9.2 %all_to_all.17 = f32[32,4,128]{2,1,0:T(4,128)S(1)} all-to-all(f32[32,4,128]{2,1,0:T(4,128)S(1)} %bitcast.17), channel_id=1, replica_groups=mesh['bins'=8,'scans'=4] {'bins','scans'}, dimensions={0} | all-to-all | bytes 131072 | tf_op jit(solution)/shard_map/all_to_all | solution.py:544
  36.3 0.0 copy-done.2
  36.3 0.0 copy-done.4
  36.3 0.0 copy-done.5
  36.3 1.0 %state_update.1 = f32[64,128]{1,0:T(8,128)} custom-call(f32[128,128]{1,0:T(8,128)S(1)} %bitcast.16, bf16[336,128]{1,0:T(8,128)(2,1)S(1)} %copy-done.4, s32[1,128]{1,0:T(1,128)S(1)} %get-tuple-element.10.lane_band_ref, s32[64,128]{1,0:T(8,128)S(1)} %get-tuple-element.8.band_ref.row_band_ref, f32[320,64]{1,0:T(8,128)S(1)} %bitcast.18, f32[64,128]{1,0:T(8,128)S(1)} %bitcast.20), custom_call_target="tpu_custom_call" | custom-call | tf_op jit(solution)/shard_map/state_update/pallas_call | solution.py:517
Async XLA Ops:
  0.0 0.7 %copy-start.7 = (s32[6]{0:T(128)S(1)}, s32[6]{0:T(128)}, u32[]{:S(2)}) copy-start(s32[6]{0:T(128)} %param.10) | copy-start | bytes 76
  0.0 0.7 %copy-start.8 = (s32[8]{0:T(128)S(1)}, s32[8]{0:T(128)}, u32[]{:S(2)}) copy-start(s32[8]{0:T(128)} %param.11) | copy-start | bytes 100
  0.1 0.9 %copy-start.3 = (f32[1,32768]{1,0:T(1,128)S(1)}, f32[1,32768]{1,0:T(1,128)}, u32[]{:S(2)}) copy-start(f32[1,32768]{1,0:T(1,128)} %param.9) | copy-start | bytes 393220
  1.0 14.5 %copy-start = (bf16[256,512]{1,0:T(8,128)(2,1)S(1)}, bf16[256,512]{1,0:T(8,128)(2,1)}, u32[]{:S(2)}) copy-start(bf16[256,512]{1,0:T(8,128)(2,1)} %constant.8.clone.table_ref) | copy-start | bytes 786436
  15.5 10.8 %copy-start.6 = (f32[32,128]{1,0:T(8,128)S(1)}, f32[32,128]{1,0:T(8,128)}, u32[]{:S(2)}) copy-start(f32[32,128]{1,0:T(8,128)} %constant.9.clone.turns_ref) | copy-start | bytes 49156
  15.9 10.4 %copy-start.1 = (bf16[256,512]{1,0:T(8,128)(2,1)S(1)}, bf16[256,512]{1,0:T(8,128)(2,1)}, u32[]{:S(2)}) copy-start(bf16[256,512]{1,0:T(8,128)(2,1)} %constant.10.clone.table_ref) | copy-start | bytes 786436
  26.3 10.0 %copy-start.2 = (f32[5,64,64]{2,1,0:T(8,128)S(1)}, f32[5,64,64]{2,1,0:T(8,128)}, u32[]{:S(2)}) copy-start(f32[5,64,64]{2,1,0:T(8,128)} %param.12) | copy-start | bytes 245764
  27.1 9.3 %copy-start.4 = (bf16[336,128]{1,0:T(8,128)(2,1)S(1)}, bf16[336,128]{1,0:T(8,128)(2,1)}, u32[]{:S(2)}) copy-start(bf16[336,128]{1,0:T(8,128)(2,1)} %constant.11.clone.pool_ref) | copy-start | bytes 258052
  27.1 9.3 %copy-start.5 = (f32[64,1,128]{2,1,0:T(1,128)S(1)}, f32[64,1,128]{2,1,0:T(1,128)}, u32[]{:S(2)}) copy-start(f32[64,1,128]{2,1,0:T(1,128)} %param.13) | copy-start | bytes 98308

commit v11 on v10

--- a/solution.py
+++ b/solution.py
@@ -87,9 +87,18 @@
     )()
 
 
-def slots_kernel(turn_ref, edges_ref, counts_ref, chosen_ref, lane_band_ref, row_band_ref):
+def columns_kernel(
+    x_ref, turn_ref, edges_ref, counts_ref, out_ref, wanted_ref, lane_band_ref, row_band_ref
+):
     del turn_ref
-    groups, capacity = counts_ref.shape[1], row_band_ref.shape[0]
+    groups, rows, _ = out_ref.shape
+    capacity = row_band_ref.shape[0]
+    low_lanes = iotas((rows, LANES))[1] < HALF
+    for pair in range(groups // 2):
+        even = x_ref[pl.ds(pair, rows, stride=groups), :]
+        odd = x_ref[pl.ds(groups // 2 + pair, rows, stride=groups), :]
+        out_ref[2 * pair] = jnp.where(low_lanes, even, pltpu.roll(odd, HALF, 1))
+        out_ref[2 * pair + 1] = jnp.where(low_lanes, pltpu.roll(even, HALF, 1), odd)
     own = lax.axis_index("bins")
     counts = [
         jnp.broadcast_to(counts_ref[:, owner : owner + 1], (1, LANES)) for owner in range(groups)
@@ -104,14 +113,10 @@
         own_start = jnp.where(own == owner, start, own_start)
         own_count = jnp.where(own == owner, count, own_count)
         start = start + count
-    quarter = HALF // 2
-    tile = groups * iotas((quarter, LANES))[0]
     for pair in range(groups // 2):
-        tiles = jnp.where(lane < HALF, wanted[2 * pair], wanted[2 * pair + 1])
-        for u in range(groups):
-            chosen_ref[u * quarter : (u + 1) * quarter, pair * LANES : (pair + 1) * LANES] = (
-                jnp.where(tile + u == tiles, 1.0, 0.0).astype(BF16)
-            )
+        wanted_ref[:, pair * LANES : (pair + 1) * LANES] = jnp.where(
+            lane < HALF, wanted[2 * pair], wanted[2 * pair + 1]
+        )
     edges = [jnp.broadcast_to(edges_ref[:, at : at + 1], (1, LANES)) for at in range(1, NCLASS)]
     for ref, slot in ((lane_band_ref, rank), (row_band_ref, iotas((capacity, LANES))[0])):
         band = jnp.zeros_like(slot)
@@ -120,43 +125,22 @@
         ref[...] = jnp.where(slot < own_count, band, -1)
 
 
-def slots_step(turn, band_edges, owner_counts, capacity):
+def columns_step(profile, turn, band_edges, owner_counts, capacity):
     groups = owner_counts.shape[0]
+    rows = profile.shape[0] // (groups * LANES)
     return pl.pallas_call(
-        slots_kernel,
+        columns_kernel,
         out_shape=(
-            jax.ShapeDtypeStruct((groups * HALF // 2, groups * capacity), BF16),
+            jax.ShapeDtypeStruct((groups, rows, LANES), F32),
+            jax.ShapeDtypeStruct((1, groups * capacity), jnp.int32),
             jax.ShapeDtypeStruct((1, LANES), jnp.int32),
             jax.ShapeDtypeStruct((capacity, LANES), jnp.int32),
         ),
-        in_specs=[VMEM] * 3,
-        out_specs=(VMEM,) * 3,
-        compiler_params=PARAMS,
-        name="slots",
-    )(turn, band_edges.reshape(1, -1), owner_counts.reshape(1, -1))
-
-
-def columns_kernel(x_ref, band_ref, out_ref):
-    del band_ref
-    groups, rows, _ = out_ref.shape
-    low_lanes = iotas((rows, LANES))[1] < HALF
-    for pair in range(groups // 2):
-        even = x_ref[pl.ds(pair, rows, stride=groups), :]
-        odd = x_ref[pl.ds(groups // 2 + pair, rows, stride=groups), :]
-        out_ref[2 * pair] = jnp.where(low_lanes, even, pltpu.roll(odd, HALF, 1))
-        out_ref[2 * pair + 1] = jnp.where(low_lanes, pltpu.roll(even, HALF, 1), odd)
-
-
-def columns_step(profile, band, groups):
-    rows = profile.shape[0] // (groups * LANES)
-    return pl.pallas_call(
-        columns_kernel,
-        out_shape=jax.ShapeDtypeStruct((groups, rows, LANES), F32),
-        in_specs=[VMEM] * 2,
-        out_specs=VMEM,
+        in_specs=[VMEM] * 4,
+        out_specs=(VMEM,) * 4,
         compiler_params=PARAMS,
         name="columns",
-    )(profile.reshape(-1, LANES), band)
+    )(profile.reshape(-1, LANES), turn, band_edges.reshape(1, -1), owner_counts.reshape(1, -1))
 
 
 def coarse_table(coarse):
@@ -167,7 +151,9 @@
     imag[0] = 1
     parts = [part.reshape(quarter // 16, 2, 2, 1, 4, half) for part in (real, imag)]
     parts = np.concatenate(parts, axis=3).transpose(0, 2, 3, 1, 4, 5)
-    return np.concatenate(two_terms(parts.reshape(half, half)), axis=1)
+    high, low = two_terms(parts.reshape(half, half))
+    terms = [term[:, at : at + quarter] for at in (0, quarter) for term in (high, low)]
+    return np.concatenate(terms, axis=1)
 
 
 def coarse_kernel(shares, x_ref, table_ref, out_ref):
@@ -178,10 +164,15 @@
     sums = []
     for parity in range(2):
         high, low = split_two(x_ref[pl.ds(parity, quarter, stride=2), :])
-        at = parity * quarter
-        both = dot(table_ref[:, at : at + quarter], jnp.concatenate([high, low], axis=1))
-        rest = dot(table_ref[:, half + at : half + at + quarter], high)
-        sums.append(both[:, :LANES] + both[:, LANES:] + rest)
+        right = jnp.concatenate(
+            [
+                jnp.concatenate([high, low], axis=1),
+                jnp.concatenate([high, jnp.zeros_like(low)], axis=1),
+            ],
+            axis=0,
+        )
+        both = dot(table_ref[:, parity * half : (parity + 1) * half], right)
+        sums.append(both[:, :LANES] + both[:, LANES:])
     base = 8 * (row >> 2) + 4 * (lane >> 6) + (row & 3)
     base_cosine, base_sine = unit_turn(base, 2 * half)
     packed = low_lanes & (row == 0)
@@ -287,7 +278,7 @@
     return [add(e, t) for e, t in zip(even, turned)] + [sub(e, t) for e, t in zip(even, turned)]
 
 
-def fine_kernel(profiles, x_ref, turn_ref, chosen_ref, turns_ref, table_ref, out_ref):
+def fine_kernel(profiles, x_ref, turn_ref, wanted_ref, turns_ref, table_ref, out_ref):
     groups = turn_ref.shape[0] // 4
     first = (lax.axis_index("bins") == 0) & (lax.axis_index("scans") == 0)
     row, lane = iotas((8, LANES))
@@ -361,9 +352,12 @@
             left[2 * part + 1].append(jnp.where(even, rest, power))
     left = jnp.concatenate([jnp.concatenate(pieces, axis=1) for pieces in left], axis=0)
     left = jnp.concatenate(split_two(left), axis=0)
-    quarter = HALF // 2
-    chosen = [chosen_ref[u * quarter : (u + 1) * quarter, :] for u in range(groups)]
-    routed = dot(left, jnp.concatenate([piece for piece in chosen for _ in range(4)], axis=0))
+    wanted = wanted_ref[...]
+    chosen = []
+    for u in range(groups):
+        tile = u + groups * iotas((HALF // 2, wanted.shape[1]))[0]
+        chosen += [jnp.where(tile == wanted, 1.0, 0.0).astype(BF16)] * 4
+    routed = dot(left, jnp.concatenate(chosen, axis=0))
     routed = routed[:32] + routed[32:]
     for pair in range(groups // 2):
         for at in range(2):
@@ -378,7 +372,7 @@
             )
 
 
-def fine_step(arrived, turn, chosen, profiles, coarse):
+def fine_step(arrived, turn, wanted, profiles, coarse):
     groups = turn.shape[0] // 4
     turns, table = fine_tables(groups, coarse)
     out = pl.pallas_call(
@@ -388,7 +382,7 @@
         out_specs=VMEM,
         compiler_params=PARAMS,
         name="fine_dft",
-    )(arrived, turn, chosen, jnp.asarray(turns), jnp.asarray(table))
+    )(arrived, turn, wanted, jnp.asarray(turns), jnp.asarray(table))
     return out.reshape(groups * profiles, KINDS, LANES)
 
 
@@ -554,12 +548,13 @@
     state = prev_state.reshape(capacity, 2 * STATES)
     if groups == 8 and scans == 4 and coarse == 16 * shares and capacity == HALF:
         turn = turns_step(groups, groups * length)
-        chosen, lane_band, row_band = slots_step(turn, band_edges, owner_counts, capacity)
-        columns = columns_step(profiles.reshape(length), row_band, groups)
+        columns, wanted, lane_band, row_band = columns_step(
+            profiles.reshape(length), turn, band_edges, owner_counts, capacity
+        )
         columns = exchanged(columns, "bins").reshape(coarse // 2, LANES)
         blocks = coarse_step(columns, shares)
         blocks = exchanged(blocks.reshape(shares, 8, LANES), ("bins", "scans"))
-        payload = fine_step(blocks.reshape(8 * shares, LANES), turn, chosen, scans, coarse)
+        payload = fine_step(blocks.reshape(8 * shares, LANES), turn, wanted, scans, coarse)
         arrived = exchanged(payload, ("bins", "scans"))
     else:
         lane_band, row_band = bands_general(band_edges, owner_counts, capacity)

time: 37.6 us -> 37.4 us (level)
  no operation moved by 1% of the time
where the time goes in v11:
time: 37.4 us; the launch traced here: 37.2 us
  blocking collectives  34.1 us (91%)
  Pallas kernels  2.23 us (6%)
  local copies, waits for them, and re-layouts  0.83 us (2%)
    all_to_all x3, blocking collectives, exchanged(): return lax.all_to_all(values, axes, split_axis=0, concat_axis=0, tiled=True)  34.1 us
    pallas_call x1, Pallas kernels, update_step(): pl.pallas_call(functools.partial(update_kernel, count), out_shape=jax.Sha...  0.99 us
    unnamed x18, local copies, waits for them, and re-layouts  0.83 us

profile of v11, /device:TPU:0, one launch (start us, length us, event | category | flops | bytes accessed | tf_op | source)
XLA Modules:
  0.0 37.2 jit_solution(3755105149461248416)
XLA Ops:
  0.0 0.0 copy-start.3
  0.0 0.1 turns.1.turn_ref
  0.1 0.0 copy-start.7
  0.1 0.0 copy-start.8
  0.1 0.8 %copy-done.3 = f32[1,32768]{1,0:T(1,128)S(1)} copy-done((f32[1,32768]{1,0:T(1,128)S(1)}, f32[1,32768]{1,0:T(1,128)}, u32[]{:S(2)}) %copy-start.3) | copy-done | bytes 131096
  0.9 0.0 copy-done.7
  0.9 0.0 copy-done.8
  0.9 0.0 copy-start.1
  0.9 0.1 columns.1
  1.0 14.4 %all_to_all.15 = f32[8,32,128]{2,1,0:T(8,128)S(1)} all-to-all(f32[8,32,128]{2,1,0:T(8,128)S(1)} %get-tuple-element.9), channel_id=1, replica_groups=mesh['bins'=8,'scans'=4] {'bins'}, dimensions={0} | all-to-all | bytes 262144 | tf_op jit(solution)/shard_map/all_to_all | solution.py:538
  15.5 0.0 copy-done.1
  15.5 0.0 copy-start.6
  15.5 0.3 coarse_dft.1
  15.8 0.0 copy-start
  15.8 10.4 %all_to_all.16 = f32[32,8,128]{2,1,0:T(8,128)S(1)} all-to-all(f32[32,8,128]{2,1,0:T(8,128)S(1)} %bitcast.15), channel_id=1, replica_groups=mesh['bins'=8,'scans'=4] {'bins','scans'}, dimensions={0} | all-to-all | bytes 262144 | tf_op jit(solution)/shard_map/all_to_all | solution.py:538
  26.2 0.0 copy-done.6
  26.2 0.0 copy-done
  26.2 0.0 copy-start.2
  26.2 0.7 %fine_dft.1 = f32[128,128]{1,0:T(8,128)S(1)} custom-call(f32[256,128]{1,0:T(8,128)S(1)} %bitcast.13, f32[32,8,128]{2,1,0:T(8,128)S(1)} %turns.1.turn_ref, s32[1,512]{1,0:T(1,128)S(1)} %get-tuple-element.10.wanted_ref, f32[32,128]{1,0:T(8,128)S(1)} %copy-done.6, bf16[256,512]{1,0:T(8,128)(2,1)S(1)} %copy-done), custom_call_target="tpu_custom_call" | custom-call | tf_op jit(solution)/shard_map/fine_dft/pallas_call | solution.py:378
  26.9 0.0 copy-start.4
  27.0 0.0 copy-start.5
  27.0 9.2 %all_to_all.17 = f32[32,4,128]{2,1,0:T(4,128)S(1)} all-to-all(f32[32,4,128]{2,1,0:T(4,128)S(1)} %bitcast.16), channel_id=1, replica_groups=mesh['bins'=8,'scans'=4] {'bins','scans'}, dimensions={0} | all-to-all | bytes 131072 | tf_op jit(solution)/shard_map/all_to_all | solution.py:538
  36.2 0.0 copy-done.2
  36.2 0.0 copy-done.4
  36.2 0.0 copy-done.5
  36.2 1.0 %state_update.1 = f32[64,128]{1,0:T(8,128)} custom-call(f32[128,128]{1,0:T(8,128)S(1)} %bitcast.17, bf16[336,128]{1,0:T(8,128)(2,1)S(1)} %copy-done.4, s32[1,128]{1,0:T(1,128)S(1)} %get-tuple-element.11.lane_band_ref, s32[64,128]{1,0:T(8,128)S(1)} %get-tuple-element.12.row_band_ref, f32[320,64]{1,0:T(8,128)S(1)} %bitcast.18, f32[64,128]{1,0:T(8,128)S(1)} %bitcast.20), custom_call_target="tpu_custom_call" | custom-call | tf_op jit(solution)/shard_map/state_update/pallas_call | solution.py:511
Async XLA Ops:
  0.0 0.9 %copy-start.3 = (f32[1,32768]{1,0:T(1,128)S(1)}, f32[1,32768]{1,0:T(1,128)}, u32[]{:S(2)}) copy-start(f32[1,32768]{1,0:T(1,128)} %param.9) | copy-start | bytes 393220
  0.1 0.8 %copy-start.7 = (s32[6]{0:T(128)S(1)}, s32[6]{0:T(128)}, u32[]{:S(2)}) copy-start(s32[6]{0:T(128)} %param.10) | copy-start | bytes 76
  0.1 0.8 %copy-start.8 = (s32[8]{0:T(128)S(1)}, s32[8]{0:T(128)}, u32[]{:S(2)}) copy-start(s32[8]{0:T(128)} %param.11) | copy-start | bytes 100
  0.9 14.6 %copy-start.1 = (bf16[256,512]{1,0:T(8,128)(2,1)S(1)}, bf16[256,512]{1,0:T(8,128)(2,1)}, u32[]{:S(2)}) copy-start(bf16[256,512]{1,0:T(8,128)(2,1)} %constant.8.clone.table_ref) | copy-start | bytes 786436
  15.5 10.7 %copy-start.6 = (f32[32,128]{1,0:T(8,128)S(1)}, f32[32,128]{1,0:T(8,128)}, u32[]{:S(2)}) copy-start(f32[32,128]{1,0:T(8,128)} %constant.9.clone.turns_ref) | copy-start | bytes 49156
  15.8 10.4 %copy-start = (bf16[256,512]{1,0:T(8,128)(2,1)S(1)}, bf16[256,512]{1,0:T(8,128)(2,1)}, u32[]{:S(2)}) copy-start(bf16[256,512]{1,0:T(8,128)(2,1)} %constant.10.clone.table_ref) | copy-start | bytes 786436
  26.2 10.0 %copy-start.2 = (f32[5,64,64]{2,1,0:T(8,128)S(1)}, f32[5,64,64]{2,1,0:T(8,128)}, u32[]{:S(2)}) copy-start(f32[5,64,64]{2,1,0:T(8,128)} %param.12) | copy-start | bytes 245764
  26.9 9.3 %copy-start.4 = (bf16[336,128]{1,0:T(8,128)(2,1)S(1)}, bf16[336,128]{1,0:T(8,128)(2,1)}, u32[]{:S(2)}) copy-start(bf16[336,128]{1,0:T(8,128)(2,1)} %constant.11.clone.pool_ref) | copy-start | bytes 258052
  27.0 9.3 %copy-start.5 = (f32[64,1,128]{2,1,0:T(1,128)S(1)}, f32[64,1,128]{2,1,0:T(1,128)}, u32[]{:S(2)}) copy-start(f32[64,1,128]{2,1,0:T(1,128)} %param.13) | copy-start | bytes 98308

commit v12 on v11

--- a/solution.py
+++ b/solution.py
@@ -31,9 +31,22 @@
     return high, low
 
 
+def three_terms(values):
+    high, middle = two_terms(values)
+    rest = np.asarray(values, np.float64) - high.astype(np.float64) - middle.astype(np.float64)
+    return high, middle, rest.astype(BF16)
+
+
 def split_two(values):
     high = values.astype(BF16)
     return high, (values - high.astype(F32)).astype(BF16)
+
+
+def split_three(values):
+    high = values.astype(BF16)
+    rest = values - high.astype(F32)
+    middle = rest.astype(BF16)
+    return high, middle, (rest - middle.astype(F32)).astype(BF16)
 
 
 def dot(left, right):
@@ -151,8 +164,8 @@
     imag[0] = 1
     parts = [part.reshape(quarter // 16, 2, 2, 1, 4, half) for part in (real, imag)]
     parts = np.concatenate(parts, axis=3).transpose(0, 2, 3, 1, 4, 5)
-    high, low = two_terms(parts.reshape(half, half))
-    terms = [term[:, at : at + quarter] for at in (0, quarter) for term in (high, low)]
+    high, middle, low = three_terms(parts.reshape(half, half))
+    terms = [term[:, at : at + quarter] for at in (0, quarter) for term in (middle, high, low)]
     return np.concatenate(terms, axis=1)
 
 
@@ -163,15 +176,14 @@
     low_lanes = lane < HALF
     sums = []
     for parity in range(2):
-        high, low = split_two(x_ref[pl.ds(parity, quarter, stride=2), :])
-        right = jnp.concatenate(
-            [
-                jnp.concatenate([high, low], axis=1),
-                jnp.concatenate([high, jnp.zeros_like(low)], axis=1),
-            ],
-            axis=0,
+        high, middle, low = split_three(x_ref[pl.ds(parity, quarter, stride=2), :])
+        main = jnp.concatenate([high, middle], axis=1)
+        rest = [jnp.concatenate([term, jnp.zeros_like(term)], axis=1) for term in (low, high)]
+        at = 3 * quarter * parity
+        left = jnp.concatenate(
+            [table_ref[:, at : at + 2 * quarter], table_ref[:, at + quarter : at + 3 * quarter]], axis=1
         )
-        both = dot(table_ref[:, parity * half : (parity + 1) * half], right)
+        both = dot(left, jnp.concatenate([main, main] + rest, axis=0))
         sums.append(both[:, :LANES] + both[:, LANES:])
     base = 8 * (row >> 2) + 4 * (lane >> 6) + (row & 3)
     base_cosine, base_sine = unit_turn(base, 2 * half)
@@ -234,14 +246,11 @@
     order[HALF // 2 :] = order[HALF // 2 :][::-1]
     real, imag = unit_root(HALF, np.arange(HALF)[:, None] * order[None, :])
     sign = np.where(np.arange(HALF) < HALF // 2, 1, -1)
-    both = np.eye(2)
-    matrix = np.block(
-        [
-            [np.kron(both, real), np.kron(both, imag * sign)],
-            [np.kron(both, -imag), np.kron(both, real * sign)],
-        ]
-    )
-    return turns, np.concatenate(two_terms(matrix), axis=1)
+    matrix = np.block([[real, imag * sign], [-imag, real * sign]])
+    high, middle, low = three_terms(matrix)
+    both = np.concatenate([high, middle], axis=1)
+    rest = [np.concatenate([term, np.zeros_like(term)], axis=1) for term in (low, high)]
+    return turns, np.concatenate([both, both] + rest, axis=0)
 
 
 def add(p, q):
@@ -305,58 +314,56 @@
         for u, value in enumerate(eight_point(column)):
             cosine, sine = turns_ref[u : u + 1, :], -turns_ref[groups + u : groups + u + 1, :]
             blocks[u][at] = times(value, cosine, sine) if u else value
-    rows = [block for blocks_u in blocks for block in blocks_u]
-    left = jnp.concatenate(
-        [jnp.concatenate([block[part] for block in rows], axis=0) for part in range(2)], axis=1
-    )
-    wide = 2 * LANES
-    high, low = split_two(left)
-    product = dot(high, table_ref[...])
-    product = product[:, :wide] + product[:, wide:] + dot(low, table_ref[:, :wide])
+    rows = []
+    for u in range(groups):
+        for at in range(3):
+            real, imag = blocks[u][at]
+            rows.append(jnp.where(low_lanes, real, pltpu.roll(imag, HALF, 1)))
+            if at < 2:
+                rows.append(jnp.where(low_lanes, pltpu.roll(real, HALF, 1), imag))
+    high, middle, low = split_three(jnp.concatenate(rows, axis=0))
+    product = dot(jnp.concatenate([high, middle, high, low], axis=1), table_ref[...])
+    product = product[:, :LANES] + product[:, LANES:]
     spectrum = []
     for u in range(groups):
-        spectrum.append([])
-        for at in range(3):
-            start = 8 * (3 * u + at)
-            block = (product[start : start + 8, :LANES], product[start : start + 8, LANES:])
-            if at != 1:
-                dropped = ~low_side & packed if at == 0 else ~low_side
-                block = tuple(jnp.where(dropped, 0.0, part) for part in block)
-            spectrum[u].append(block)
-    squares = [
-        sum(block[0] * block[0] + block[1] * block[1] for block in spectrum[u])
-        for u in range(groups)
-    ]
-    rest_place = ~low_side & low_lanes & even
-    left = [[], [], [], []]
+        spectrum.append([product[8 * at : 8 * (at + 1)] for at in range(5 * u, 5 * (u + 1))])
+        spectrum[u][0] = jnp.where(first & even & ~low_side, 0.0, spectrum[u][0])
+        spectrum[u][4] = jnp.where(low_side, spectrum[u][4], 0.0)
+    squares = [sum(block * block for block in spectrum[u]) for u in range(groups)]
+    rest_place = ~low_side & even
+    pieces = []
     for u in range(groups):
         mirror = groups - 1 - u
         power = jnp.where(low_side, squares[u], squares[mirror])
         for shift in (4, 2, 1):
             power = power + pltpu.roll(power, shift, 0)
-        for part in range(2):
-            evens, odds = (
-                jnp.where(low_side, spectrum[u][at][part], spectrum[mirror][at][part])
-                for at in range(2)
-            )
-            sums = jnp.where(rest_place, 0.0, evens) + odds
-            sums = sums + pltpu.roll(sums, 7, 0)
-            left[2 * part].append(
-                jnp.where(
-                    even,
-                    jnp.where(low_side, sums, 0.0),
-                    jnp.where(low_side, 0.0, pltpu.roll(sums, 1, 0)),
-                )
-            )
-            rest = jnp.where(rest_place, evens, spectrum[u][2][part])
-            left[2 * part + 1].append(jnp.where(even, rest, power))
-    left = jnp.concatenate([jnp.concatenate(pieces, axis=1) for pieces in left], axis=0)
+        evens, *others = (
+            jnp.where(low_side, spectrum[u][at], spectrum[mirror][at]) for at in range(4)
+        )
+        sums = jnp.where(rest_place, 0.0, evens) + sum(others)
+        sums = sums + pltpu.roll(sums, 7, 0)
+        lows = jnp.where(low_side, sums, 0.0)
+        highs = jnp.where(low_side, 0.0, pltpu.roll(sums, 1, 0))
+        rest = jnp.where(rest_place, evens, spectrum[u][4])
+        pieces.append((jnp.where(even, lows, highs), jnp.where(even, rest, power)))
+    left = [[], [], [], []]
+    for u in range(0, groups, 2):
+        for at in range(2):
+            one, two = pieces[u][at], pieces[u + 1][at]
+            real = jnp.where(low_lanes, one, pltpu.roll(two, HALF, 1))
+            imag = jnp.where(low_lanes, pltpu.roll(one, HALF, 1), two)
+            if at == 1:
+                power = real + imag
+                real, imag = jnp.where(even, real, power), jnp.where(even, imag, power)
+            left[at].append(real)
+            left[2 + at].append(imag)
+    left = jnp.concatenate([jnp.concatenate(parts, axis=1) for parts in left], axis=0)
     left = jnp.concatenate(split_two(left), axis=0)
     wanted = wanted_ref[...]
     chosen = []
     for u in range(groups):
         tile = u + groups * iotas((HALF // 2, wanted.shape[1]))[0]
-        chosen += [jnp.where(tile == wanted, 1.0, 0.0).astype(BF16)] * 4
+        chosen += [jnp.where(tile == wanted, 1.0, 0.0).astype(BF16)] * 2
     routed = dot(left, jnp.concatenate(chosen, axis=0))
     routed = routed[:32] + routed[32:]
     for pair in range(groups // 2):

time: 37.4 us -> 37.6 us (level)
  no operation moved by 1% of the time
where the time goes in v12:
time: 37.6 us; the launch traced here: 37.3 us
  blocking collectives  34.1 us (91%)
  Pallas kernels  2.36 us (6%)
  local copies, waits for them, and re-layouts  0.83 us (2%)
    all_to_all x3, blocking collectives, exchanged(): return lax.all_to_all(values, axes, split_axis=0, concat_axis=0, tiled=True)  34.1 us
    pallas_call x1, Pallas kernels, update_step(): pl.pallas_call(functools.partial(update_kernel, count), out_shape=jax.Sha...  0.99 us
    unnamed x18, local copies, waits for them, and re-layouts  0.83 us
    pallas_call x1, Pallas kernels, fine_step(): pl.pallas_call(functools.partial(fine_kernel, profiles), out_shape=jax.Sh...  0.78 us

profile of v12, /device:TPU:0, one launch (start us, length us, event | category | flops | bytes accessed | tf_op | source)
XLA Modules:
  0.0 37.3 jit_solution(17341627786878163619)
XLA Ops:
  0.0 0.0 copy-start.3
  0.0 0.0 copy-start.7
  0.0 0.0 copy-start.8
  0.0 0.1 turns.1.turn_ref
  0.1 0.0 copy-start
  0.1 0.8 %copy-done.3 = f32[1,32768]{1,0:T(1,128)S(1)} copy-done((f32[1,32768]{1,0:T(1,128)S(1)}, f32[1,32768]{1,0:T(1,128)}, u32[]{:S(2)}) %copy-start.3) | copy-done | bytes 131096
  0.9 0.0 copy-done.7
  0.9 0.0 copy-done.8
  0.9 0.1 columns.1
  1.0 14.4 %all_to_all.15 = f32[8,32,128]{2,1,0:T(8,128)S(1)} all-to-all(f32[8,32,128]{2,1,0:T(8,128)S(1)} %get-tuple-element.9), channel_id=1, replica_groups=mesh['bins'=8,'scans'=4] {'bins'}, dimensions={0} | all-to-all | bytes 262144 | tf_op jit(solution)/shard_map/all_to_all | solution.py:545
  15.5 0.0 copy-done
  15.5 0.0 copy-start.6
  15.5 0.4 coarse_dft.1
  15.8 0.0 copy-start.1
  15.9 10.4 %all_to_all.16 = f32[32,8,128]{2,1,0:T(8,128)S(1)} all-to-all(f32[32,8,128]{2,1,0:T(8,128)S(1)} %bitcast.15), channel_id=1, replica_groups=mesh['bins'=8,'scans'=4] {'bins','scans'}, dimensions={0} | all-to-all | bytes 262144 | tf_op jit(solution)/shard_map/all_to_all | solution.py:545
  26.3 0.0 copy-done.6
  26.3 0.0 copy-done.1
  26.3 0.0 copy-start.2
  26.3 0.8 %fine_dft.1 = f32[128,128]{1,0:T(8,128)S(1)} custom-call(f32[256,128]{1,0:T(8,128)S(1)} %bitcast.13, f32[32,8,128]{2,1,0:T(8,128)S(1)} %turns.1.turn_ref, s32[1,512]{1,0:T(1,128)S(1)} %get-tuple-element.10.wanted_ref, f32[32,128]{1,0:T(8,128)S(1)} %copy-done.6, bf16[512,256]{1,0:T(8,128)(2,1)S(1)} %copy-done.1), custom_call_target="tpu_custom_call" | custom-call | tf_op jit(solution)/shard_map/fine_dft/pallas_call | solution.py:385
  27.1 0.0 copy-start.4
  27.1 0.0 copy-start.5
  27.1 9.2 %all_to_all.17 = f32[32,4,128]{2,1,0:T(4,128)S(1)} all-to-all(f32[32,4,128]{2,1,0:T(4,128)S(1)} %bitcast.16), channel_id=1, replica_groups=mesh['bins'=8,'scans'=4] {'bins','scans'}, dimensions={0} | all-to-all | bytes 131072 | tf_op jit(solution)/shard_map/all_to_all | solution.py:545
  36.3 0.0 copy-done.2
  36.3 0.0 copy-done.4
  36.3 0.0 copy-done.5
  36.3 1.0 %state_update.1 = f32[64,128]{1,0:T(8,128)} custom-call(f32[128,128]{1,0:T(8,128)S(1)} %bitcast.17, bf16[336,128]{1,0:T(8,128)(2,1)S(1)} %copy-done.4, s32[1,128]{1,0:T(1,128)S(1)} %get-tuple-element.11.lane_band_ref, s32[64,128]{1,0:T(8,128)S(1)} %get-tuple-element.12.row_band_ref, f32[320,64]{1,0:T(8,128)S(1)} %bitcast.18, f32[64,128]{1,0:T(8,128)S(1)} %bitcast.20), custom_call_target="tpu_custom_call" | custom-call | tf_op jit(solution)/shard_map/state_update/pallas_call | solution.py:518
Async XLA Ops:
  0.0 0.9 %copy-start.3 = (f32[1,32768]{1,0:T(1,128)S(1)}, f32[1,32768]{1,0:T(1,128)}, u32[]{:S(2)}) copy-start(f32[1,32768]{1,0:T(1,128)} %param.9) | copy-start | bytes 393220
  0.0 0.9 %copy-start.7 = (s32[6]{0:T(128)S(1)}, s32[6]{0:T(128)}, u32[]{:S(2)}) copy-start(s32[6]{0:T(128)} %param.10) | copy-start | bytes 76
  0.0 0.9 %copy-start.8 = (s32[8]{0:T(128)S(1)}, s32[8]{0:T(128)}, u32[]{:S(2)}) copy-start(s32[8]{0:T(128)} %param.11) | copy-start | bytes 100
  0.1 15.4 %copy-start = (bf16[256,768]{1,0:T(8,128)(2,1)S(1)}, bf16[256,768]{1,0:T(8,128)(2,1)}, u32[]{:S(2)}) copy-start(bf16[256,768]{1,0:T(8,128)(2,1)} %constant.8.clone.table_ref) | copy-start | bytes 1179652
  15.5 10.8 %copy-start.6 = (f32[32,128]{1,0:T(8,128)S(1)}, f32[32,128]{1,0:T(8,128)}, u32[]{:S(2)}) copy-start(f32[32,128]{1,0:T(8,128)} %constant.9.clone.turns_ref) | copy-start | bytes 49156
  15.8 10.4 %copy-start.1 = (bf16[512,256]{1,0:T(8,128)(2,1)S(1)}, bf16[512,256]{1,0:T(8,128)(2,1)}, u32[]{:S(2)}) copy-start(bf16[512,256]{1,0:T(8,128)(2,1)} %constant.10.clone.table_ref) | copy-start | bytes 786436
  26.3 10.1 %copy-start.2 = (f32[5,64,64]{2,1,0:T(8,128)S(1)}, f32[5,64,64]{2,1,0:T(8,128)}, u32[]{:S(2)}) copy-start(f32[5,64,64]{2,1,0:T(8,128)} %param.12) | copy-start | bytes 245764
  27.1 9.3 %copy-start.4 = (bf16[336,128]{1,0:T(8,128)(2,1)S(1)}, bf16[336,128]{1,0:T(8,128)(2,1)}, u32[]{:S(2)}) copy-start(bf16[336,128]{1,0:T(8,128)(2,1)} %constant.11.clone.pool_ref) | copy-start | bytes 258052
  27.1 9.3 %copy-start.5 = (f32[64,1,128]{2,1,0:T(1,128)S(1)}, f32[64,1,128]{2,1,0:T(1,128)}, u32[]{:S(2)}) copy-start(f32[64,1,128]{2,1,0:T(1,128)} %param.13) | copy-start | bytes 98308

commit v13 on v12

--- a/solution.py
+++ b/solution.py
@@ -321,9 +321,13 @@
             rows.append(jnp.where(low_lanes, real, pltpu.roll(imag, HALF, 1)))
             if at < 2:
                 rows.append(jnp.where(low_lanes, pltpu.roll(real, HALF, 1), imag))
-    high, middle, low = split_three(jnp.concatenate(rows, axis=0))
-    product = dot(jnp.concatenate([high, middle, high, low], axis=1), table_ref[...])
-    product = product[:, :LANES] + product[:, LANES:]
+    product = []
+    for at in range(0, len(rows), len(rows) // 2):
+        part = jnp.concatenate(rows[at : at + len(rows) // 2], axis=0)
+        high, middle, low = split_three(part)
+        both = dot(jnp.concatenate([high, middle, high, low], axis=1), table_ref[...])
+        product.append(both[:, :LANES] + both[:, LANES:])
+    product = jnp.concatenate(product, axis=0)
     spectrum = []
     for u in range(groups):
         spectrum.append([product[8 * at : 8 * (at + 1)] for at in range(5 * u, 5 * (u + 1))])
@@ -495,7 +499,8 @@
     count, x_ref, pool_ref, lane_band_ref, row_band_ref, dynamics_ref, state_ref, out_ref
 ):
     band = lane_band_ref[...]
-    sums = dot(pool_ref[...], jnp.concatenate(split_two(x_ref[...]), axis=1))
+    right = jnp.concatenate(split_two(x_ref[...]), axis=1)
+    sums = jnp.concatenate([dot(pool_ref[:160], right), dot(pool_ref[160:], right)], axis=0)
     sums = sums[:, :LANES] + sums[:, LANES:]
     power = sums[NCLASS * STATES : NCLASS * STATES + 1] * (1.0 / count)
     span = jnp.left_shift(TILE // STATES, jnp.maximum(band, 0)).astype(F32)

time: 37.6 us -> 37.4 us (level)
  no operation moved by 1% of the time
where the time goes in v13:
time: 37.4 us; the launch traced here: 37.2 us
  blocking collectives  34.1 us (91%)
  Pallas kernels  2.24 us (6%)
  local copies, waits for them, and re-layouts  0.83 us (2%)
    all_to_all x3, blocking collectives, exchanged(): return lax.all_to_all(values, axes, split_axis=0, concat_axis=0, tiled=True)  34.1 us
    pallas_call x1, Pallas kernels, update_step(): pl.pallas_call(functools.partial(update_kernel, count), out_shape=jax.Sha...  0.99 us
    unnamed x18, local copies, waits for them, and re-layouts  0.83 us

profile of v13, /device:TPU:0, one launch (start us, length us, event | category | flops | bytes accessed | tf_op | source)
XLA Modules:
  0.0 37.2 jit_solution(3421446356172194106)
XLA Ops:
  0.0 0.0 copy-start.3
  0.0 0.0 copy-start.7
  0.0 0.0 copy-start.8
  0.0 0.1 turns.1.turn_ref
  0.1 0.0 copy-start
  0.1 0.8 %copy-done.3 = f32[1,32768]{1,0:T(1,128)S(1)} copy-done((f32[1,32768]{1,0:T(1,128)S(1)}, f32[1,32768]{1,0:T(1,128)}, u32[]{:S(2)}) %copy-start.3) | copy-done | bytes 131096
  0.9 0.0 copy-done.7
  0.9 0.0 copy-done.8
  0.9 0.1 columns.1
  1.0 14.4 %all_to_all.15 = f32[8,32,128]{2,1,0:T(8,128)S(1)} all-to-all(f32[8,32,128]{2,1,0:T(8,128)S(1)} %get-tuple-element.9), channel_id=1, replica_groups=mesh['bins'=8,'scans'=4] {'bins'}, dimensions={0} | all-to-all | bytes 262144 | tf_op jit(solution)/shard_map/all_to_all | solution.py:550
  15.5 0.0 copy-done
  15.5 0.0 copy-start.6
  15.5 0.4 coarse_dft.1
  15.8 0.0 copy-start.1
  15.9 10.4 %all_to_all.16 = f32[32,8,128]{2,1,0:T(8,128)S(1)} all-to-all(f32[32,8,128]{2,1,0:T(8,128)S(1)} %bitcast.15), channel_id=1, replica_groups=mesh['bins'=8,'scans'=4] {'bins','scans'}, dimensions={0} | all-to-all | bytes 262144 | tf_op jit(solution)/shard_map/all_to_all | solution.py:550
  26.3 0.0 copy-done.6
  26.3 0.0 copy-done.1
  26.3 0.0 copy-start.2
  26.3 0.7 %fine_dft.1 = f32[128,128]{1,0:T(8,128)S(1)} custom-call(f32[256,128]{1,0:T(8,128)S(1)} %bitcast.13, f32[32,8,128]{2,1,0:T(8,128)S(1)} %turns.1.turn_ref, s32[1,512]{1,0:T(1,128)S(1)} %get-tuple-element.10.wanted_ref, f32[32,128]{1,0:T(8,128)S(1)} %copy-done.6, bf16[512,256]{1,0:T(8,128)(2,1)S(1)} %copy-done.1), custom_call_target="tpu_custom_call" | custom-call | tf_op jit(solution)/shard_map/fine_dft/pallas_call | solution.py:389
  27.0 0.0 copy-start.4
  27.0 0.0 copy-start.5
  27.0 9.2 %all_to_all.17 = f32[32,4,128]{2,1,0:T(4,128)S(1)} all-to-all(f32[32,4,128]{2,1,0:T(4,128)S(1)} %bitcast.16), channel_id=1, replica_groups=mesh['bins'=8,'scans'=4] {'bins','scans'}, dimensions={0} | all-to-all | bytes 131072 | tf_op jit(solution)/shard_map/all_to_all | solution.py:550
  36.2 0.0 copy-done.2
  36.2 0.0 copy-done.4
  36.2 0.0 copy-done.5
  36.2 1.0 %state_update.1 = f32[64,128]{1,0:T(8,128)} custom-call(f32[128,128]{1,0:T(8,128)S(1)} %bitcast.17, bf16[336,128]{1,0:T(8,128)(2,1)S(1)} %copy-done.4, s32[1,128]{1,0:T(1,128)S(1)} %get-tuple-element.11.lane_band_ref, s32[64,128]{1,0:T(8,128)S(1)} %get-tuple-element.12.row_band_ref, f32[320,64]{1,0:T(8,128)S(1)} %bitcast.18, f32[64,128]{1,0:T(8,128)S(1)} %bitcast.20), custom_call_target="tpu_custom_call" | custom-call | tf_op jit(solution)/shard_map/state_update/pallas_call | solution.py:523
Async XLA Ops:
  0.0 0.9 %copy-start.3 = (f32[1,32768]{1,0:T(1,128)S(1)}, f32[1,32768]{1,0:T(1,128)}, u32[]{:S(2)}) copy-start(f32[1,32768]{1,0:T(1,128)} %param.9) | copy-start | bytes 393220
  0.0 0.9 %copy-start.7 = (s32[6]{0:T(128)S(1)}, s32[6]{0:T(128)}, u32[]{:S(2)}) copy-start(s32[6]{0:T(128)} %param.10) | copy-start | bytes 76
  0.0 0.9 %copy-start.8 = (s32[8]{0:T(128)S(1)}, s32[8]{0:T(128)}, u32[]{:S(2)}) copy-start(s32[8]{0:T(128)} %param.11) | copy-start | bytes 100
  0.1 15.4 %copy-start = (bf16[256,768]{1,0:T(8,128)(2,1)S(1)}, bf16[256,768]{1,0:T(8,128)(2,1)}, u32[]{:S(2)}) copy-start(bf16[256,768]{1,0:T(8,128)(2,1)} %constant.8.clone.table_ref) | copy-start | bytes 1179652
  15.5 10.8 %copy-start.6 = (f32[32,128]{1,0:T(8,128)S(1)}, f32[32,128]{1,0:T(8,128)}, u32[]{:S(2)}) copy-start(f32[32,128]{1,0:T(8,128)} %constant.9.clone.turns_ref) | copy-start | bytes 49156
  15.8 10.4 %copy-start.1 = (bf16[512,256]{1,0:T(8,128)(2,1)S(1)}, bf16[512,256]{1,0:T(8,128)(2,1)}, u32[]{:S(2)}) copy-start(bf16[512,256]{1,0:T(8,128)(2,1)} %constant.10.clone.table_ref) | copy-start | bytes 786436
  26.3 9.9 %copy-start.2 = (f32[5,64,64]{2,1,0:T(8,128)S(1)}, f32[5,64,64]{2,1,0:T(8,128)}, u32[]{:S(2)}) copy-start(f32[5,64,64]{2,1,0:T(8,128)} %param.12) | copy-start | bytes 245764
  27.0 9.3 %copy-start.4 = (bf16[336,128]{1,0:T(8,128)(2,1)S(1)}, bf16[336,128]{1,0:T(8,128)(2,1)}, u32[]{:S(2)}) copy-start(bf16[336,128]{1,0:T(8,128)(2,1)} %constant.11.clone.pool_ref) | copy-start | bytes 258052
  27.0 9.3 %copy-start.5 = (f32[64,1,128]{2,1,0:T(1,128)S(1)}, f32[64,1,128]{2,1,0:T(1,128)}, u32[]{:S(2)}) copy-start(f32[64,1,128]{2,1,0:T(1,128)} %param.13) | copy-start | bytes 98308

commit v14 on v13

--- a/solution.py
+++ b/solution.py
@@ -169,7 +169,9 @@
     return np.concatenate(terms, axis=1)
 
 
-def coarse_kernel(shares, x_ref, table_ref, out_ref):
+def coarse_kernel(
+    shares, x_ref, table_ref, row_band_ref, dynamics_ref, state_ref, out_ref, moved_ref
+):
     half = x_ref.shape[0]
     quarter = half // 2
     row, lane = iotas((8, LANES))
@@ -210,18 +212,28 @@
         imag = even_imag + odd_imag * cosine - odd_real * sine
         out_ref[pl.ds(8 * first, 8, stride=2), :] = real
         out_ref[pl.ds(8 * first + 1, 8, stride=2), :] = imag
-
-
-def coarse_step(columns, shares):
+    moved_ref[...] = state_product(dynamics_ref[...], state_ref[...], row_band_ref[...])
+
+
+def coarse_step(columns, row_band, dynamics, state, shares):
     half = columns.shape[0]
     return pl.pallas_call(
         functools.partial(coarse_kernel, shares),
-        out_shape=jax.ShapeDtypeStruct((half, LANES), F32),
-        in_specs=[VMEM] * 2,
-        out_specs=VMEM,
+        out_shape=(
+            jax.ShapeDtypeStruct((half, LANES), F32),
+            jax.ShapeDtypeStruct(state.shape, F32),
+        ),
+        in_specs=[VMEM] * 5,
+        out_specs=(VMEM,) * 2,
         compiler_params=PARAMS,
         name="coarse_dft",
-    )(columns, jnp.asarray(coarse_table(2 * half)))
+    )(
+        columns,
+        jnp.asarray(coarse_table(2 * half)),
+        row_band,
+        dynamics.reshape(NCLASS * STATES, STATES),
+        state,
+    )
 
 
 def coarse_step_general(columns, shares):
@@ -287,7 +299,57 @@
     return [add(e, t) for e, t in zip(even, turned)] + [sub(e, t) for e, t in zip(even, turned)]
 
 
-def fine_kernel(profiles, x_ref, turn_ref, wanted_ref, turns_ref, table_ref, out_ref):
+def state_product(dynamics, state, band):
+    row, column = iotas((NCLASS * STATES, STATES))
+    limit = STATES >> (row >> 6)
+    inside = ((row & (STATES - 1)) < limit) & (column < limit)
+    dynamics = jnp.where(inside, dynamics, 0.0)
+    empty = jnp.zeros_like(dynamics)
+    halves = [
+        jnp.concatenate([dynamics, empty], axis=1),
+        jnp.concatenate([empty, dynamics], axis=1),
+    ]
+    matrix = jnp.concatenate(
+        [half[k * STATES : (k + 1) * STATES] for k in range(NCLASS) for half in halves], axis=0
+    )
+    state_high, state_low = split_two(state)
+    high, low = split_two(matrix)
+    moved = lax.dot_general(
+        jnp.concatenate([state_high, state_low, state_high], axis=1),
+        jnp.concatenate([high, high, low], axis=1),
+        (((1,), (1,)), ((), ())),
+        preferred_element_type=F32,
+    )
+    result = jnp.zeros(state.shape, F32)
+    for k in range(NCLASS):
+        result = jnp.where(band == k, moved[:, k * LANES : (k + 1) * LANES], result)
+    return result
+
+
+def moved_kernel(row_band_ref, dynamics_ref, state_ref, out_ref):
+    out_ref[...] = state_product(dynamics_ref[...], state_ref[...], row_band_ref[...])
+
+
+def moved_step(row_band, dynamics, state):
+    return pl.pallas_call(
+        moved_kernel,
+        out_shape=jax.ShapeDtypeStruct(state.shape, F32),
+        in_specs=[VMEM] * 3,
+        out_specs=VMEM,
+        compiler_params=PARAMS,
+        name="moved",
+    )(row_band, dynamics.reshape(NCLASS * STATES, STATES), state)
+
+
+def fine_kernel(
+    profiles,
+    x_ref,
+    turn_ref,
+    wanted_ref,
+    turns_ref,
+    table_ref,
+    out_ref,
+):
     groups = turn_ref.shape[0] // 4
     first = (lax.axis_index("bins") == 0) & (lax.axis_index("scans") == 0)
     row, lane = iotas((8, LANES))
@@ -393,7 +455,13 @@
         out_specs=VMEM,
         compiler_params=PARAMS,
         name="fine_dft",
-    )(arrived, turn, wanted, jnp.asarray(turns), jnp.asarray(table))
+    )(
+        arrived,
+        turn,
+        wanted,
+        jnp.asarray(turns),
+        jnp.asarray(table),
+    )
     return out.reshape(groups * profiles, KINDS, LANES)
 
 
@@ -468,35 +536,8 @@
     return pool.reshape(-1, shares * KINDS).astype(BF16)
 
 
-def state_product(dynamics, state, band):
-    row, column = iotas((NCLASS * STATES, STATES))
-    limit = STATES >> (row >> 6)
-    inside = ((row & (STATES - 1)) < limit) & (column < limit)
-    dynamics = jnp.where(inside, dynamics, 0.0)
-    empty = jnp.zeros_like(dynamics)
-    halves = [
-        jnp.concatenate([dynamics, empty], axis=1),
-        jnp.concatenate([empty, dynamics], axis=1),
-    ]
-    matrix = jnp.concatenate(
-        [half[k * STATES : (k + 1) * STATES] for k in range(NCLASS) for half in halves], axis=0
-    )
-    state_high, state_low = split_two(state)
-    high, low = split_two(matrix)
-    moved = lax.dot_general(
-        jnp.concatenate([state_high, state_low, state_high], axis=1),
-        jnp.concatenate([high, high, low], axis=1),
-        (((1,), (1,)), ((), ())),
-        preferred_element_type=F32,
-    )
-    result = jnp.zeros(state.shape, F32)
-    for k in range(NCLASS):
-        result = jnp.where(band == k, moved[:, k * LANES : (k + 1) * LANES], result)
-    return result
-
-
 def update_kernel(
-    count, x_ref, pool_ref, lane_band_ref, row_band_ref, dynamics_ref, state_ref, out_ref
+    count, x_ref, pool_ref, lane_band_ref, moved_ref, out_ref
 ):
     band = lane_band_ref[...]
     right = jnp.concatenate(split_two(x_ref[...]), axis=1)
@@ -513,17 +554,15 @@
     turned = jnp.transpose(jnp.concatenate([chosen, chosen], axis=0))
     half = turned.shape[0] // 2
     measured = jnp.where(iotas((half, LANES))[1] < STATES, turned[:half], turned[half:])
-    out_ref[...] = measured + state_product(
-        dynamics_ref[...], state_ref[...], row_band_ref[...]
-    )
-
-
-def update_step(arrived, lane_band, row_band, dynamics, state, coarse, count):
+    out_ref[...] = measured + moved_ref[...]
+
+
+def update_step(arrived, lane_band, moved, coarse, count):
     shares = arrived.shape[0]
     return pl.pallas_call(
         functools.partial(update_kernel, count),
-        out_shape=jax.ShapeDtypeStruct(state.shape, F32),
-        in_specs=[VMEM] * 6,
+        out_shape=jax.ShapeDtypeStruct(moved.shape, F32),
+        in_specs=[VMEM] * 4,
         out_specs=VMEM,
         compiler_params=PARAMS,
         name="state_update",
@@ -531,9 +570,7 @@
         arrived.reshape(shares * KINDS, LANES),
         jnp.asarray(pool_table(shares, coarse)),
         lane_band,
-        row_band,
-        dynamics.reshape(NCLASS * STATES, STATES),
-        state,
+        moved,
     )
 
 
@@ -564,19 +601,21 @@
             profiles.reshape(length), turn, band_edges, owner_counts, capacity
         )
         columns = exchanged(columns, "bins").reshape(coarse // 2, LANES)
-        blocks = coarse_step(columns, shares)
+        blocks, moved = coarse_step(columns, row_band, dynamics, state, shares)
         blocks = exchanged(blocks.reshape(shares, 8, LANES), ("bins", "scans"))
-        payload = fine_step(blocks.reshape(8 * shares, LANES), turn, wanted, scans, coarse)
+        blocks = blocks.reshape(8 * shares, LANES)
+        payload = fine_step(blocks, turn, wanted, scans, coarse)
         arrived = exchanged(payload, ("bins", "scans"))
     else:
         lane_band, row_band = bands_general(band_edges, owner_counts, capacity)
+        moved = moved_step(row_band, dynamics, state)
         columns = profiles.reshape(coarse // groups, groups, HALF).transpose(1, 0, 2)
         columns = exchanged(columns, "bins").reshape(coarse, HALF)
         blocks = exchanged(coarse_step_general(columns, groups), "bins")
         arrived = exchanged(fine_step_general(blocks, owner_counts, capacity), "bins")
         power = lax.psum(arrived[:, 3:], "scans")
         arrived = jnp.concatenate([arrived[:, :3], power], axis=1)
-    updated = update_step(arrived, lane_band, row_band, dynamics, state, coarse, count)
+    updated = update_step(arrived, lane_band, moved, coarse, count)
     return updated.reshape(prev_state.shape)
 
 

time: 37.4 us -> 37.5 us (level)
  no operation moved by 1% of the time
where the time goes in v14:
time: 37.5 us; the launch traced here: 37.2 us
  blocking collectives  34.1 us (91%)
  Pallas kernels  2.2 us (6%)
  local copies, waits for them, and re-layouts  0.83 us (2%)
    all_to_all x3, blocking collectives, exchanged(): return lax.all_to_all(values, axes, split_axis=0, concat_axis=0, tiled=True)  34.1 us
    pallas_call x1, Pallas kernels, update_step(): pl.pallas_call(functools.partial(update_kernel, count), out_shape=jax.Sha...  0.93 us
    unnamed x18, local copies, waits for them, and re-layouts  0.83 us

profile of v14, /device:TPU:0, one launch (start us, length us, event | category | flops | bytes accessed | tf_op | source)
XLA Modules:
  0.0 37.2 jit_solution(11614380394734472927)
XLA Ops:
  0.0 0.0 copy-start.3
  0.0 0.0 copy-start.7
  0.0 0.0 copy-start.8
  0.0 0.0 copy-start.2
  0.0 0.1 turns.1.turn_ref
  0.1 0.0 copy-start
  0.1 0.8 %copy-done.3 = f32[1,32768]{1,0:T(1,128)S(1)} copy-done((f32[1,32768]{1,0:T(1,128)S(1)}, f32[1,32768]{1,0:T(1,128)}, u32[]{:S(2)}) %copy-start.3) | copy-done | bytes 131096
  0.9 0.0 copy-done.7
  0.9 0.0 copy-done.8
  0.9 0.1 columns.1
  1.0 0.0 copy-start.5
  1.1 14.4 %all_to_all.15 = f32[8,32,128]{2,1,0:T(8,128)S(1)} all-to-all(f32[8,32,128]{2,1,0:T(8,128)S(1)} %get-tuple-element.11), channel_id=1, replica_groups=mesh['bins'=8,'scans'=4] {'bins'}, dimensions={0} | all-to-all | bytes 262144 | tf_op jit(solution)/shard_map/all_to_all | solution.py:587
  15.5 0.0 copy-done.2
  15.5 0.0 copy-done
  15.5 0.0 copy-done.5
  15.5 0.0 copy-start.6
  15.5 0.4 %coarse_dft.1 = (f32[256,128]{1,0:T(8,128)S(1)}, f32[64,128]{1,0:T(8,128)S(1)}) custom-call(f32[256,128]{1,0:T(8,128)S(1)} %bitcast.14, bf16[256,768]{1,0:T(8,128)(2,1)S(1)} %copy-done, s32[64,128]{1,0:T(8,128)S(1)} %get-tuple-element.12.row_band_ref, f32[320,64]{1,0:T(8,128)S(1)} %bitcast.17, f32[64,128]{1,0:T(8,128)S(1)} %bitcast.20), custom_call_target="tpu_custom_call" | custom-call | tf_op jit(solution)/shard_map/coarse_dft/pallas_call | solution.py:220
  15.9 0.0 copy-start.1
  15.9 10.4 %all_to_all.16 = f32[32,8,128]{2,1,0:T(8,128)S(1)} all-to-all(f32[32,8,128]{2,1,0:T(8,128)S(1)} %bitcast.19), channel_id=1, replica_groups=mesh['bins'=8,'scans'=4] {'bins','scans'}, dimensions={0} | all-to-all | bytes 262144 | tf_op jit(solution)/shard_map/all_to_all | solution.py:587
  26.3 0.0 copy-done.6
  26.3 0.0 copy-done.1
  26.3 0.7 %fine_dft.1 = f32[128,128]{1,0:T(8,128)S(1)} custom-call(f32[256,128]{1,0:T(8,128)S(1)} %bitcast.13, f32[32,8,128]{2,1,0:T(8,128)S(1)} %turns.1.turn_ref, s32[1,512]{1,0:T(1,128)S(1)} %get-tuple-element.14.wanted_ref, f32[32,128]{1,0:T(8,128)S(1)} %copy-done.6, bf16[512,256]{1,0:T(8,128)(2,1)S(1)} %copy-done.1), custom_call_target="tpu_custom_call" | custom-call | tf_op jit(solution)/shard_map/fine_dft/pallas_call | solution.py:451
  27.0 0.0 copy-start.4
  27.0 9.2 %all_to_all.17 = f32[32,4,128]{2,1,0:T(4,128)S(1)} all-to-all(f32[32,4,128]{2,1,0:T(4,128)S(1)} %bitcast.15), channel_id=1, replica_groups=mesh['bins'=8,'scans'=4] {'bins','scans'}, dimensions={0} | all-to-all | bytes 131072 | tf_op jit(solution)/shard_map/all_to_all | solution.py:587
  36.2 0.0 copy-done.4
  36.2 0.9 %state_update.1 = f32[64,128]{1,0:T(8,128)} custom-call(f32[128,128]{1,0:T(8,128)S(1)} %bitcast.16, bf16[336,128]{1,0:T(8,128)(2,1)S(1)} %copy-done.4, s32[1,128]{1,0:T(1,128)S(1)} %get-tuple-element.15.lane_band_ref, f32[64,128]{1,0:T(8,128)S(1)} %get-tuple-element.16.moved_ref), custom_call_target="tpu_custom_call" | custom-call | tf_op jit(solution)/shard_map/state_update/pallas_call | solution.py:562
Async XLA Ops:
  0.0 0.9 %copy-start.3 = (f32[1,32768]{1,0:T(1,128)S(1)}, f32[1,32768]{1,0:T(1,128)}, u32[]{:S(2)}) copy-start(f32[1,32768]{1,0:T(1,128)} %param.9) | copy-start | bytes 393220
  0.0 0.9 %copy-start.7 = (s32[6]{0:T(128)S(1)}, s32[6]{0:T(128)}, u32[]{:S(2)}) copy-start(s32[6]{0:T(128)} %param.10) | copy-start | bytes 76
  0.0 0.9 %copy-start.8 = (s32[8]{0:T(128)S(1)}, s32[8]{0:T(128)}, u32[]{:S(2)}) copy-start(s32[8]{0:T(128)} %param.11) | copy-start | bytes 100
  0.0 15.5 %copy-start.2 = (f32[5,64,64]{2,1,0:T(8,128)S(1)}, f32[5,64,64]{2,1,0:T(8,128)}, u32[]{:S(2)}) copy-start(f32[5,64,64]{2,1,0:T(8,128)} %param.12) | copy-start | bytes 245764
  0.1 15.4 %copy-start = (bf16[256,768]{1,0:T(8,128)(2,1)S(1)}, bf16[256,768]{1,0:T(8,128)(2,1)}, u32[]{:S(2)}) copy-start(bf16[256,768]{1,0:T(8,128)(2,1)} %constant.8.clone.table_ref) | copy-start | bytes 1179652
  1.0 14.4 %copy-start.5 = (f32[64,1,128]{2,1,0:T(1,128)S(1)}, f32[64,1,128]{2,1,0:T(1,128)}, u32[]{:S(2)}) copy-start(f32[64,1,128]{2,1,0:T(1,128)} %param.13) | copy-start | bytes 98308
  15.5 10.8 %copy-start.6 = (f32[32,128]{1,0:T(8,128)S(1)}, f32[32,128]{1,0:T(8,128)}, u32[]{:S(2)}) copy-start(f32[32,128]{1,0:T(8,128)} %constant.9.clone.turns_ref) | copy-start | bytes 49156
  15.9 10.4 %copy-start.1 = (bf16[512,256]{1,0:T(8,128)(2,1)S(1)}, bf16[512,256]{1,0:T(8,128)(2,1)}, u32[]{:S(2)}) copy-start(bf16[512,256]{1,0:T(8,128)(2,1)} %constant.10.clone.table_ref) | copy-start | bytes 786436
  27.0 9.3 %copy-start.4 = (bf16[336,128]{1,0:T(8,128)(2,1)S(1)}, bf16[336,128]{1,0:T(8,128)(2,1)}, u32[]{:S(2)}) copy-start(bf16[336,128]{1,0:T(8,128)(2,1)} %constant.11.clone.pool_ref) | copy-start | bytes 258052

commit v15 on v14

--- a/solution.py
+++ b/solution.py
@@ -100,21 +100,53 @@
     )()
 
 
-def columns_kernel(
-    x_ref, turn_ref, edges_ref, counts_ref, out_ref, wanted_ref, lane_band_ref, row_band_ref
-):
+def columns_kernel(x_ref, turn_ref, edges_ref, counts_ref, out_ref, whole_ref):
     del turn_ref
     groups, rows, _ = out_ref.shape
-    capacity = row_band_ref.shape[0]
     low_lanes = iotas((rows, LANES))[1] < HALF
     for pair in range(groups // 2):
         even = x_ref[pl.ds(pair, rows, stride=groups), :]
         odd = x_ref[pl.ds(groups // 2 + pair, rows, stride=groups), :]
         out_ref[2 * pair] = jnp.where(low_lanes, even, pltpu.roll(odd, HALF, 1))
         out_ref[2 * pair + 1] = jnp.where(low_lanes, pltpu.roll(even, HALF, 1), odd)
+    whole_ref[:, : NCLASS + 1] = edges_ref[...]
+    whole_ref[:, 8 : 8 + groups] = counts_ref[...]
+
+
+def columns_step(profile, turn, band_edges, owner_counts):
+    groups = owner_counts.shape[0]
+    rows = profile.shape[0] // (groups * LANES)
+    return pl.pallas_call(
+        columns_kernel,
+        out_shape=(
+            jax.ShapeDtypeStruct((groups, rows, LANES), F32),
+            jax.ShapeDtypeStruct((1, LANES), jnp.int32),
+        ),
+        in_specs=[VMEM] * 4,
+        out_specs=(VMEM,) * 2,
+        compiler_params=PARAMS,
+        name="columns",
+    )(profile.reshape(-1, LANES), turn, band_edges.reshape(1, -1), owner_counts.reshape(1, -1))
+
+
+def coarse_table(coarse):
+    half, quarter = coarse // 2, coarse // 4
+    k_index = np.arange(quarter)
+    a_index = np.concatenate([np.arange(0, half, 2), np.arange(1, half, 2)])
+    real, imag = unit_root(half, k_index[:, None] * a_index[None, :])
+    imag[0] = 1
+    parts = [part.reshape(quarter // 16, 2, 2, 1, 4, half) for part in (real, imag)]
+    parts = np.concatenate(parts, axis=3).transpose(0, 2, 3, 1, 4, 5)
+    high, middle, low = three_terms(parts.reshape(half, half))
+    terms = [term[:, at : at + quarter] for at in (0, quarter) for term in (middle, high, low)]
+    return np.concatenate(terms, axis=1)
+
+
+def slot_bands(groups, whole_ref, wanted_ref, lane_band_ref, row_band_ref):
+    capacity = row_band_ref.shape[0]
     own = lax.axis_index("bins")
     counts = [
-        jnp.broadcast_to(counts_ref[:, owner : owner + 1], (1, LANES)) for owner in range(groups)
+        jnp.broadcast_to(whole_ref[:, 8 + owner : 9 + owner], (1, LANES)) for owner in range(groups)
     ]
     lane = iotas((1, LANES))[1]
     rank = lane & (capacity - 1)
@@ -130,7 +162,7 @@
         wanted_ref[:, pair * LANES : (pair + 1) * LANES] = jnp.where(
             lane < HALF, wanted[2 * pair], wanted[2 * pair + 1]
         )
-    edges = [jnp.broadcast_to(edges_ref[:, at : at + 1], (1, LANES)) for at in range(1, NCLASS)]
+    edges = [jnp.broadcast_to(whole_ref[:, at : at + 1], (1, LANES)) for at in range(1, NCLASS)]
     for ref, slot in ((lane_band_ref, rank), (row_band_ref, iotas((capacity, LANES))[0])):
         band = jnp.zeros_like(slot)
         for edge in edges:
@@ -138,40 +170,21 @@
         ref[...] = jnp.where(slot < own_count, band, -1)
 
 
-def columns_step(profile, turn, band_edges, owner_counts, capacity):
-    groups = owner_counts.shape[0]
-    rows = profile.shape[0] // (groups * LANES)
-    return pl.pallas_call(
-        columns_kernel,
-        out_shape=(
-            jax.ShapeDtypeStruct((groups, rows, LANES), F32),
-            jax.ShapeDtypeStruct((1, groups * capacity), jnp.int32),
-            jax.ShapeDtypeStruct((1, LANES), jnp.int32),
-            jax.ShapeDtypeStruct((capacity, LANES), jnp.int32),
-        ),
-        in_specs=[VMEM] * 4,
-        out_specs=(VMEM,) * 4,
-        compiler_params=PARAMS,
-        name="columns",
-    )(profile.reshape(-1, LANES), turn, band_edges.reshape(1, -1), owner_counts.reshape(1, -1))
-
-
-def coarse_table(coarse):
-    half, quarter = coarse // 2, coarse // 4
-    k_index = np.arange(quarter)
-    a_index = np.concatenate([np.arange(0, half, 2), np.arange(1, half, 2)])
-    real, imag = unit_root(half, k_index[:, None] * a_index[None, :])
-    imag[0] = 1
-    parts = [part.reshape(quarter // 16, 2, 2, 1, 4, half) for part in (real, imag)]
-    parts = np.concatenate(parts, axis=3).transpose(0, 2, 3, 1, 4, 5)
-    high, middle, low = three_terms(parts.reshape(half, half))
-    terms = [term[:, at : at + quarter] for at in (0, quarter) for term in (middle, high, low)]
-    return np.concatenate(terms, axis=1)
-
-
 def coarse_kernel(
-    shares, x_ref, table_ref, row_band_ref, dynamics_ref, state_ref, out_ref, moved_ref
+    groups,
+    shares,
+    x_ref,
+    table_ref,
+    whole_ref,
+    dynamics_ref,
+    state_ref,
+    out_ref,
+    moved_ref,
+    wanted_ref,
+    lane_band_ref,
+    row_band_ref,
 ):
+    slot_bands(groups, whole_ref, wanted_ref, lane_band_ref, row_band_ref)
     half = x_ref.shape[0]
     quarter = half // 2
     row, lane = iotas((8, LANES))
@@ -215,22 +228,26 @@
     moved_ref[...] = state_product(dynamics_ref[...], state_ref[...], row_band_ref[...])
 
 
-def coarse_step(columns, row_band, dynamics, state, shares):
+def coarse_step(columns, whole, dynamics, state, groups, shares):
+    capacity = state.shape[0]
     half = columns.shape[0]
     return pl.pallas_call(
-        functools.partial(coarse_kernel, shares),
+        functools.partial(coarse_kernel, groups, shares),
         out_shape=(
             jax.ShapeDtypeStruct((half, LANES), F32),
             jax.ShapeDtypeStruct(state.shape, F32),
+            jax.ShapeDtypeStruct((1, groups * capacity), jnp.int32),
+            jax.ShapeDtypeStruct((1, LANES), jnp.int32),
         ),
         in_specs=[VMEM] * 5,
-        out_specs=(VMEM,) * 2,
+        out_specs=(VMEM,) * 4,
+        scratch_shapes=[pltpu.VMEM((capacity, LANES), jnp.int32)],
         compiler_params=PARAMS,
         name="coarse_dft",
     )(
         columns,
         jnp.asarray(coarse_table(2 * half)),
-        row_band,
+        whole,
         dynamics.reshape(NCLASS * STATES, STATES),
         state,
     )
@@ -523,7 +540,7 @@
 
 def pool_table(shares, coarse):
     pool = np.zeros((21, 16, shares, KINDS), np.float32)
-    sums = pool[:20].reshape(NCLASS, STATES, shares, KINDS)
+    sums = pool[1:].reshape(NCLASS, STATES, shares, KINDS)
     wide = TILE // STATES
     rows = coarse // 2 // shares
     for share in range(shares):
@@ -532,7 +549,7 @@
         for kind, at in enumerate((first, rest, coarse - first - 1)):
             for band in range(NCLASS):
                 sums[band, at // wide >> band, share, kind] = 1.0
-    pool[20, :, :, 3] = 1.0
+    pool[0, :, :, 3] = 1.0
     return pool.reshape(-1, shares * KINDS).astype(BF16)
 
 
@@ -541,11 +558,12 @@
 ):
     band = lane_band_ref[...]
     right = jnp.concatenate(split_two(x_ref[...]), axis=1)
-    sums = jnp.concatenate([dot(pool_ref[:160], right), dot(pool_ref[160:], right)], axis=0)
+    sums = jnp.concatenate([dot(pool_ref[:176], right), dot(pool_ref[176:], right)], axis=0)
     sums = sums[:, :LANES] + sums[:, LANES:]
-    power = sums[NCLASS * STATES : NCLASS * STATES + 1] * (1.0 / count)
+    power = sums[:1] * (1.0 / count)
+    sums = sums[16:]
     span = jnp.left_shift(TILE // STATES, jnp.maximum(band, 0)).astype(F32)
-    scaling = 1.0 / jnp.sqrt(span * (power + EPSILON))
+    scaling = lax.rsqrt(span * (power + EPSILON))
     scaling = jnp.where(band < 0, 0.0, scaling)
     chosen = sums[:STATES]
     for k in range(1, NCLASS):
@@ -597,11 +615,11 @@
     state = prev_state.reshape(capacity, 2 * STATES)
     if groups == 8 and scans == 4 and coarse == 16 * shares and capacity == HALF:
         turn = turns_step(groups, groups * length)
-        columns, wanted, lane_band, row_band = columns_step(
-            profiles.reshape(length), turn, band_edges, owner_counts, capacity
+        columns, whole = columns_step(profiles.reshape(length), turn, band_edges, owner_counts)
+        columns = exchanged(columns, "bins").reshape(coarse // 2, LANES)
+        blocks, moved, wanted, lane_band = coarse_step(
+            columns, whole, dynamics, state, groups, shares
         )
-        columns = exchanged(columns, "bins").reshape(coarse // 2, LANES)
-        blocks, moved = coarse_step(columns, row_band, dynamics, state, shares)
         blocks = exchanged(blocks.reshape(shares, 8, LANES), ("bins", "scans"))
         blocks = blocks.reshape(8 * shares, LANES)
         payload = fine_step(blocks, turn, wanted, scans, coarse)

time: 37.5 us -> 37.4 us (level)
  no operation moved by 1% of the time
where the time goes in v15:
time: 37.4 us; the launch traced here: 37.1 us
  blocking collectives  34.1 us (91%)
  Pallas kernels  2.15 us (6%)
  local copies, waits for them, and re-layouts  0.83 us (2%)
    all_to_all x3, blocking collectives, exchanged(): return lax.all_to_all(values, axes, split_axis=0, concat_axis=0, tiled=True)  34.1 us
    pallas_call x1, Pallas kernels, update_step(): pl.pallas_call(functools.partial(update_kernel, count), out_shape=jax.Sha...  0.91 us
    unnamed x18, local copies, waits for them, and re-layouts  0.83 us

profile of v15, /device:TPU:0, one launch (start us, length us, event | category | flops | bytes accessed | tf_op | source)
XLA Modules:
  0.0 37.1 jit_solution(9708774325076985187)
XLA Ops:
  0.0 0.0 copy-start.3
  0.0 0.0 copy-start.7
  0.0 0.0 copy-start.8
  0.0 0.0 copy-start.2
  0.0 0.1 turns.1.turn_ref
  0.1 0.0 copy-start
  0.1 0.8 %copy-done.3 = f32[1,32768]{1,0:T(1,128)S(1)} copy-done((f32[1,32768]{1,0:T(1,128)S(1)}, f32[1,32768]{1,0:T(1,128)}, u32[]{:S(2)}) %copy-start.3) | copy-done | bytes 131096
  0.9 0.0 copy-done.7
  0.9 0.0 copy-done.8
  0.9 0.1 columns.1
  1.0 0.0 copy-start.5
  1.0 14.4 %all_to_all.15 = f32[8,32,128]{2,1,0:T(8,128)S(1)} all-to-all(f32[8,32,128]{2,1,0:T(8,128)S(1)} %get-tuple-element.11), channel_id=1, replica_groups=mesh['bins'=8,'scans'=4] {'bins'}, dimensions={0} | all-to-all | bytes 262144 | tf_op jit(solution)/shard_map/all_to_all | solution.py:605
  15.5 0.0 copy-done.2
  15.5 0.0 copy-done
  15.5 0.0 copy-done.5
  15.5 0.0 copy-start.6
  15.5 0.4 %coarse_dft.1 = (f32[256,128]{1,0:T(8,128)S(1)}, f32[64,128]{1,0:T(8,128)S(1)}, s32[1,512]{1,0:T(1,128)S(1)}, s32[1,128]{1,0:T(1,128)S(1)}) custom-call(f32[256,128]{1,0:T(8,128)S(1)} %bitcast.13, bf16[256,768]{1,0:T(8,128)(2,1)S(1)} %copy-done, s32[1,128]{1,0:T(1,128)S(1)} %get-tuple-element.12.whole_ref, f32[320,64]{1,0:T(8,128)S(1)} %bitcast.17, ...), custom_call_target="tpu_custom_call" | custom-call | tf_op jit(solution)/shard_map/coarse_dft/pallas_call | solution.py:234
  15.9 0.0 copy-start.1
  15.9 10.4 %all_to_all.16 = f32[32,8,128]{2,1,0:T(8,128)S(1)} all-to-all(f32[32,8,128]{2,1,0:T(8,128)S(1)} %bitcast.19), channel_id=1, replica_groups=mesh['bins'=8,'scans'=4] {'bins','scans'}, dimensions={0} | all-to-all | bytes 262144 | tf_op jit(solution)/shard_map/all_to_all | solution.py:605
  26.3 0.0 copy-done.6
  26.3 0.0 copy-done.1
  26.3 0.7 %fine_dft.1 = f32[128,128]{1,0:T(8,128)S(1)} custom-call(f32[256,128]{1,0:T(8,128)S(1)} %bitcast.14, f32[32,8,128]{2,1,0:T(8,128)S(1)} %turns.1.turn_ref, s32[1,512]{1,0:T(1,128)S(1)} %get-tuple-element.14.wanted_ref, f32[32,128]{1,0:T(8,128)S(1)} %copy-done.6, bf16[512,256]{1,0:T(8,128)(2,1)S(1)} %copy-done.1), custom_call_target="tpu_custom_call" | custom-call | tf_op jit(solution)/shard_map/fine_dft/pallas_call | solution.py:468
  27.0 0.0 copy-start.4
  27.0 9.2 %all_to_all.17 = f32[32,4,128]{2,1,0:T(4,128)S(1)} all-to-all(f32[32,4,128]{2,1,0:T(4,128)S(1)} %bitcast.15), channel_id=1, replica_groups=mesh['bins'=8,'scans'=4] {'bins','scans'}, dimensions={0} | all-to-all | bytes 131072 | tf_op jit(solution)/shard_map/all_to_all | solution.py:605
  36.2 0.0 copy-done.4
  36.2 0.9 %state_update.1 = f32[64,128]{1,0:T(8,128)} custom-call(f32[128,128]{1,0:T(8,128)S(1)} %bitcast.16, bf16[336,128]{1,0:T(8,128)(2,1)S(1)} %copy-done.4, s32[1,128]{1,0:T(1,128)S(1)} %get-tuple-element.15.lane_band_ref, f32[64,128]{1,0:T(8,128)S(1)} %get-tuple-element.16.moved_ref), custom_call_target="tpu_custom_call" | custom-call | tf_op jit(solution)/shard_map/state_update/pallas_call | solution.py:580
Async XLA Ops:
  0.0 0.9 %copy-start.3 = (f32[1,32768]{1,0:T(1,128)S(1)}, f32[1,32768]{1,0:T(1,128)}, u32[]{:S(2)}) copy-start(f32[1,32768]{1,0:T(1,128)} %param.9) | copy-start | bytes 393220
  0.0 0.9 %copy-start.7 = (s32[6]{0:T(128)S(1)}, s32[6]{0:T(128)}, u32[]{:S(2)}) copy-start(s32[6]{0:T(128)} %param.10) | copy-start | bytes 76
  0.0 0.9 %copy-start.8 = (s32[8]{0:T(128)S(1)}, s32[8]{0:T(128)}, u32[]{:S(2)}) copy-start(s32[8]{0:T(128)} %param.11) | copy-start | bytes 100
  0.0 15.4 %copy-start.2 = (f32[5,64,64]{2,1,0:T(8,128)S(1)}, f32[5,64,64]{2,1,0:T(8,128)}, u32[]{:S(2)}) copy-start(f32[5,64,64]{2,1,0:T(8,128)} %param.12) | copy-start | bytes 245764
  0.1 15.3 %copy-start = (bf16[256,768]{1,0:T(8,128)(2,1)S(1)}, bf16[256,768]{1,0:T(8,128)(2,1)}, u32[]{:S(2)}) copy-start(bf16[256,768]{1,0:T(8,128)(2,1)} %constant.8.clone.table_ref) | copy-start | bytes 1179652
  1.0 14.4 %copy-start.5 = (f32[64,1,128]{2,1,0:T(1,128)S(1)}, f32[64,1,128]{2,1,0:T(1,128)}, u32[]{:S(2)}) copy-start(f32[64,1,128]{2,1,0:T(1,128)} %param.13) | copy-start | bytes 98308
  15.5 10.8 %copy-start.6 = (f32[32,128]{1,0:T(8,128)S(1)}, f32[32,128]{1,0:T(8,128)}, u32[]{:S(2)}) copy-start(f32[32,128]{1,0:T(8,128)} %constant.9.clone.turns_ref) | copy-start | bytes 49156
  15.9 10.4 %copy-start.1 = (bf16[512,256]{1,0:T(8,128)(2,1)S(1)}, bf16[512,256]{1,0:T(8,128)(2,1)}, u32[]{:S(2)}) copy-start(bf16[512,256]{1,0:T(8,128)(2,1)} %constant.10.clone.table_ref) | copy-start | bytes 786436
  27.0 9.3 %copy-start.4 = (bf16[336,128]{1,0:T(8,128)(2,1)S(1)}, bf16[336,128]{1,0:T(8,128)(2,1)}, u32[]{:S(2)}) copy-start(bf16[336,128]{1,0:T(8,128)(2,1)} %constant.11.clone.pool_ref) | copy-start | bytes 258052

commit v16 on v15

--- a/solution.py
+++ b/solution.py
@@ -79,6 +79,12 @@
     return [lax.broadcasted_iota(jnp.int32, shape, axis) for axis in range(len(shape))]
 
 
+def halves(one, two):
+    low_lanes = iotas(one.shape)[1] < HALF
+    crossed = pltpu.roll(jnp.where(low_lanes, two, one), HALF, 1)
+    return jnp.where(low_lanes, one, crossed), jnp.where(low_lanes, crossed, two)
+
+
 def turns_kernel(order, turn_ref):
     row, lane = iotas((8, LANES))
     own = lax.axis_index("bins") * lax.axis_size("scans") + lax.axis_index("scans")
@@ -103,12 +109,10 @@
 def columns_kernel(x_ref, turn_ref, edges_ref, counts_ref, out_ref, whole_ref):
     del turn_ref
     groups, rows, _ = out_ref.shape
-    low_lanes = iotas((rows, LANES))[1] < HALF
     for pair in range(groups // 2):
         even = x_ref[pl.ds(pair, rows, stride=groups), :]
         odd = x_ref[pl.ds(groups // 2 + pair, rows, stride=groups), :]
-        out_ref[2 * pair] = jnp.where(low_lanes, even, pltpu.roll(odd, HALF, 1))
-        out_ref[2 * pair + 1] = jnp.where(low_lanes, pltpu.roll(even, HALF, 1), odd)
+        out_ref[2 * pair], out_ref[2 * pair + 1] = halves(even, odd)
     whole_ref[:, : NCLASS + 1] = edges_ref[...]
     whole_ref[:, 8 : 8 + groups] = counts_ref[...]
 
@@ -211,10 +215,8 @@
         real_low, imag_low, real_high, imag_high = pieces
         if block == 0 and sign < 0:
             imag_low = jnp.where(row == 0, 0.0, imag_low)
-        even_real = jnp.where(low_lanes, real_low, pltpu.roll(real_high, HALF, 1))
-        even_imag = jnp.where(low_lanes, imag_low, pltpu.roll(imag_high, HALF, 1))
-        odd_real = jnp.where(low_lanes, pltpu.roll(real_low, HALF, 1), real_high)
-        odd_imag = jnp.where(low_lanes, pltpu.roll(imag_low, HALF, 1), imag_high)
+        even_real, odd_real = halves(real_low, real_high)
+        even_imag, odd_imag = halves(imag_low, imag_high)
         first = 2 * block + (0 if sign > 0 else shares // 2)
         angle = math.pi * 8 * first / half
         cosine = base_cosine * math.cos(angle) - base_sine * math.sin(angle)
@@ -396,10 +398,7 @@
     rows = []
     for u in range(groups):
         for at in range(3):
-            real, imag = blocks[u][at]
-            rows.append(jnp.where(low_lanes, real, pltpu.roll(imag, HALF, 1)))
-            if at < 2:
-                rows.append(jnp.where(low_lanes, pltpu.roll(real, HALF, 1), imag))
+            rows += halves(*blocks[u][at])[: 2 if at < 2 else 1]
     product = []
     for at in range(0, len(rows), len(rows) // 2):
         part = jnp.concatenate(rows[at : at + len(rows) // 2], axis=0)
@@ -433,8 +432,7 @@
     for u in range(0, groups, 2):
         for at in range(2):
             one, two = pieces[u][at], pieces[u + 1][at]
-            real = jnp.where(low_lanes, one, pltpu.roll(two, HALF, 1))
-            imag = jnp.where(low_lanes, pltpu.roll(one, HALF, 1), two)
+            real, imag = halves(one, two)
             if at == 1:
                 power = real + imag
                 real, imag = jnp.where(even, real, power), jnp.where(even, imag, power)
@@ -454,12 +452,9 @@
             real = routed[8 * at : 8 * (at + 1), pair * LANES : (pair + 1) * LANES]
             imag = routed[16 + 8 * at : 16 + 8 * (at + 1), pair * LANES : (pair + 1) * LANES]
             start = 2 * pair * profiles * KINDS + at
-            out_ref[pl.ds(start, 8, stride=2), :] = jnp.where(
-                low_lanes, real, pltpu.roll(imag, HALF, 1)
-            )
-            out_ref[pl.ds(start + profiles * KINDS, 8, stride=2), :] = jnp.where(
-                low_lanes, pltpu.roll(real, HALF, 1), imag
-            )
+            one, two = halves(real, imag)
+            out_ref[pl.ds(start, 8, stride=2), :] = one
+            out_ref[pl.ds(start + profiles * KINDS, 8, stride=2), :] = two
 
 
 def fine_step(arrived, turn, wanted, profiles, coarse):

time: 37.4 us -> 37.4 us (level)
  no operation moved by 1% of the time
where the time goes in v16:
time: 37.4 us; the launch traced here: 37.1 us
  blocking collectives  34.1 us (91%)
  Pallas kernels  2.12 us (6%)
  local copies, waits for them, and re-layouts  0.84 us (2%)
    all_to_all x3, blocking collectives, exchanged(): return lax.all_to_all(values, axes, split_axis=0, concat_axis=0, tiled=True)  34.1 us
    pallas_call x1, Pallas kernels, update_step(): pl.pallas_call(functools.partial(update_kernel, count), out_shape=jax.Sha...  0.91 us
    unnamed x18, local copies, waits for them, and re-layouts  0.84 us

profile of v16, /device:TPU:0, one launch (start us, length us, event | category | flops | bytes accessed | tf_op | source)
XLA Modules:
  0.0 37.1 jit_solution(3537413691145598703)
XLA Ops:
  0.0 0.0 copy-start.3
  0.0 0.0 copy-start.7
  0.0 0.0 copy-start.8
  0.0 0.0 copy-start.2
  0.0 0.1 turns.1.turn_ref
  0.1 0.0 copy-start
  0.1 0.8 %copy-done.3 = f32[1,32768]{1,0:T(1,128)S(1)} copy-done((f32[1,32768]{1,0:T(1,128)S(1)}, f32[1,32768]{1,0:T(1,128)}, u32[]{:S(2)}) %copy-start.3) | copy-done | bytes 131096
  0.9 0.0 copy-done.7
  0.9 0.0 copy-done.8
  0.9 0.1 columns.1
  1.0 0.0 copy-start.5
  1.0 14.4 %all_to_all.15 = f32[8,32,128]{2,1,0:T(8,128)S(1)} all-to-all(f32[8,32,128]{2,1,0:T(8,128)S(1)} %get-tuple-element.11), channel_id=1, replica_groups=mesh['bins'=8,'scans'=4] {'bins'}, dimensions={0} | all-to-all | bytes 262144 | tf_op jit(solution)/shard_map/all_to_all | solution.py:600
  15.4 0.0 copy-done.2
  15.4 0.0 copy-done
  15.4 0.0 copy-done.5
  15.4 0.0 copy-start.6
  15.5 0.4 %coarse_dft.1 = (f32[256,128]{1,0:T(8,128)S(1)}, f32[64,128]{1,0:T(8,128)S(1)}, s32[1,512]{1,0:T(1,128)S(1)}, s32[1,128]{1,0:T(1,128)S(1)}) custom-call(f32[256,128]{1,0:T(8,128)S(1)} %bitcast.13, bf16[256,768]{1,0:T(8,128)(2,1)S(1)} %copy-done, s32[1,128]{1,0:T(1,128)S(1)} %get-tuple-element.12.whole_ref, f32[320,64]{1,0:T(8,128)S(1)} %bitcast.17, ...), custom_call_target="tpu_custom_call" | custom-call | tf_op jit(solution)/shard_map/coarse_dft/pallas_call | solution.py:236
  15.8 0.0 copy-start.1
  15.9 10.4 %all_to_all.16 = f32[32,8,128]{2,1,0:T(8,128)S(1)} all-to-all(f32[32,8,128]{2,1,0:T(8,128)S(1)} %bitcast.19), channel_id=1, replica_groups=mesh['bins'=8,'scans'=4] {'bins','scans'}, dimensions={0} | all-to-all | bytes 262144 | tf_op jit(solution)/shard_map/all_to_all | solution.py:600
  26.3 0.0 copy-done.6
  26.3 0.0 copy-done.1
  26.3 0.7 %fine_dft.1 = f32[128,128]{1,0:T(8,128)S(1)} custom-call(f32[256,128]{1,0:T(8,128)S(1)} %bitcast.14, f32[32,8,128]{2,1,0:T(8,128)S(1)} %turns.1.turn_ref, s32[1,512]{1,0:T(1,128)S(1)} %get-tuple-element.14.wanted_ref, f32[32,128]{1,0:T(8,128)S(1)} %copy-done.6, bf16[512,256]{1,0:T(8,128)(2,1)S(1)} %copy-done.1), custom_call_target="tpu_custom_call" | custom-call | tf_op jit(solution)/shard_map/fine_dft/pallas_call | solution.py:463
  26.9 0.0 copy-start.4
  27.0 9.2 %all_to_all.17 = f32[32,4,128]{2,1,0:T(4,128)S(1)} all-to-all(f32[32,4,128]{2,1,0:T(4,128)S(1)} %bitcast.15), channel_id=1, replica_groups=mesh['bins'=8,'scans'=4] {'bins','scans'}, dimensions={0} | all-to-all | bytes 131072 | tf_op jit(solution)/shard_map/all_to_all | solution.py:600
  36.2 0.0 copy-done.4
  36.2 0.9 %state_update.1 = f32[64,128]{1,0:T(8,128)} custom-call(f32[128,128]{1,0:T(8,128)S(1)} %bitcast.16, bf16[336,128]{1,0:T(8,128)(2,1)S(1)} %copy-done.4, s32[1,128]{1,0:T(1,128)S(1)} %get-tuple-element.15.lane_band_ref, f32[64,128]{1,0:T(8,128)S(1)} %get-tuple-element.16.moved_ref), custom_call_target="tpu_custom_call" | custom-call | tf_op jit(solution)/shard_map/state_update/pallas_call | solution.py:575
Async XLA Ops:
  0.0 0.9 %copy-start.3 = (f32[1,32768]{1,0:T(1,128)S(1)}, f32[1,32768]{1,0:T(1,128)}, u32[]{:S(2)}) copy-start(f32[1,32768]{1,0:T(1,128)} %param.9) | copy-start | bytes 393220
  0.0 0.9 %copy-start.7 = (s32[6]{0:T(128)S(1)}, s32[6]{0:T(128)}, u32[]{:S(2)}) copy-start(s32[6]{0:T(128)} %param.10) | copy-start | bytes 76
  0.0 0.9 %copy-start.8 = (s32[8]{0:T(128)S(1)}, s32[8]{0:T(128)}, u32[]{:S(2)}) copy-start(s32[8]{0:T(128)} %param.11) | copy-start | bytes 100
  0.0 15.4 %copy-start.2 = (f32[5,64,64]{2,1,0:T(8,128)S(1)}, f32[5,64,64]{2,1,0:T(8,128)}, u32[]{:S(2)}) copy-start(f32[5,64,64]{2,1,0:T(8,128)} %param.12) | copy-start | bytes 245764
  0.1 15.3 %copy-start = (bf16[256,768]{1,0:T(8,128)(2,1)S(1)}, bf16[256,768]{1,0:T(8,128)(2,1)}, u32[]{:S(2)}) copy-start(bf16[256,768]{1,0:T(8,128)(2,1)} %constant.8.clone.table_ref) | copy-start | bytes 1179652
  1.0 14.4 %copy-start.5 = (f32[64,1,128]{2,1,0:T(1,128)S(1)}, f32[64,1,128]{2,1,0:T(1,128)}, u32[]{:S(2)}) copy-start(f32[64,1,128]{2,1,0:T(1,128)} %param.13) | copy-start | bytes 98308
  15.4 10.8 %copy-start.6 = (f32[32,128]{1,0:T(8,128)S(1)}, f32[32,128]{1,0:T(8,128)}, u32[]{:S(2)}) copy-start(f32[32,128]{1,0:T(8,128)} %constant.9.clone.turns_ref) | copy-start | bytes 49156
  15.8 10.4 %copy-start.1 = (bf16[512,256]{1,0:T(8,128)(2,1)S(1)}, bf16[512,256]{1,0:T(8,128)(2,1)}, u32[]{:S(2)}) copy-start(bf16[512,256]{1,0:T(8,128)(2,1)} %constant.10.clone.table_ref) | copy-start | bytes 786436
  26.9 9.3 %copy-start.4 = (bf16[336,128]{1,0:T(8,128)(2,1)S(1)}, bf16[336,128]{1,0:T(8,128)(2,1)}, u32[]{:S(2)}) copy-start(bf16[336,128]{1,0:T(8,128)(2,1)} %constant.11.clone.pool_ref) | copy-start | bytes 258052

commit v17 on v15

--- a/solution.py
+++ b/solution.py
@@ -107,8 +107,9 @@
     for pair in range(groups // 2):
         even = x_ref[pl.ds(pair, rows, stride=groups), :]
         odd = x_ref[pl.ds(groups // 2 + pair, rows, stride=groups), :]
-        out_ref[2 * pair] = jnp.where(low_lanes, even, pltpu.roll(odd, HALF, 1))
-        out_ref[2 * pair + 1] = jnp.where(low_lanes, pltpu.roll(even, HALF, 1), odd)
+        crossed = pltpu.roll(jnp.where(low_lanes, odd, even), HALF, 1)
+        out_ref[2 * pair] = jnp.where(low_lanes, even, crossed)
+        out_ref[2 * pair + 1] = jnp.where(low_lanes, crossed, odd)
     whole_ref[:, : NCLASS + 1] = edges_ref[...]
     whole_ref[:, 8 : 8 + groups] = counts_ref[...]
 

time: 37.4 us -> 37.4 us (level)
  no operation moved by 1% of the time
where the time goes in v17:
time: 37.4 us; the launch traced here: 37.1 us
  blocking collectives  34.1 us (91%)
  Pallas kernels  2.13 us (6%)
  local copies, waits for them, and re-layouts  0.83 us (2%)
    all_to_all x3, blocking collectives, exchanged(): return lax.all_to_all(values, axes, split_axis=0, concat_axis=0, tiled=True)  34.1 us
    pallas_call x1, Pallas kernels, update_step(): pl.pallas_call(functools.partial(update_kernel, count), out_shape=jax.Sha...  0.9 us
    unnamed x18, local copies, waits for them, and re-layouts  0.83 us

profile of v17, /device:TPU:0, one launch (start us, length us, event | category | flops | bytes accessed | tf_op | source)
XLA Modules:
  0.0 37.1 jit_solution(4132763958521175795)
XLA Ops:
  0.0 0.0 copy-start.3
  0.0 0.0 copy-start.7
  0.0 0.0 copy-start.8
  0.0 0.0 copy-start.2
  0.0 0.1 turns.1.turn_ref
  0.1 0.0 copy-start
  0.1 0.8 %copy-done.3 = f32[1,32768]{1,0:T(1,128)S(1)} copy-done((f32[1,32768]{1,0:T(1,128)S(1)}, f32[1,32768]{1,0:T(1,128)}, u32[]{:S(2)}) %copy-start.3) | copy-done | bytes 131096
  0.9 0.0 copy-done.7
  0.9 0.0 copy-done.8
  0.9 0.1 columns.1
  1.0 0.0 copy-start.5
  1.0 14.4 %all_to_all.15 = f32[8,32,128]{2,1,0:T(8,128)S(1)} all-to-all(f32[8,32,128]{2,1,0:T(8,128)S(1)} %get-tuple-element.11), channel_id=1, replica_groups=mesh['bins'=8,'scans'=4] {'bins'}, dimensions={0} | all-to-all | bytes 262144 | tf_op jit(solution)/shard_map/all_to_all | solution.py:606
  15.4 0.0 copy-done.2
  15.4 0.0 copy-done
  15.4 0.0 copy-done.5
  15.4 0.0 copy-start.6
  15.5 0.4 %coarse_dft.1 = (f32[256,128]{1,0:T(8,128)S(1)}, f32[64,128]{1,0:T(8,128)S(1)}, s32[1,512]{1,0:T(1,128)S(1)}, s32[1,128]{1,0:T(1,128)S(1)}) custom-call(f32[256,128]{1,0:T(8,128)S(1)} %bitcast.13, bf16[256,768]{1,0:T(8,128)(2,1)S(1)} %copy-done, s32[1,128]{1,0:T(1,128)S(1)} %get-tuple-element.12.whole_ref, f32[320,64]{1,0:T(8,128)S(1)} %bitcast.17, ...), custom_call_target="tpu_custom_call" | custom-call | tf_op jit(solution)/shard_map/coarse_dft/pallas_call | solution.py:235
  15.8 0.0 copy-start.1
  15.9 10.4 %all_to_all.16 = f32[32,8,128]{2,1,0:T(8,128)S(1)} all-to-all(f32[32,8,128]{2,1,0:T(8,128)S(1)} %bitcast.19), channel_id=1, replica_groups=mesh['bins'=8,'scans'=4] {'bins','scans'}, dimensions={0} | all-to-all | bytes 262144 | tf_op jit(solution)/shard_map/all_to_all | solution.py:606
  26.3 0.0 copy-done.6
  26.3 0.0 copy-done.1
  26.3 0.7 %fine_dft.1 = f32[128,128]{1,0:T(8,128)S(1)} custom-call(f32[256,128]{1,0:T(8,128)S(1)} %bitcast.14, f32[32,8,128]{2,1,0:T(8,128)S(1)} %turns.1.turn_ref, s32[1,512]{1,0:T(1,128)S(1)} %get-tuple-element.14.wanted_ref, f32[32,128]{1,0:T(8,128)S(1)} %copy-done.6, bf16[512,256]{1,0:T(8,128)(2,1)S(1)} %copy-done.1), custom_call_target="tpu_custom_call" | custom-call | tf_op jit(solution)/shard_map/fine_dft/pallas_call | solution.py:469
  27.0 0.0 copy-start.4
  27.0 9.2 %all_to_all.17 = f32[32,4,128]{2,1,0:T(4,128)S(1)} all-to-all(f32[32,4,128]{2,1,0:T(4,128)S(1)} %bitcast.15), channel_id=1, replica_groups=mesh['bins'=8,'scans'=4] {'bins','scans'}, dimensions={0} | all-to-all | bytes 131072 | tf_op jit(solution)/shard_map/all_to_all | solution.py:606
  36.2 0.0 copy-done.4
  36.2 0.9 %state_update.1 = f32[64,128]{1,0:T(8,128)} custom-call(f32[128,128]{1,0:T(8,128)S(1)} %bitcast.16, bf16[336,128]{1,0:T(8,128)(2,1)S(1)} %copy-done.4, s32[1,128]{1,0:T(1,128)S(1)} %get-tuple-element.15.lane_band_ref, f32[64,128]{1,0:T(8,128)S(1)} %get-tuple-element.16.moved_ref), custom_call_target="tpu_custom_call" | custom-call | tf_op jit(solution)/shard_map/state_update/pallas_call | solution.py:581
Async XLA Ops:
  0.0 0.9 %copy-start.3 = (f32[1,32768]{1,0:T(1,128)S(1)}, f32[1,32768]{1,0:T(1,128)}, u32[]{:S(2)}) copy-start(f32[1,32768]{1,0:T(1,128)} %param.9) | copy-start | bytes 393220
  0.0 0.9 %copy-start.7 = (s32[6]{0:T(128)S(1)}, s32[6]{0:T(128)}, u32[]{:S(2)}) copy-start(s32[6]{0:T(128)} %param.10) | copy-start | bytes 76
  0.0 0.9 %copy-start.8 = (s32[8]{0:T(128)S(1)}, s32[8]{0:T(128)}, u32[]{:S(2)}) copy-start(s32[8]{0:T(128)} %param.11) | copy-start | bytes 100
  0.0 15.4 %copy-start.2 = (f32[5,64,64]{2,1,0:T(8,128)S(1)}, f32[5,64,64]{2,1,0:T(8,128)}, u32[]{:S(2)}) copy-start(f32[5,64,64]{2,1,0:T(8,128)} %param.12) | copy-start | bytes 245764
  0.1 15.3 %copy-start = (bf16[256,768]{1,0:T(8,128)(2,1)S(1)}, bf16[256,768]{1,0:T(8,128)(2,1)}, u32[]{:S(2)}) copy-start(bf16[256,768]{1,0:T(8,128)(2,1)} %constant.8.clone.table_ref) | copy-start | bytes 1179652
  1.0 14.4 %copy-start.5 = (f32[64,1,128]{2,1,0:T(1,128)S(1)}, f32[64,1,128]{2,1,0:T(1,128)}, u32[]{:S(2)}) copy-start(f32[64,1,128]{2,1,0:T(1,128)} %param.13) | copy-start | bytes 98308
  15.4 10.8 %copy-start.6 = (f32[32,128]{1,0:T(8,128)S(1)}, f32[32,128]{1,0:T(8,128)}, u32[]{:S(2)}) copy-start(f32[32,128]{1,0:T(8,128)} %constant.9.clone.turns_ref) | copy-start | bytes 49156
  15.8 10.4 %copy-start.1 = (bf16[512,256]{1,0:T(8,128)(2,1)S(1)}, bf16[512,256]{1,0:T(8,128)(2,1)}, u32[]{:S(2)}) copy-start(bf16[512,256]{1,0:T(8,128)(2,1)} %constant.10.clone.table_ref) | copy-start | bytes 786436
  27.0 9.3 %copy-start.4 = (bf16[336,128]{1,0:T(8,128)(2,1)S(1)}, bf16[336,128]{1,0:T(8,128)(2,1)}, u32[]{:S(2)}) copy-start(bf16[336,128]{1,0:T(8,128)(2,1)} %constant.11.clone.pool_ref) | copy-start | bytes 258052

commit v18 on v15

--- a/solution.py
+++ b/solution.py
@@ -211,10 +211,12 @@
         real_low, imag_low, real_high, imag_high = pieces
         if block == 0 and sign < 0:
             imag_low = jnp.where(row == 0, 0.0, imag_low)
-        even_real = jnp.where(low_lanes, real_low, pltpu.roll(real_high, HALF, 1))
-        even_imag = jnp.where(low_lanes, imag_low, pltpu.roll(imag_high, HALF, 1))
-        odd_real = jnp.where(low_lanes, pltpu.roll(real_low, HALF, 1), real_high)
-        odd_imag = jnp.where(low_lanes, pltpu.roll(imag_low, HALF, 1), imag_high)
+        crossed_real = pltpu.roll(jnp.where(low_lanes, real_high, real_low), HALF, 1)
+        crossed_imag = pltpu.roll(jnp.where(low_lanes, imag_high, imag_low), HALF, 1)
+        even_real = jnp.where(low_lanes, real_low, crossed_real)
+        even_imag = jnp.where(low_lanes, imag_low, crossed_imag)
+        odd_real = jnp.where(low_lanes, crossed_real, real_high)
+        odd_imag = jnp.where(low_lanes, crossed_imag, imag_high)
         first = 2 * block + (0 if sign > 0 else shares // 2)
         angle = math.pi * 8 * first / half
         cosine = base_cosine * math.cos(angle) - base_sine * math.sin(angle)

time: 37.4 us -> 37.4 us (level)
  no operation moved by 1% of the time
where the time goes in v18:
time: 37.4 us; the launch traced here: 37.1 us
  blocking collectives  34.1 us (91%)
  Pallas kernels  2.14 us (6%)
  local copies, waits for them, and re-layouts  0.83 us (2%)
    all_to_all x3, blocking collectives, exchanged(): return lax.all_to_all(values, axes, split_axis=0, concat_axis=0, tiled=True)  34.1 us
    pallas_call x1, Pallas kernels, update_step(): pl.pallas_call(functools.partial(update_kernel, count), out_shape=jax.Sha...  0.91 us
    unnamed x18, local copies, waits for them, and re-layouts  0.83 us

profile of v18, /device:TPU:0, one launch (start us, length us, event | category | flops | bytes accessed | tf_op | source)
XLA Modules:
  0.0 37.1 jit_solution(13855220116370323595)
XLA Ops:
  0.0 0.0 copy-start.3
  0.0 0.0 copy-start.7
  0.0 0.0 copy-start.8
  0.0 0.0 copy-start.2
  0.0 0.1 turns.1.turn_ref
  0.1 0.0 copy-start
  0.1 0.8 %copy-done.3 = f32[1,32768]{1,0:T(1,128)S(1)} copy-done((f32[1,32768]{1,0:T(1,128)S(1)}, f32[1,32768]{1,0:T(1,128)}, u32[]{:S(2)}) %copy-start.3) | copy-done | bytes 131096
  0.9 0.0 copy-done.7
  0.9 0.0 copy-done.8
  0.9 0.1 columns.1
  1.0 0.0 copy-start.5
  1.0 14.4 %all_to_all.15 = f32[8,32,128]{2,1,0:T(8,128)S(1)} all-to-all(f32[8,32,128]{2,1,0:T(8,128)S(1)} %get-tuple-element.11), channel_id=1, replica_groups=mesh['bins'=8,'scans'=4] {'bins'}, dimensions={0} | all-to-all | bytes 262144 | tf_op jit(solution)/shard_map/all_to_all | solution.py:607
  15.5 0.0 copy-done.2
  15.5 0.0 copy-done
  15.5 0.0 copy-done.5
  15.5 0.0 copy-start.6
  15.5 0.4 %coarse_dft.1 = (f32[256,128]{1,0:T(8,128)S(1)}, f32[64,128]{1,0:T(8,128)S(1)}, s32[1,512]{1,0:T(1,128)S(1)}, s32[1,128]{1,0:T(1,128)S(1)}) custom-call(f32[256,128]{1,0:T(8,128)S(1)} %bitcast.13, bf16[256,768]{1,0:T(8,128)(2,1)S(1)} %copy-done, s32[1,128]{1,0:T(1,128)S(1)} %get-tuple-element.12.whole_ref, f32[320,64]{1,0:T(8,128)S(1)} %bitcast.17, ...), custom_call_target="tpu_custom_call" | custom-call | tf_op jit(solution)/shard_map/coarse_dft/pallas_call | solution.py:236
  15.9 0.0 copy-start.1
  15.9 10.4 %all_to_all.16 = f32[32,8,128]{2,1,0:T(8,128)S(1)} all-to-all(f32[32,8,128]{2,1,0:T(8,128)S(1)} %bitcast.19), channel_id=1, replica_groups=mesh['bins'=8,'scans'=4] {'bins','scans'}, dimensions={0} | all-to-all | bytes 262144 | tf_op jit(solution)/shard_map/all_to_all | solution.py:607
  26.3 0.0 copy-done.6
  26.3 0.0 copy-done.1
  26.3 0.7 %fine_dft.1 = f32[128,128]{1,0:T(8,128)S(1)} custom-call(f32[256,128]{1,0:T(8,128)S(1)} %bitcast.14, f32[32,8,128]{2,1,0:T(8,128)S(1)} %turns.1.turn_ref, s32[1,512]{1,0:T(1,128)S(1)} %get-tuple-element.14.wanted_ref, f32[32,128]{1,0:T(8,128)S(1)} %copy-done.6, bf16[512,256]{1,0:T(8,128)(2,1)S(1)} %copy-done.1), custom_call_target="tpu_custom_call" | custom-call | tf_op jit(solution)/shard_map/fine_dft/pallas_call | solution.py:470
  27.0 0.0 copy-start.4
  27.0 9.2 %all_to_all.17 = f32[32,4,128]{2,1,0:T(4,128)S(1)} all-to-all(f32[32,4,128]{2,1,0:T(4,128)S(1)} %bitcast.15), channel_id=1, replica_groups=mesh['bins'=8,'scans'=4] {'bins','scans'}, dimensions={0} | all-to-all | bytes 131072 | tf_op jit(solution)/shard_map/all_to_all | solution.py:607
  36.2 0.0 copy-done.4
  36.2 0.9 %state_update.1 = f32[64,128]{1,0:T(8,128)} custom-call(f32[128,128]{1,0:T(8,128)S(1)} %bitcast.16, bf16[336,128]{1,0:T(8,128)(2,1)S(1)} %copy-done.4, s32[1,128]{1,0:T(1,128)S(1)} %get-tuple-element.15.lane_band_ref, f32[64,128]{1,0:T(8,128)S(1)} %get-tuple-element.16.moved_ref), custom_call_target="tpu_custom_call" | custom-call | tf_op jit(solution)/shard_map/state_update/pallas_call | solution.py:582
Async XLA Ops:
  0.0 0.9 %copy-start.3 = (f32[1,32768]{1,0:T(1,128)S(1)}, f32[1,32768]{1,0:T(1,128)}, u32[]{:S(2)}) copy-start(f32[1,32768]{1,0:T(1,128)} %param.9) | copy-start | bytes 393220
  0.0 0.9 %copy-start.7 = (s32[6]{0:T(128)S(1)}, s32[6]{0:T(128)}, u32[]{:S(2)}) copy-start(s32[6]{0:T(128)} %param.10) | copy-start | bytes 76
  0.0 0.9 %copy-start.8 = (s32[8]{0:T(128)S(1)}, s32[8]{0:T(128)}, u32[]{:S(2)}) copy-start(s32[8]{0:T(128)} %param.11) | copy-start | bytes 100
  0.0 15.4 %copy-start.2 = (f32[5,64,64]{2,1,0:T(8,128)S(1)}, f32[5,64,64]{2,1,0:T(8,128)}, u32[]{:S(2)}) copy-start(f32[5,64,64]{2,1,0:T(8,128)} %param.12) | copy-start | bytes 245764
  0.1 15.3 %copy-start = (bf16[256,768]{1,0:T(8,128)(2,1)S(1)}, bf16[256,768]{1,0:T(8,128)(2,1)}, u32[]{:S(2)}) copy-start(bf16[256,768]{1,0:T(8,128)(2,1)} %constant.8.clone.table_ref) | copy-start | bytes 1179652
  1.0 14.4 %copy-start.5 = (f32[64,1,128]{2,1,0:T(1,128)S(1)}, f32[64,1,128]{2,1,0:T(1,128)}, u32[]{:S(2)}) copy-start(f32[64,1,128]{2,1,0:T(1,128)} %param.13) | copy-start | bytes 98308
  15.5 10.8 %copy-start.6 = (f32[32,128]{1,0:T(8,128)S(1)}, f32[32,128]{1,0:T(8,128)}, u32[]{:S(2)}) copy-start(f32[32,128]{1,0:T(8,128)} %constant.9.clone.turns_ref) | copy-start | bytes 49156
  15.9 10.4 %copy-start.1 = (bf16[512,256]{1,0:T(8,128)(2,1)S(1)}, bf16[512,256]{1,0:T(8,128)(2,1)}, u32[]{:S(2)}) copy-start(bf16[512,256]{1,0:T(8,128)(2,1)} %constant.10.clone.table_ref) | copy-start | bytes 786436
  27.0 9.3 %copy-start.4 = (bf16[336,128]{1,0:T(8,128)(2,1)S(1)}, bf16[336,128]{1,0:T(8,128)(2,1)}, u32[]{:S(2)}) copy-start(bf16[336,128]{1,0:T(8,128)(2,1)} %constant.11.clone.pool_ref) | copy-start | bytes 258052

commit v19 on v15

--- a/solution.py
+++ b/solution.py
@@ -454,11 +454,10 @@
             real = routed[8 * at : 8 * (at + 1), pair * LANES : (pair + 1) * LANES]
             imag = routed[16 + 8 * at : 16 + 8 * (at + 1), pair * LANES : (pair + 1) * LANES]
             start = 2 * pair * profiles * KINDS + at
-            out_ref[pl.ds(start, 8, stride=2), :] = jnp.where(
-                low_lanes, real, pltpu.roll(imag, HALF, 1)
-            )
+            crossed = pltpu.roll(jnp.where(low_lanes, imag, real), HALF, 1)
+            out_ref[pl.ds(start, 8, stride=2), :] = jnp.where(low_lanes, real, crossed)
             out_ref[pl.ds(start + profiles * KINDS, 8, stride=2), :] = jnp.where(
-                low_lanes, pltpu.roll(real, HALF, 1), imag
+                low_lanes, crossed, imag
             )
 
 

time: 37.4 us -> 37.4 us (level)
  no operation moved by 1% of the time
where the time goes in v19:
time: 37.4 us; the launch traced here: 37.1 us
  blocking collectives  34.1 us (91%)
  Pallas kernels  2.12 us (6%)
  local copies, waits for them, and re-layouts  0.84 us (2%)
    all_to_all x3, blocking collectives, exchanged(): return lax.all_to_all(values, axes, split_axis=0, concat_axis=0, tiled=True)  34.1 us
    pallas_call x1, Pallas kernels, update_step(): pl.pallas_call(functools.partial(update_kernel, count), out_shape=jax.Sha...  0.9 us
    unnamed x18, local copies, waits for them, and re-layouts  0.84 us

profile of v19, /device:TPU:0, one launch (start us, length us, event | category | flops | bytes accessed | tf_op | source)
XLA Modules:
  0.0 37.1 jit_solution(863793936963344827)
XLA Ops:
  0.0 0.0 copy-start.3
  0.0 0.0 copy-start.7
  0.0 0.0 copy-start.8
  0.0 0.0 copy-start.2
  0.0 0.1 turns.1.turn_ref
  0.1 0.0 copy-start
  0.1 0.8 %copy-done.3 = f32[1,32768]{1,0:T(1,128)S(1)} copy-done((f32[1,32768]{1,0:T(1,128)S(1)}, f32[1,32768]{1,0:T(1,128)}, u32[]{:S(2)}) %copy-start.3) | copy-done | bytes 131096
  0.9 0.0 copy-done.7
  0.9 0.0 copy-done.8
  0.9 0.1 columns.1
  1.0 0.0 copy-start.5
  1.0 14.4 %all_to_all.15 = f32[8,32,128]{2,1,0:T(8,128)S(1)} all-to-all(f32[8,32,128]{2,1,0:T(8,128)S(1)} %get-tuple-element.11), channel_id=1, replica_groups=mesh['bins'=8,'scans'=4] {'bins'}, dimensions={0} | all-to-all | bytes 262144 | tf_op jit(solution)/shard_map/all_to_all | solution.py:604
  15.5 0.0 copy-done.2
  15.5 0.0 copy-done
  15.5 0.0 copy-done.5
  15.5 0.0 copy-start.6
  15.5 0.4 %coarse_dft.1 = (f32[256,128]{1,0:T(8,128)S(1)}, f32[64,128]{1,0:T(8,128)S(1)}, s32[1,512]{1,0:T(1,128)S(1)}, s32[1,128]{1,0:T(1,128)S(1)}) custom-call(f32[256,128]{1,0:T(8,128)S(1)} %bitcast.13, bf16[256,768]{1,0:T(8,128)(2,1)S(1)} %copy-done, s32[1,128]{1,0:T(1,128)S(1)} %get-tuple-element.12.whole_ref, f32[320,64]{1,0:T(8,128)S(1)} %bitcast.17, ...), custom_call_target="tpu_custom_call" | custom-call | tf_op jit(solution)/shard_map/coarse_dft/pallas_call | solution.py:234
  15.9 0.0 copy-start.1
  15.9 10.4 %all_to_all.16 = f32[32,8,128]{2,1,0:T(8,128)S(1)} all-to-all(f32[32,8,128]{2,1,0:T(8,128)S(1)} %bitcast.19), channel_id=1, replica_groups=mesh['bins'=8,'scans'=4] {'bins','scans'}, dimensions={0} | all-to-all | bytes 262144 | tf_op jit(solution)/shard_map/all_to_all | solution.py:604
  26.3 0.0 copy-done.6
  26.3 0.0 copy-done.1
  26.3 0.6 %fine_dft.1 = f32[128,128]{1,0:T(8,128)S(1)} custom-call(f32[256,128]{1,0:T(8,128)S(1)} %bitcast.14, f32[32,8,128]{2,1,0:T(8,128)S(1)} %turns.1.turn_ref, s32[1,512]{1,0:T(1,128)S(1)} %get-tuple-element.14.wanted_ref, f32[32,128]{1,0:T(8,128)S(1)} %copy-done.6, bf16[512,256]{1,0:T(8,128)(2,1)S(1)} %copy-done.1), custom_call_target="tpu_custom_call" | custom-call | tf_op jit(solution)/shard_map/fine_dft/pallas_call | solution.py:467
  26.9 0.0 copy-start.4
  27.0 9.2 %all_to_all.17 = f32[32,4,128]{2,1,0:T(4,128)S(1)} all-to-all(f32[32,4,128]{2,1,0:T(4,128)S(1)} %bitcast.15), channel_id=1, replica_groups=mesh['bins'=8,'scans'=4] {'bins','scans'}, dimensions={0} | all-to-all | bytes 131072 | tf_op jit(solution)/shard_map/all_to_all | solution.py:604
  36.2 0.0 copy-done.4
  36.2 0.9 %state_update.1 = f32[64,128]{1,0:T(8,128)} custom-call(f32[128,128]{1,0:T(8,128)S(1)} %bitcast.16, bf16[336,128]{1,0:T(8,128)(2,1)S(1)} %copy-done.4, s32[1,128]{1,0:T(1,128)S(1)} %get-tuple-element.15.lane_band_ref, f32[64,128]{1,0:T(8,128)S(1)} %get-tuple-element.16.moved_ref), custom_call_target="tpu_custom_call" | custom-call | tf_op jit(solution)/shard_map/state_update/pallas_call | solution.py:579
Async XLA Ops:
  0.0 0.9 %copy-start.3 = (f32[1,32768]{1,0:T(1,128)S(1)}, f32[1,32768]{1,0:T(1,128)}, u32[]{:S(2)}) copy-start(f32[1,32768]{1,0:T(1,128)} %param.9) | copy-start | bytes 393220
  0.0 0.9 %copy-start.7 = (s32[6]{0:T(128)S(1)}, s32[6]{0:T(128)}, u32[]{:S(2)}) copy-start(s32[6]{0:T(128)} %param.10) | copy-start | bytes 76
  0.0 0.9 %copy-start.8 = (s32[8]{0:T(128)S(1)}, s32[8]{0:T(128)}, u32[]{:S(2)}) copy-start(s32[8]{0:T(128)} %param.11) | copy-start | bytes 100
  0.0 15.4 %copy-start.2 = (f32[5,64,64]{2,1,0:T(8,128)S(1)}, f32[5,64,64]{2,1,0:T(8,128)}, u32[]{:S(2)}) copy-start(f32[5,64,64]{2,1,0:T(8,128)} %param.12) | copy-start | bytes 245764
  0.1 15.3 %copy-start = (bf16[256,768]{1,0:T(8,128)(2,1)S(1)}, bf16[256,768]{1,0:T(8,128)(2,1)}, u32[]{:S(2)}) copy-start(bf16[256,768]{1,0:T(8,128)(2,1)} %constant.8.clone.table_ref) | copy-start | bytes 1179652
  1.0 14.4 %copy-start.5 = (f32[64,1,128]{2,1,0:T(1,128)S(1)}, f32[64,1,128]{2,1,0:T(1,128)}, u32[]{:S(2)}) copy-start(f32[64,1,128]{2,1,0:T(1,128)} %param.13) | copy-start | bytes 98308
  15.5 10.8 %copy-start.6 = (f32[32,128]{1,0:T(8,128)S(1)}, f32[32,128]{1,0:T(8,128)}, u32[]{:S(2)}) copy-start(f32[32,128]{1,0:T(8,128)} %constant.9.clone.turns_ref) | copy-start | bytes 49156
  15.9 10.4 %copy-start.1 = (bf16[512,256]{1,0:T(8,128)(2,1)S(1)}, bf16[512,256]{1,0:T(8,128)(2,1)}, u32[]{:S(2)}) copy-start(bf16[512,256]{1,0:T(8,128)(2,1)} %constant.10.clone.table_ref) | copy-start | bytes 786436
  26.9 9.3 %copy-start.4 = (bf16[336,128]{1,0:T(8,128)(2,1)S(1)}, bf16[336,128]{1,0:T(8,128)(2,1)}, u32[]{:S(2)}) copy-start(bf16[336,128]{1,0:T(8,128)(2,1)} %constant.11.clone.pool_ref) | copy-start | bytes 258052
